TPU v7x, 256 devices: a whole 4x4x8 slice. The times are simulated.
256 devices in a mesh: rows: 64 (over z, y, core), tp: 4 (over x).
Axes of the slice: x: 4, y: 4, z: 8, core: 2. Of those that a mesh axis runs over, the one named last changes fastest.
Arguments:
- normed_rows: bfloat16 [16384, 8192], P('rows'), may hold values from -6 to 6
- value_weight: bfloat16 [8192, 1024], P(None, 'tp'), may hold values from -0.0625 to 0.0625
- adapter_a: bfloat16 [128, 8192, 64], P('rows', 'tp'), may hold values from -0.0625 to 0.0625
- adapter_b: bfloat16 [128, 64, 1024], P('rows', None, 'tp'), may hold values from -0.75 to 0.75
- page_table: int32 [128], replicated, may hold values from 0 to 127, as said below
- group_list: int32 [64, 64], replicated, may hold values from 0 to 127, as said below
- seg_len: int32 [64, 64], P('rows'), may hold values from 1 to 8, 256 in all within a row
- kv_len: int32 [64, 256], P('rows'), may hold values from 1 to 32, 4096 in all within a row
- queries: bfloat16 [16384, 8192], P('rows', 'tp'), may hold values from -8 to 8
- new_key: bfloat16 [16384, 1024], P('rows', 'tp'), may hold values from -8 to 8
- cache_keys: bfloat16 [16384, 32, 1024], P('rows', None, 'tp'), may hold values from -8 to 8
- cache_values: bfloat16 [16384, 32, 1024], P('rows', None, 'tp'), may hold values from -6 to 6
Outputs:
- new_value: bfloat16 [16384, 1024], P('rows', 'tp')
- attended: bfloat16 [16384, 8192], P('rows', 'tp')
Inputs may be any that keep to these rules, and one draw needn't show every extreme that they name: `page_table`: each adapter has one position; the device of rows index p // 2 stores position p. `group_list`: the 64 adapters of a group are stored on 64 different indices of rows.
All inputs are finite; a program needn't handle non-finite values.
Results may differ from a plain program's by a relative error of at most 0.0048.
Values may be sent and summed in bfloat16 or wider, within the bound.
No kernel may reach another device: no remote copies, remote signals or barrier semaphores. Data moves between devices by JAX's collectives and lax.ppermute only.
A program may use at most 128 MiB of HBM per device.

v0:
```python
import math

import jax
import jax.numpy as jnp
from jax import lax
from jax.sharding import PartitionSpec as P

HEAD = 128


def cache_scores(q_four, k_four, lengths, scale):
    score = (
        jnp.einsum("rhgd,rchd->rhgc", q_four, k_four, preferred_element_type=jnp.float32) * scale
    )
    valid = (jnp.arange(k_four.shape[1], dtype=jnp.int32)[None, :] < lengths[:, None])[
        :, None, None, :
    ]
    return (score, valid)


def body(
    normed_rows,
    value_weight,
    adapter_a,
    adapter_b,
    page_table,
    group_list,
    seg_len,
    kv_len,
    queries,
    new_key,
    cache_keys,
    cache_values,
):
    tp_index = lax.axis_index("tp")
    groups = lax.axis_size("rows")
    own_group = lax.axis_index("rows")
    rows_count = normed_rows.shape[0]
    part = normed_rows.shape[1] // lax.axis_size("tp")
    per_owner = adapter_a.shape[0]
    adapters_count = page_table.shape[0]
    lens = seg_len[0]
    slots = lens.shape[0]
    most = 2 * rows_count // slots
    heads_kv = new_key.shape[1] // HEAD
    group = queries.shape[1] // new_key.shape[1]
    scale = 1.0 / math.sqrt(HEAD)
    lengths = kv_len[0]
    q_four = queries.reshape(rows_count, heads_kv, group, HEAD)
    k_four = cache_keys.reshape(rows_count, -1, heads_kv, HEAD)
    v_four = cache_values.reshape(rows_count, -1, heads_kv, HEAD)
    k_own = new_key.reshape(rows_count, heads_kv, HEAD)
    x_part = lax.dynamic_slice_in_dim(normed_rows, tp_index * part, part, 1)
    ends = jnp.cumsum(lens)
    starts = ends - lens
    rowpos = jnp.arange(rows_count, dtype=jnp.int32)
    segment = jnp.sum((rowpos[:, None] >= ends[None, :]).astype(jnp.int32), axis=1)
    in_segment = segment[:, None] == jnp.arange(slots, dtype=jnp.int32)[None, :]
    within = rowpos - jnp.sum(jnp.where(in_segment, starts[None, :], 0), axis=1)
    listed = group_list.reshape(-1)
    positions = jnp.sum(
        jnp.where(
            listed[:, None] == jnp.arange(adapters_count, dtype=jnp.int32)[None, :],
            page_table[None, :],
            0,
        ),
        axis=1,
    ).reshape(groups, slots)
    owners = positions // per_owner
    my_owners = lax.dynamic_index_in_dim(owners, own_group, 0, keepdims=False)
    owner_of_row = jnp.sum(jnp.where(in_segment, my_owners[None, :], 0), axis=1)
    target = owner_of_row * most + within
    placing = (jnp.arange(groups * most, dtype=jnp.int32)[:, None] == target[None, :]).astype(
        jnp.bfloat16
    )
    placed_rows = (
        jnp.dot(placing, x_part, preferred_element_type=jnp.float32)
        .astype(jnp.bfloat16)
        .reshape(groups, most, part)
    )
    mine = owners == own_group
    local = positions % per_owner
    hits = mine[:, :, None] & (
        local[:, :, None] == jnp.arange(per_owner, dtype=jnp.int32)[None, None, :]
    )
    selector = jnp.sum(hits.astype(jnp.float32), axis=1)
    arrived = lax.all_to_all(placed_rows, "rows", split_axis=0, concat_axis=0, tiled=True)
    low_each = jnp.einsum("nmd,jdr->njmr", arrived, adapter_a, preferred_element_type=jnp.float32)
    low_part = jnp.sum(low_each * selector[:, :, None, None], axis=1)
    low = lax.psum(low_part, "tp").astype(jnp.bfloat16)
    delta_each = jnp.einsum("nmr,jrk->njmk", low, adapter_b, preferred_element_type=jnp.float32)
    delta_out = jnp.sum(delta_each * selector[:, :, None, None], axis=1).astype(jnp.bfloat16)
    delta = lax.all_to_all(delta_out, "rows", split_axis=0, concat_axis=0, tiled=True)
    delta_rows = lax.dot_general(
        placing,
        delta.reshape(groups * most, -1),
        (((0,), (0,)), ((), ())),
        preferred_element_type=jnp.float32,
    )
    base = jnp.dot(normed_rows, value_weight, preferred_element_type=jnp.float32)
    new_value = (base + delta_rows).astype(jnp.bfloat16)
    v_own = new_value.reshape(rows_count, heads_kv, HEAD)
    k_joined = jnp.concatenate([k_four, k_own[:, None]], axis=1)
    v_joined = jnp.concatenate([v_four, v_own[:, None]], axis=1)
    score, valid = cache_scores(q_four, k_joined, lengths, scale)
    valid = (
        valid
        | (jnp.arange(k_joined.shape[1], dtype=jnp.int32) == k_joined.shape[1] - 1)[
            None, None, None, :
        ]
    )
    top = jnp.max(jnp.where(valid, score, -jnp.inf), axis=-1)
    expd = jnp.where(valid, jnp.exp(score - top[..., None]), 0.0)
    total = jnp.sum(expd, axis=-1)
    context = jnp.einsum(
        "rhgc,rchd->rhgd", expd.astype(jnp.bfloat16), v_joined, preferred_element_type=jnp.float32
    )
    attended = (context / total[..., None]).astype(jnp.bfloat16).reshape(rows_count, -1)
    return (new_value, attended)


def solution(mesh):
    return jax.shard_map(
        body,
        mesh=mesh,
        in_specs=(
            P("rows", None),
            P(None, "tp"),
            P("rows", "tp", None),
            P("rows", None, "tp"),
            P(),
            P(),
            P("rows", None),
            P("rows", None),
            P("rows", "tp"),
            P("rows", "tp"),
            P("rows", None, "tp"),
            P("rows", None, "tp"),
        ),
        out_specs=(P("rows", "tp"), P("rows", "tp")),
        check_vma=False,
    )
```

profile of v0, /device:TPU:1, one launch (start us, length us, event | category | flops | bytes accessed | tf_op | source)
XLA Modules:
  0.0 119.7 jit_solution(12656168245607540480)
XLA Ops:
  0.6 0.0 copy-start
  0.7 0.9 eq.80
  1.5 1.9 %select_reduce_fusion.1 = s32[4096]{0:T(1024)S(1)} fusion(s32[128]{0:T(128)} %param.16, s32[4096]{0:T(1024)S(1)} %eq.80), kind=kLoop, calls=%fused_computation.19 | loop fusion | flops 1568768 | bytes 33280 | tf_op jit(solution)/shard_map/reduce_sum | solution.py:61
  3.5 0.1 reshape.142
  3.6 0.7 copy.26
  4.3 0.1 reduce-window.4
  4.4 0.1 reduce.3
  4.5 0.1 convert_reduce_fusion.1
  4.6 0.7 fusion.41
  5.3 0.1 select_reduce_fusion.3
  5.4 3.3 %fusion.9 = bf16[64,8,2048]{2,1,0:T(8,128)(2,1)} fusion(bf16[256,8192]{1,0:T(8,128)(2,1)} %param.12, s32[]{:T(128)S(6)} %select_n.54, s32[256]{0:T(256)S(1)} %subtract_add_fusion), kind=kOutput, calls=%fused_computation.10 | convolution fusion | flops 538050560 | bytes 3146756 | tf_op jit(solution)/shard_map/dot_general | solution.py:77
  8.7 13.2 %all-to-all-start = ((bf16[64,8,2048]{2,1,0:T(8,128)(2,1)}), bf16[64,8,2048]{2,1,0:T(8,128)(2,1)S(1)}, u32[]{:S(2)}, u32[]{:S(2)}) async-start(bf16[64,8,2048]{2,1,0:T(8,128)(2,1)} %fusion.9), calls=%async_computation | async-start | bytes 4194304 | tf_op jit(solution)/shard_map/all_to_all | solution.py:87
  21.9 0.1 convert_reduce_fusion
  22.0 0.1 copy.27
  22.1 7.5 %copy.29 = bf16[256,32,256]{0,2,1:T(8,128)(2,1)} copy(bf16[256,32,256]{2,1,0:T(8,128)(2,1)} %param.22) | data formatting | bytes 8388608 | tf_op args[10]
  29.6 0.0 copy-start.1
  29.6 8.0 %copy.31 = bf16[256,32,2,128]{3,1,2,0:T(8,128)(2,1)} copy(bf16[256,32,2,128]{0,3,2,1:T(8,128)(2,1)} %bitcast.59) | data formatting | bytes 8388608 | tf_op jit(solution)/shard_map/reshape | solution.py:50
  37.6 2.4 %copy.39 = bf16[32,8,16,128]{3,2,1,0:T(8,128)(2,1)} copy(bf16[32,8,16,128]{3,1,2,0:T(8,128)(2,1)} %bitcast.62) | data formatting | bytes 2097152
  40.0 0.0 copy-done.1
  40.0 0.1 copy.30
  40.1 0.2 copy.32
  40.3 7.5 %copy.33 = bf16[256,32,256]{0,2,1:T(8,128)(2,1)} copy(bf16[256,32,256]{2,1,0:T(8,128)(2,1)} %param.23) | data formatting | bytes 8388608 | tf_op args[11]
  47.8 0.0 copy-start.2
  47.8 8.0 %copy.34 = bf16[256,32,2,128]{3,1,2,0:T(8,128)(2,1)} copy(bf16[256,32,2,128]{0,3,2,1:T(8,128)(2,1)} %bitcast.60) | data formatting | bytes 8388608 | tf_op jit(solution)/shard_map/reshape | solution.py:51
  55.8 0.0 copy-done.2
  55.8 0.1 fusion.36
  55.9 5.3 %fusion.1 = f32[256,2,33,8]{2,3,1,0:T(8,128)S(1)} fusion(bf16[256,2,8,128]{3,2,1,0:T(8,128)(2,1)} %bitcast.64, bf16[256,1,2,128]{3,1,2,0:T(2,128)(2,1)S(1)} %copy.32, bf16[256,32,2,128]{3,1,2,0:T(8,128)(2,1)} %copy.31), kind=kOutput, calls=%fused_computation.1 | convolution fusion | flops 43253760 | bytes 5914624 | tf_op jit(solution)/shard_map/rhgd,rchd->rhgc/dot_general | solution.py:13
  61.2 0.0 copy-start.3
  61.2 2.3 %bitcast_reduce_fusion = (f32[256,2,8]{2,1,0:T(2,128)S(1)}, bf16[256,2,33,8]{2,3,1,0:T(8,128)(2,1)}) fusion(f32[256,2,33,8]{2,3,1,0:T(8,128)S(1)} %fusion.1, pred[256,33]{1,0:T(8,128)(4,1)S(1)} %fusion.36), kind=kOutput, calls=%fused_computation.13 | output fusion | flops 946208 | bytes 835840 | tf_op jit(solution)/shard_map/sub | solution.py:113
  63.5 8.1 %all-to-all-done = bf16[64,8,2048]{2,1,0:T(8,128)(2,1)S(1)} async-done(((bf16[64,8,2048]{2,1,0:T(8,128)(2,1)}), bf16[64,8,2048]{2,1,0:T(8,128)(2,1)S(1)}, u32[]{:S(2)}, u32[]{:S(2)}) %all-to-all-start) | async-done | bytes 2097184 | tf_op jit(solution)/shard_map/all_to_all | solution.py:87
  71.6 0.0 copy-done
  71.6 0.7 fusion.20
  72.3 16.7 %all-reduce.1 = bf16[64,8,64]{2,1,0:T(8,128)(2,1)S(1)} all-reduce(f32[64,8,64]{2,1,0:T(8,128)S(1)} %fusion.20), channel_id=1, replica_groups=mesh['rows'=64,'tp'=4] {'tp'}, use_global_device_ids=true, to_apply=%region_7.8 | all-reduce | flops 32768 | bytes 196608 | tf_op jit(solution)/shard_map/psum | solution.py:90
  89.0 0.0 copy-done.3
  89.0 1.0 fusion.16
  90.0 10.2 %all-to-all-start.1 = ((bf16[64,8,256]{2,1,0:T(8,128)(2,1)}), bf16[64,8,256]{2,1,0:T(8,128)(2,1)S(1)}, u32[]{:S(2)}, u32[]{:S(2)}) async-start(bf16[64,8,256]{2,1,0:T(8,128)(2,1)} %fusion.16), calls=%async_computation.1 | async-start | bytes 524288 | tf_op jit(solution)/shard_map/all_to_all | solution.py:93
  100.2 0.0 copy-start.4
  100.2 5.3 %fusion.49 = f32[256,256]{0,1:T(8,128)S(1)} fusion(bf16[256,8192]{1,0:T(8,128)(2,1)} %param.12, bf16[8192,256]{1,0:T(8,128)(2,1)} %param.13), kind=kOutput, calls=%fused_computation.71 | convolution fusion | flops 1073741824 | bytes 8650752 | tf_op jit(solution)/shard_map/dot_general | solution.py:100
  105.5 7.9 %all-to-all-done.1 = bf16[64,8,256]{2,1,0:T(8,128)(2,1)S(1)} async-done(((bf16[64,8,256]{2,1,0:T(8,128)(2,1)}), bf16[64,8,256]{2,1,0:T(8,128)(2,1)S(1)}, u32[]{:S(2)}, u32[]{:S(2)}) %all-to-all-start.1) | async-done | bytes 262176 | tf_op jit(solution)/shard_map/all_to_all | solution.py:93
  113.4 0.3 fusion.23
  113.7 0.8 copy.36
  114.4 0.2 copy.35
  114.6 0.0 copy-done.4
  114.6 3.8 %divide_convert_fusion = bf16[256,2,8,128]{3,2,1,0:T(8,128)(2,1)S(1)} fusion(f32[256,2,8]{2,1,0:T(2,128)S(1)} %get-tuple-element.12, bf16[256,1,2,128]{3,1,2,0:T(2,128)(2,1)S(1)} %copy.35, bf16[256,32,2,128]{3,1,2,0:T(8,128)(2,1)} %copy.34, bf16[256,2,33,8]{2,3,1,0:T(8,128)(2,1)S(1)} %copy-done.4), kind=kOutput, calls=%fused_computation.15 | convolution fusion | flops 44302336 | bytes 5660672 | tf_op jit(solution)/shard_map/rhgc,rchd->rhgd/dot_general | solution.py:115
  118.5 1.2 %copy.42 = bf16[32,8,16,128]{3,1,2,0:T(8,128)(2,1)} copy(bf16[32,8,16,128]{3,2,1,0:T(8,128)(2,1)S(1)} %bitcast.65) | data formatting | bytes 2097152
  (4 shorter events, 0.1 us)
Async XLA Ops:
  0.6 70.9 %copy-start = (bf16[2,2048,64]{1,2,0:T(8,128)(2,1)S(1)}, bf16[2,2048,64]{1,2,0:T(8,128)(2,1)}, u32[]{:S(2)}) copy-start(bf16[2,2048,64]{1,2,0:T(8,128)(2,1)} %param.14) | copy-start | bytes 1572868
  8.7 62.8 %all-to-all-start = ((bf16[64,8,2048]{2,1,0:T(8,128)(2,1)}), bf16[64,8,2048]{2,1,0:T(8,128)(2,1)S(1)}, u32[]{:S(2)}, u32[]{:S(2)}) async-start(bf16[64,8,2048]{2,1,0:T(8,128)(2,1)} %fusion.9), calls=%async_computation | async-start | bytes 4194304 | tf_op jit(solution)/shard_map/all_to_all | solution.py:87
  29.6 10.4 %copy-start.1 = (bf16[256,256]{1,0:T(8,128)(2,1)S(1)}, bf16[256,256]{1,0:T(8,128)(2,1)}, u32[]{:S(2)}) copy-start(bf16[256,256]{1,0:T(8,128)(2,1)} %param.21) | copy-start | bytes 393220
  47.8 8.0 %copy-start.2 = (s32[1,256]{1,0:T(1,128)S(1)}, s32[1,256]{1,0:T(1,128)}, u32[]{:S(2)}) copy-start(s32[1,256]{1,0:T(1,128)} %param.19) | copy-start | bytes 3076
  61.2 27.9 %copy-start.3 = (bf16[2,64,256]{2,1,0:T(8,128)(2,1)S(1)}, bf16[2,64,256]{2,1,0:T(8,128)(2,1)}, u32[]{:S(2)}) copy-start(bf16[2,64,256]{2,1,0:T(8,128)(2,1)} %param.15) | copy-start | bytes 196612
  90.0 23.3 %all-to-all-start.1 = ((bf16[64,8,256]{2,1,0:T(8,128)(2,1)}), bf16[64,8,256]{2,1,0:T(8,128)(2,1)S(1)}, u32[]{:S(2)}, u32[]{:S(2)}) async-start(bf16[64,8,256]{2,1,0:T(8,128)(2,1)} %fusion.16), calls=%async_computation.1 | async-start | bytes 524288 | tf_op jit(solution)/shard_map/all_to_all | solution.py:93
  100.2 14.4 %copy-start.4 = (bf16[256,2,33,8]{2,3,1,0:T(8,128)(2,1)S(1)}, bf16[256,2,33,8]{2,3,1,0:T(8,128)(2,1)}, u32[]{:S(2)}) copy-start(bf16[256,2,33,8]{2,3,1,0:T(8,128)(2,1)} %get-tuple-element.13) | copy-start | bytes 811012
where the time goes:
time: 121 us; the launch traced here: 120 us
  local copies, waits for them, and re-layouts  37.6 us (31%)
  starting transfers between devices  23.3 us (19%)
  matrix products  19.7 us (16%)
  blocking collectives  16.7 us (14%)
  waiting for transfers between devices  15.9 us (13%)
  other arithmetic  5.56 us (5%)
    unnamed x16, local copies, waits for them, and re-layouts  19.6 us
    psum x1, blocking collectives, body(): low = lax.psum(low_part, 'tp').astype(jnp.bfloat16)  16.7 us
    all_to_all x1, starting transfers between devices, body(): lax.all_to_all(placed_rows, 'rows', split_axis=0, concat_axis=0, tiled=True)  13.2 us
    all_to_all x1, starting transfers between devices, body(): lax.all_to_all(delta_out, 'rows', split_axis=0, concat_axis=0, tiled=True)  10.2 us
    all_to_all x1, waiting for transfers between devices, body(): lax.all_to_all(placed_rows, 'rows', split_axis=0, concat_axis=0, tiled=True)  8.08 us
    reshape x1, local copies, waits for them, and re-layouts, body(): v_four = cache_values.reshape(rows_count, -1, heads_kv, HEAD)  7.97 us
    reshape x1, local copies, waits for them, and re-layouts, body(): k_four = cache_keys.reshape(rows_count, -1, heads_kv, HEAD)  7.96 us
    all_to_all x1, waiting for transfers between devices, body(): lax.all_to_all(delta_out, 'rows', split_axis=0, concat_axis=0, tiled=True)  7.86 us
  transfers between devices with their start and end apart: 2, of which 2 were waited for; matrix products, arithmetic and copies ran while one was open for 39% of the time, Pallas kernels for 0%

commit v1 on v0

v1 whole, which is shorter than its diff:
```python
import functools
import math

import jax
import jax.numpy as jnp
from jax import lax
from jax.experimental import pallas as pl
from jax.experimental.pallas import tpu as pltpu
from jax.sharding import PartitionSpec as P

HEAD = 128
MOST = 8
f32 = jnp.float32
bf16 = jnp.bfloat16
i32 = jnp.int32
NT = (((1,), (1,)), ((), ()))
VMEM_LIMIT = 48 * 1024 * 1024


def params():
    return pltpu.CompilerParams(vmem_limit_bytes=VMEM_LIMIT)


def iota(shape, dim):
    return lax.broadcasted_iota(i32, shape, dim)


def segment_rows(group, glist_ref, table_ref, lens_ref):
    slots = lens_ref.shape[1]
    adapters = table_ref.shape[1]
    listed = glist_ref[pl.ds(group, 1), :]
    hit = (iota((adapters, slots), 0) == listed).astype(f32)
    table = jnp.broadcast_to(table_ref[...].astype(f32), (8, adapters))
    position = jnp.dot(table, hit, preferred_element_type=f32)[:1]
    owner = jnp.right_shift(position.astype(i32), 1).astype(f32)
    lens = lens_ref[...].astype(f32)
    before = (iota((slots, slots), 0) < iota((slots, slots), 1)).astype(f32)
    start = jnp.dot(jnp.broadcast_to(lens, (8, slots)), before, preferred_element_type=f32)[:1]
    return owner, start, lens


def place_kernel(where_ref, glist_ref, table_ref, lens_ref, x_ref, out_ref, placing):
    slots = lens_ref.shape[1]
    rows = x_ref.shape[0]
    count = out_ref.shape[0]

    @pl.when(pl.program_id(0) == 0)
    def _():
        owner, start, lens = segment_rows(where_ref[0], glist_ref, table_ref, lens_ref)
        slot = iota((count, 1), 0)
        mine = owner == jnp.right_shift(slot, 3).astype(f32)
        first = jnp.sum(jnp.where(mine, start, 0.0), axis=1, keepdims=True)
        length = jnp.sum(jnp.where(mine, lens, 0.0), axis=1, keepdims=True)
        within = jnp.bitwise_and(slot, MOST - 1).astype(f32)
        source = jnp.where(within < length, first + within, -1.0)
        placing[...] = (iota((count, rows), 1).astype(f32) == source).astype(bf16)

    out_ref[...] = jnp.dot(placing[...], x_ref[...], preferred_element_type=f32).astype(bf16)


def place(where, glist, table, lens, rows_x, part, count):
    rows = rows_x.shape[0]
    steps = 4
    wide = part // steps
    return pl.pallas_call(
        place_kernel,
        out_shape=jax.ShapeDtypeStruct((count, part), bf16),
        grid_spec=pltpu.PrefetchScalarGridSpec(
            num_scalar_prefetch=1,
            grid=(steps,),
            in_specs=[
                pl.BlockSpec(glist.shape, lambda i, s: (0, 0)),
                pl.BlockSpec(table.shape, lambda i, s: (0, 0)),
                pl.BlockSpec(lens.shape, lambda i, s: (0, 0)),
                pl.BlockSpec((rows, wide), lambda i, s: (0, s[1] * steps + i)),
            ],
            out_specs=pl.BlockSpec((count, wide), lambda i, s: (0, i)),
            scratch_shapes=[pltpu.VMEM((count, rows), bf16)],
        ),
        compiler_params=params(),
    )(where, glist, table, lens, rows_x)


def unplace_kernel(where_ref, glist_ref, table_ref, lens_ref, out_ref):
    rows, count = out_ref.shape
    owner, start, lens = segment_rows(where_ref[0], glist_ref, table_ref, lens_ref)
    row = iota((rows, 1), 0).astype(f32)
    inside = (row >= start) & (row < start + lens)
    target = jnp.sum(jnp.where(inside, owner * MOST + row - start, 0.0), axis=1, keepdims=True)
    out_ref[...] = (iota((rows, count), 1).astype(f32) == target).astype(bf16)


def unplace(where, glist, table, lens, rows, count):
    return pl.pallas_call(
        unplace_kernel,
        out_shape=jax.ShapeDtypeStruct((rows, count), bf16),
        in_specs=[pl.BlockSpec(memory_space=pltpu.SMEM)]
        + [pl.BlockSpec(memory_space=pltpu.VMEM)] * 3,
        out_specs=pl.BlockSpec(memory_space=pltpu.VMEM),
        compiler_params=params(),
    )(where, glist, table, lens)


def second_of_slots(owner, glist_ref, table_ref, count):
    groups, adapters = glist_ref.shape[0], table_ref.shape[1]
    ids = iota((1, adapters), 1)
    second = jnp.max(jnp.where(table_ref[...] == 2 * owner + 1, ids, -1), axis=1, keepdims=True)
    uses = (glist_ref[...] == second).astype(f32)
    uses = jnp.max(uses, axis=1, keepdims=True)
    spread = (jnp.right_shift(iota((count, groups), 0), 3) == iota((count, groups), 1)).astype(f32)
    wide = jnp.dot(spread, jnp.broadcast_to(uses, (groups, 128)), preferred_element_type=f32)
    return wide > 0.5


def low_kernel(where_ref, glist_ref, table_ref, x_ref, a_ref, out_ref):
    count, half = x_ref.shape[0], x_ref.shape[0] // 2
    rank = a_ref.shape[0] // 2
    second = second_of_slots(where_ref[0], glist_ref, table_ref, count)
    each = lax.dot_general(x_ref[...], a_ref[...], NT, preferred_element_type=f32)
    turned = pltpu.roll(each, rank, 1)
    left = jnp.where(second, turned, each)
    right = jnp.where(second, each, turned)
    out_ref[...] = jnp.where(iota((half, 2 * rank), 1) < rank, left[:half], right[half:])


def delta_kernel(where_ref, glist_ref, table_ref, p0, p1, p2, p3, b_ref, out_ref):
    count = out_ref.shape[0]
    half, rank = count // 2, b_ref.shape[0] // 2
    second = second_of_slots(where_ref[0], glist_ref, table_ref, count)
    low = (p0[...] + p1[...]) + (p2[...] + p3[...])
    turned = pltpu.roll(low, rank, 1)
    lane = iota((half, 2 * rank), 1) < rank
    both = jnp.concatenate([jnp.where(lane, low, turned), jnp.where(lane, turned, low)], axis=0)
    keep = (iota((count, 2 * rank), 1) >= rank) == second
    low = jnp.where(keep, both, 0.0).astype(bf16)
    out_ref[...] = jnp.dot(low, b_ref[...], preferred_element_type=f32).astype(bf16)


def whole_call(kernel, shape, dtype, *args):
    return pl.pallas_call(
        kernel,
        out_shape=jax.ShapeDtypeStruct(shape, dtype),
        in_specs=[pl.BlockSpec(memory_space=pltpu.SMEM)]
        + [pl.BlockSpec(memory_space=pltpu.VMEM)] * (len(args) - 1),
        out_specs=pl.BlockSpec(memory_space=pltpu.VMEM),
        compiler_params=params(),
    )(*args)


def attend_kernel(scale, q_ref, nk_ref, k_ref, v_ref, len_ref, ctx_ref, own_ref):
    rows, cache, width = k_ref.shape
    kv_heads = width // HEAD
    group = q_ref.shape[1] // width
    many = 8 * group
    row = jnp.bitwise_and(iota((many, 128), 0), 7)
    lane = iota((many, 128), 1)
    upper = row >= 4
    place_ok = jnp.right_shift(lane, 5) == jnp.bitwise_and(row, 3)
    cell = jnp.bitwise_and(lane, cache - 1)
    lane8 = iota((8, 128), 1)
    for pair in range(rows // 16):
        q16 = q_ref[pl.ds(pair * 16, 16), :].astype(f32)
        nk16 = nk_ref[pl.ds(pair * 16, 16), :].astype(f32)
        for sub in range(2):
            base = pair * 16 + sub * 8
            q8 = q16[sub * 8 : sub * 8 + 8]
            nk8 = nk16[sub * 8 : sub * 8 + 8]
            keys = k_ref[pl.ds(base, 8)].reshape(8 * cache, width)
            values = v_ref[pl.ds(base, 8)].reshape(8 * cache, width)
            lens = jnp.concatenate([len_ref[pl.ds(base, 8), :]] * group, axis=0)
            valid = place_ok & (cell < lens)
            own_tile = jnp.zeros((8, 128), f32)
            for h in range(kv_heads):
                cut = slice(h * HEAD, (h + 1) * HEAD)
                q = jnp.concatenate(
                    [q8[:, (h * group + g) * HEAD : (h * group + g + 1) * HEAD] for g in range(group)],
                    axis=0,
                )
                score = lax.dot_general(
                    q.astype(bf16), keys[:, cut], NT, preferred_element_type=f32
                )
                score = jnp.where(upper, score[:, 128:], score[:, :128]) * scale
                score = jnp.where(valid, score, -1e30)
                own = jnp.sum(
                    q * jnp.concatenate([nk8[:, cut]] * group, axis=0), axis=1, keepdims=True
                ) * scale
                top = jnp.maximum(jnp.max(score, axis=1, keepdims=True), own)
                weight = jnp.where(valid, jnp.exp(score - top), 0.0)
                e_own = jnp.exp(own - top)
                inv = 1.0 / (jnp.sum(weight, axis=1, keepdims=True) + e_own)
                split = jnp.concatenate(
                    [jnp.where(upper, 0.0, weight), jnp.where(upper, weight, 0.0)], axis=1
                ).astype(bf16)
                ctx = jnp.dot(split, values[:, cut], preferred_element_type=f32) * inv
                w_own = e_own.astype(bf16).astype(f32) * inv
                for g in range(group):
                    head = h * group + g
                    ctx_ref[pl.ds(base, 8), head * HEAD : (head + 1) * HEAD] = ctx[g * 8 : g * 8 + 8]
                    own_tile = jnp.where(lane8 == head, w_own[g * 8 : g * 8 + 8], own_tile)
            own_ref[pl.ds(base, 8), :] = own_tile


def attend(queries, new_key, cache_keys, cache_values, lengths):
    rows, wide = queries.shape
    cache, width = cache_keys.shape[1:]
    step = 32
    return pl.pallas_call(
        functools.partial(attend_kernel, 1.0 / math.sqrt(HEAD)),
        out_shape=(
            jax.ShapeDtypeStruct((rows, wide), f32),
            jax.ShapeDtypeStruct((rows, 128), f32),
        ),
        grid=(rows // step,),
        in_specs=[
            pl.BlockSpec((step, wide), lambda i: (i, 0)),
            pl.BlockSpec((step, width), lambda i: (i, 0)),
            pl.BlockSpec((step, cache, width), lambda i: (i, 0, 0)),
            pl.BlockSpec((step, cache, width), lambda i: (i, 0, 0)),
            pl.BlockSpec((step, 1), lambda i: (i, 0)),
        ],
        out_specs=(
            pl.BlockSpec((step, wide), lambda i: (i, 0)),
            pl.BlockSpec((step, 128), lambda i: (i, 0)),
        ),
        compiler_params=params(),
    )(queries, new_key, cache_keys, cache_values, lengths)


def finish_kernel(un_ref, delta_ref, base_ref, ctx_ref, own_ref, value_ref, out_ref):
    heads = out_ref.shape[1] // HEAD
    group = out_ref.shape[1] // value_ref.shape[1]
    delta = jnp.dot(un_ref[...], delta_ref[...], preferred_element_type=f32)
    value = (base_ref[...] + delta).astype(bf16)
    value_ref[...] = value
    value = value.astype(f32)
    for head in range(heads):
        kv = head // group
        cut = slice(head * HEAD, (head + 1) * HEAD)
        out_ref[:, cut] = (
            ctx_ref[:, cut] + own_ref[:, head : head + 1] * value[:, kv * HEAD : (kv + 1) * HEAD]
        ).astype(bf16)


def finish(un, delta, base, ctx, own):
    rows, wide = ctx.shape
    step = 64
    by_row = lambda n: pl.BlockSpec((step, n), lambda i: (i, 0))
    return pl.pallas_call(
        finish_kernel,
        out_shape=(
            jax.ShapeDtypeStruct(base.shape, bf16),
            jax.ShapeDtypeStruct((rows, wide), bf16),
        ),
        grid=(rows // step,),
        in_specs=[
            by_row(un.shape[1]),
            pl.BlockSpec(delta.shape, lambda i: (0, 0)),
            by_row(base.shape[1]),
            by_row(wide),
            by_row(128),
        ],
        out_specs=(by_row(base.shape[1]), by_row(wide)),
        compiler_params=params(),
    )(un, delta, base, ctx, own)


def body(
    normed_rows,
    value_weight,
    adapter_a,
    adapter_b,
    page_table,
    group_list,
    seg_len,
    kv_len,
    queries,
    new_key,
    cache_keys,
    cache_values,
):
    tp = lax.axis_size("tp")
    groups = lax.axis_size("rows")
    rows = normed_rows.shape[0]
    part = normed_rows.shape[1] // tp
    per_owner, _, rank = adapter_a.shape
    width = adapter_b.shape[2]
    count = groups * MOST
    where = jnp.stack([lax.axis_index("rows"), lax.axis_index("tp")]).astype(i32)
    table = page_table.reshape(1, -1)
    a_turned = jnp.swapaxes(adapter_a, 1, 2).reshape(per_owner * rank, part)
    b_flat = adapter_b.reshape(per_owner * rank, width)

    placed = place(where, group_list, table, seg_len, normed_rows, part, count)
    arrived = lax.all_to_all(
        placed.reshape(groups, MOST, part), "rows", split_axis=0, concat_axis=0, tiled=True
    ).reshape(count, part)

    un = unplace(where, group_list, table, seg_len, rows, count)
    base = jnp.dot(normed_rows, value_weight, preferred_element_type=f32)
    ctx, own = attend(queries, new_key, cache_keys, cache_values, kv_len.reshape(-1, 1))

    arrived, un, base, ctx, own = lax.optimization_barrier((arrived, un, base, ctx, own))
    partial = whole_call(
        low_kernel, (count // 2, 2 * rank), f32, where, group_list, table, arrived, a_turned
    )
    others = [
        lax.ppermute(partial, "tp", [(j, (j + k) % tp) for j in range(tp)]) for k in range(1, tp)
    ]
    delta_out = whole_call(
        delta_kernel, (count, width), bf16, where, group_list, table, partial, *others, b_flat
    )
    delta = lax.all_to_all(
        delta_out.reshape(groups, MOST, width), "rows", split_axis=0, concat_axis=0, tiled=True
    ).reshape(count, width)
    return finish(un, delta, base, ctx, own)


def solution(mesh):
    return jax.shard_map(
        body,
        mesh=mesh,
        in_specs=(
            P("rows", None),
            P(None, "tp"),
            P("rows", "tp", None),
            P("rows", None, "tp"),
            P(),
            P(),
            P("rows", None),
            P("rows", None),
            P("rows", "tp"),
            P("rows", "tp"),
            P("rows", None, "tp"),
            P("rows", None, "tp"),
        ),
        out_specs=(P("rows", "tp"), P("rows", "tp")),
        check_vma=False,
    )
```

time: 121 us -> 108 us (0.89)
  local copies, waits for them, and re-layouts: 37.6 us -> 8.01 us
  Pallas kernels: 0 us -> 27.4 us
  matrix products: 19.7 us -> 1.25 us
  waiting for transfers between devices: 15.9 us -> 30.7 us
  starting transfers between devices: 23.3 us -> 16.8 us
  blocking collectives: 16.7 us -> 22.8 us
  other arithmetic: 5.56 us -> 0.08 us
    pallas_call x0 -> x6, Pallas kernels: none -> 27.4 us  [the longest x1 17.8 us: attend(): pl.pallas_call(functools.partial(attend_kernel, 1.0 / math.sqrt(HEAD)), o...]
    all_to_all x0 -> x1, blocking collectives: none -> 22.8 us  [body(): lax.all_to_all(delta_out.reshape(groups, MOST, width), 'rows', split_axis...]
    dot_general x7 -> x1, matrix products: 19.7 us -> 1.25 us  [body(): base = jnp.dot(normed_rows, value_weight, preferred_element_type=f32)]
    psum x1 -> x0, blocking collectives: 16.7 us -> none  [body(): low = lax.psum(low_part, 'tp').astype(jnp.bfloat16)]
    reshape x4 -> x1, local copies, waits for them, and re-layouts: 16.7 us -> 0.8 us  [body(): kv_len.reshape(-1, 1)]
    unnamed x16 -> x38, local copies, waits for them, and re-layouts: 19.6 us -> 7.21 us
    all_to_all x2 -> x1, starting transfers between devices: 23.3 us -> 13.2 us  [body(): lax.all_to_all(placed.reshape(groups, MOST, part), 'rows', split_axis=0,...]
    all_to_all x2 -> x1, waiting for transfers between devices: 15.9 us -> 25.1 us  [body(): lax.all_to_all(placed.reshape(groups, MOST, part), 'rows', split_axis=0,...]
  transfers between devices with their start and end apart: 2 -> 4, of which waited for: 2 -> 4; matrix products, arithmetic and copies ran while one was open for 39% -> 2% of each run, Pallas kernels for 0% -> 17%
where the time goes in v1:
time: 108 us
  waiting for transfers between devices  30.7 us (28%)
  Pallas kernels  27.4 us (25%)
  blocking collectives  22.8 us (21%)
  starting transfers between devices  16.8 us (16%)
  local copies, waits for them, and re-layouts  8.01 us (7%)
  matrix products  1.25 us (1%)
    all_to_all x1, waiting for transfers between devices, body(): lax.all_to_all(placed.reshape(groups, MOST, part), 'rows', split_axis=0,...  25.1 us
    all_to_all x1, blocking collectives, body(): lax.all_to_all(delta_out.reshape(groups, MOST, width), 'rows', split_axis...  22.8 us
    pallas_call x1, Pallas kernels, attend(): pl.pallas_call(functools.partial(attend_kernel, 1.0 / math.sqrt(HEAD)), o...  17.8 us
    all_to_all x1, starting transfers between devices, body(): lax.all_to_all(placed.reshape(groups, MOST, part), 'rows', split_axis=0,...  13.2 us
    unnamed x38, local copies, waits for them, and re-layouts  7.21 us
    ppermute x3, waiting for transfers between devices, body(): lax.ppermute(partial, 'tp', [(j, (j + k) % tp) for j in range(tp)])  5.59 us
    pallas_call x1, Pallas kernels, place(): pl.pallas_call(place_kernel, out_shape=jax.ShapeDtypeStruct((count, part)...  3.86 us
    ppermute x3, starting transfers between devices, body(): lax.ppermute(partial, 'tp', [(j, (j + k) % tp) for j in range(tp)])  3.69 us
  transfers between devices with their start and end apart: 4, of which 4 were waited for; matrix products, arithmetic and copies ran while one was open for 2% of the time, Pallas kernels for 17%

profile of v1, /device:TPU:1, one launch (start us, length us, event | category | flops | bytes accessed | tf_op | source)
XLA Modules:
  0.0 107.8 jit_solution(2533539016696054468)
XLA Ops:
  0.6 0.1 pad_add_fusion.where_ref
  0.7 0.0 copy-start.4
  0.7 0.8 copy-done.4
  1.5 0.0 copy-start.12
  1.5 0.7 copy-done.12
  2.1 0.0 copy-start.14
  2.1 0.7 copy-done.14
  2.8 0.0 copy-start.5
  2.8 0.0 copy-start.13
  2.8 0.0 copy-start.15
  2.8 0.0 copy-start.17
  2.8 0.0 copy-start.3
  2.8 3.9 %shard_map.131 = bf16[512,2048]{1,0:T(8,128)(2,1)S(1)} custom-call(s32[2]{0:T(128)S(1)} %pad_add_fusion.where_ref, s32[64,64]{1,0:T(8,128)S(1)} %copy-done.4, s32[1,128]{1,0:T(1,128)S(1)} %bitcast.20, s32[1,64]{1,0:T(1,128)S(1)} %copy-done.14, bf16[256,8192]{1,0:T(8,128)(2,1)} %x_ref.1), custom_call_target="tpu_custom_call" | custom-call | tf_op jit(solution)/shard_map/pallas_call | solution.py:65
  6.7 0.0 copy-start
  6.7 1.3 %copy-done = bf16[512,2048]{1,0:T(8,128)(2,1)} copy-done((bf16[512,2048]{1,0:T(8,128)(2,1)}, bf16[512,2048]{1,0:T(8,128)(2,1)S(1)}, u32[]{:S(2)}) %copy-start) | copy-done | bytes 2097176
  8.0 13.2 %all-to-all-start = ((bf16[64,8,2048]{2,1,0:T(8,128)(2,1)}), bf16[64,8,2048]{2,1,0:T(8,128)(2,1)S(1)}, u32[]{:S(2)}, u32[]{:S(2)}) async-start(bf16[64,8,2048]{2,1,0:T(8,128)(2,1)} %bitcast.15), calls=%async_computation | async-start | bytes 4194304 | tf_op jit(solution)/shard_map/all_to_all | solution.py:294
  21.2 0.0 copy-done.5
  21.2 0.0 copy-done.13
  21.2 0.0 copy-done.15
  21.2 0.8 shard_map.132.un_ref
  22.0 0.0 copy-done.17
  22.0 0.8 copy.14.len_ref
  22.8 0.0 copy-done.3
  22.8 0.9 copy-done.6
  23.7 0.9 copy-done.8
  24.6 17.8 %shard_map.133 = (f32[256,2048]{1,0:T(8,128)S(1)}, f32[256,128]{1,0:T(8,128)S(1)}) custom-call(bf16[256,2048]{1,0:T(8,128)(2,1)S(1)} %copy-done.3, bf16[256,256]{1,0:T(8,128)(2,1)S(1)} %copy-done.8, bf16[256,32,256]{2,1,0:T(8,128)(2,1)} %k_ref.1, bf16[256,32,256]{2,1,0:T(8,128)(2,1)} %v_ref.1, s32[256,1]{1,0:T(8,128)S(1)} %copy-done.6), custom_call_target="tpu_custom_call" | custom-call | tf_op jit(solution)/shard_map/pallas_call | solution.py:207
  42.5 0.0 copy-start.1
  42.5 1.3 %copy-done.1 = f32[256,2048]{1,0:T(8,128)} copy-done((f32[256,2048]{1,0:T(8,128)}, f32[256,2048]{1,0:T(8,128)S(1)}, u32[]{:S(2)}) %copy-start.1) | copy-done | bytes 2097176
  43.8 0.7 copy-done.9
  44.4 0.0 copy-done.16
  44.4 0.0 copy-done.18
  44.5 1.2 %fusion.base_ref = f32[256,256]{1,0:T(8,128)S(1)} fusion(bf16[256,8192]{1,0:T(8,128)(2,1)S(1)} %copy-done.16, bf16[8192,256]{1,0:T(8,128)(2,1)S(1)} %copy-done.18), kind=kOutput, calls=%fused_computation.1 | convolution fusion | flops 1073741824 | bytes 8650752 | tf_op jit(solution)/shard_map/dot_general | solution.py:299
  45.7 0.0 copy-start.10
  45.7 25.1 %all-to-all-done = bf16[64,8,2048]{2,1,0:T(8,128)(2,1)S(1)} async-done(((bf16[64,8,2048]{2,1,0:T(8,128)(2,1)}), bf16[64,8,2048]{2,1,0:T(8,128)(2,1)S(1)}, u32[]{:S(2)}, u32[]{:S(2)}) %all-to-all-start) | async-done | bytes 2097184 | tf_op jit(solution)/shard_map/all_to_all | solution.py:294
  70.8 0.0 copy-done.7
  70.8 1.6 %shard_map.134.p0 = f32[256,128]{1,0:T(8,128)S(1)} custom-call(s32[2]{0:T(128)S(1)} %pad_add_fusion.where_ref, s32[64,64]{1,0:T(8,128)S(1)} %copy-done.5, s32[1,128]{1,0:T(1,128)S(1)} %bitcast.22, bf16[512,2048]{1,0:T(8,128)(2,1)S(1)} %bitcast.14, bf16[128,2048]{1,0:T(8,128)(2,1)S(1)} %bitcast.18), custom_call_target="tpu_custom_call" | custom-call | tf_op jit(solution)/shard_map/pallas_call | solution.py:140
  72.4 2.6 %collective-permute-start.2 = (f32[256,128]{1,0:T(8,128)S(1)}, f32[256,128]{1,0:T(8,128)S(1)}, u32[]{:S(2)}, u32[]{:S(2)}) collective-permute-start(f32[256,128]{1,0:T(8,128)S(1)} %shard_map.134.p0), channel_id=1, source_target_pairs={{0,3},{1,0},{2,1},{3,2},{4,7},{5,4},{6,5},{7,6},{8,11},{9,8},{10,9... | collective-permute-start | bytes 393224 | tf_op jit(solution)/shard_map/ppermute | solution.py:307
  75.0 0.5 collective-permute-start.1
  75.5 0.6 collective-permute-start
  76.1 1.6 %collective-permute-done.2.p3 = f32[256,128]{1,0:T(8,128)S(1)} collective-permute-done((f32[256,128]{1,0:T(8,128)S(1)}, f32[256,128]{1,0:T(8,128)S(1)}, u32[]{:S(2)}, u32[]{:S(2)}) %collective-permute-start.2) | collective-permute-done | bytes 131104 | tf_op jit(solution)/shard_map/ppermute | solution.py:307
  77.7 2.7 %collective-permute-done.1.p2 = f32[256,128]{1,0:T(8,128)S(1)} collective-permute-done((f32[256,128]{1,0:T(8,128)S(1)}, f32[256,128]{1,0:T(8,128)S(1)}, u32[]{:S(2)}, u32[]{:S(2)}) %collective-permute-start.1) | collective-permute-done | bytes 131104 | tf_op jit(solution)/shard_map/ppermute | solution.py:307
  80.4 1.3 %collective-permute-done.p1 = f32[256,128]{1,0:T(8,128)S(1)} collective-permute-done((f32[256,128]{1,0:T(8,128)S(1)}, f32[256,128]{1,0:T(8,128)S(1)}, u32[]{:S(2)}, u32[]{:S(2)}) %collective-permute-start) | collective-permute-done | bytes 131104 | tf_op jit(solution)/shard_map/ppermute | solution.py:307
  81.7 0.0 copy-done.11
  81.7 1.2 %shard_map.135 = bf16[512,256]{1,0:T(8,128)(2,1)S(1)} custom-call(s32[2]{0:T(128)S(1)} %pad_add_fusion.where_ref, s32[64,64]{1,0:T(8,128)S(1)} %copy-done.5, s32[1,128]{1,0:T(1,128)S(1)} %bitcast.23, f32[256,128]{1,0:T(8,128)S(1)} %shard_map.134.p0, f32[256,128]{1,0:T(8,128)S(1)} %collective-permute-done.p1, f32[256,128]{1,0:T(8,128)S(1)} %collective-permute-done.1.p2, ...), custom_call_target="tpu_custom_call" | custom-call | tf_op jit(solution)/shard_map/pallas_call | solution.py:140
  82.9 22.8 %all_to_all.10 = bf16[64,8,256]{2,1,0:T(8,128)(2,1)S(1)} all-to-all(bf16[64,8,256]{2,1,0:T(8,128)(2,1)S(1)} %bitcast.17), channel_id=1, replica_groups=mesh['rows'=64,'tp'=4] {'rows'}, dimensions={0} | all-to-all | bytes 524288 | tf_op jit(solution)/shard_map/all_to_all | solution.py:312
  105.6 0.0 copy-done.10
  105.7 0.0 copy-done.2
  105.7 2.2 %shard_map.136 = (bf16[256,256]{1,0:T(8,128)(2,1)}, bf16[256,2048]{1,0:T(8,128)(2,1)}) custom-call(bf16[256,512]{1,0:T(8,128)(2,1)S(1)} %shard_map.132.un_ref, bf16[512,256]{1,0:T(8,128)(2,1)S(1)} %bitcast.16, f32[256,256]{1,0:T(8,128)S(1)} %fusion.base_ref, f32[256,2048]{1,0:T(8,128)S(1)} %copy-done.2, f32[256,128]{1,0:T(8,128)S(1)} %copy-done.10), custom_call_target="tpu_custom_call" | custom-call | tf_op jit(solution)/shard_map/pallas_call | solution.py:248
  (8 shorter events, 0.0 us)
Async XLA Ops:
  0.7 0.8 copy-start.4
  1.5 0.7 copy-start.12
  2.1 0.7 copy-start.14
  2.8 18.4 %copy-start.5 = (s32[64,64]{1,0:T(8,128)S(1)}, s32[64,64]{1,0:T(8,128)}, u32[]{:S(2)}) copy-start(s32[64,64]{1,0:T(8,128)} %glist_ref.7) | copy-start | bytes 49156
  2.8 18.4 %copy-start.13 = (s32[128]{0:T(128)S(1)}, s32[128]{0:T(128)}, u32[]{:S(2)}) copy-start(s32[128]{0:T(128)} %param.16) | copy-start | bytes 1540
  2.8 18.4 %copy-start.15 = (s32[1,64]{1,0:T(1,128)S(1)}, s32[1,64]{1,0:T(1,128)}, u32[]{:S(2)}) copy-start(s32[1,64]{1,0:T(1,128)} %lens_ref.3) | copy-start | bytes 772
  2.8 19.2 %copy-start.17 = (s32[1,256]{1,0:T(1,128)S(1)}, s32[1,256]{1,0:T(1,128)}, u32[]{:S(2)}) copy-start(s32[1,256]{1,0:T(1,128)} %param.19) | copy-start | bytes 3076
  2.8 20.0 %copy-start.3 = (bf16[256,2048]{1,0:T(8,128)(2,1)S(1)}, bf16[256,2048]{1,0:T(8,128)(2,1)}, u32[]{:S(2)}) copy-start(bf16[256,2048]{1,0:T(8,128)(2,1)} %q_ref.1) | copy-start | bytes 3145732
  6.7 1.3 %copy-start = (bf16[512,2048]{1,0:T(8,128)(2,1)}, bf16[512,2048]{1,0:T(8,128)(2,1)S(1)}, u32[]{:S(2)}) copy-start(bf16[512,2048]{1,0:T(8,128)(2,1)S(1)} %shard_map.131) | copy-start | bytes 6291460
  8.0 62.8 %all-to-all-start = ((bf16[64,8,2048]{2,1,0:T(8,128)(2,1)}), bf16[64,8,2048]{2,1,0:T(8,128)(2,1)S(1)}, u32[]{:S(2)}, u32[]{:S(2)}) async-start(bf16[64,8,2048]{2,1,0:T(8,128)(2,1)} %bitcast.15), calls=%async_computation | async-start | bytes 4194304 | tf_op jit(solution)/shard_map/all_to_all | solution.py:294
  22.8 0.9 copy-start.6
  23.7 0.9 copy-start.8
  24.6 19.8 %copy-start.16 = (bf16[256,8192]{1,0:T(8,128)(2,1)S(1)}, bf16[256,8192]{1,0:T(8,128)(2,1)}, u32[]{:S(2)}) copy-start(bf16[256,8192]{1,0:T(8,128)(2,1)} %x_ref.1) | copy-start | bytes 12582916
  24.6 19.8 %copy-start.18 = (bf16[8192,256]{1,0:T(8,128)(2,1)S(1)}, bf16[8192,256]{1,0:T(8,128)(2,1)}, u32[]{:S(2)}) copy-start(bf16[8192,256]{1,0:T(8,128)(2,1)} %param.13) | copy-start | bytes 12582916
  42.5 1.3 %copy-start.1 = (f32[256,2048]{1,0:T(8,128)}, f32[256,2048]{1,0:T(8,128)S(1)}, u32[]{:S(2)}) copy-start(f32[256,2048]{1,0:T(8,128)S(1)} %get-tuple-element.14.ctx_ref) | copy-start | bytes 6291460
  43.8 0.7 copy-start.9
  44.4 26.4 %copy-start.7 = (bf16[2,2048,64]{1,2,0:T(8,128)(2,1)S(1)}, bf16[2,2048,64]{1,2,0:T(8,128)(2,1)}, u32[]{:S(2)}) copy-start(bf16[2,2048,64]{1,2,0:T(8,128)(2,1)} %param.14) | copy-start | bytes 1572868
  44.4 37.3 %copy-start.11 = (bf16[2,64,256]{2,1,0:T(8,128)(2,1)S(1)}, bf16[2,64,256]{2,1,0:T(8,128)(2,1)}, u32[]{:S(2)}) copy-start(bf16[2,64,256]{2,1,0:T(8,128)(2,1)} %param.15) | copy-start | bytes 196612
  45.7 59.9 %copy-start.10 = (f32[256,128]{1,0:T(8,128)S(1)}, f32[256,128]{1,0:T(8,128)}, u32[]{:S(2)}) copy-start(f32[256,128]{1,0:T(8,128)} %copy-done.9) | copy-start | bytes 393220
  70.8 34.8 %copy-start.2 = (f32[256,2048]{1,0:T(8,128)S(1)}, f32[256,2048]{1,0:T(8,128)}, u32[]{:S(2)}) copy-start(f32[256,2048]{1,0:T(8,128)} %copy-done.1) | copy-start | bytes 6291460
  72.4 5.3 %collective-permute-start.2 = (f32[256,128]{1,0:T(8,128)S(1)}, f32[256,128]{1,0:T(8,128)S(1)}, u32[]{:S(2)}, u32[]{:S(2)}) collective-permute-start(f32[256,128]{1,0:T(8,128)S(1)} %shard_map.134.p0), channel_id=1, source_target_pairs={{0,3},{1,0},{2,1},{3,2},{4,7},{5,4},{6,5},{7,6},{8,11},{9,8},{10,9... | collective-permute-start | bytes 393224 | tf_op jit(solution)/shard_map/ppermute | solution.py:307
  75.0 5.4 %collective-permute-start.1 = (f32[256,128]{1,0:T(8,128)S(1)}, f32[256,128]{1,0:T(8,128)S(1)}, u32[]{:S(2)}, u32[]{:S(2)}) collective-permute-start(f32[256,128]{1,0:T(8,128)S(1)} %shard_map.134.p0), channel_id=1, source_target_pairs={{0,2},{1,3},{2,0},{3,1},{4,6},{5,7},{6,4},{7,5},{8,10},{9,11},{10,... | collective-permute-start | bytes 393224 | tf_op jit(solution)/shard_map/ppermute | solution.py:307
  75.5 6.2 %collective-permute-start = (f32[256,128]{1,0:T(8,128)S(1)}, f32[256,128]{1,0:T(8,128)S(1)}, u32[]{:S(2)}, u32[]{:S(2)}) collective-permute-start(f32[256,128]{1,0:T(8,128)S(1)} %shard_map.134.p0), channel_id=1, source_target_pairs={{0,1},{1,2},{2,3},{3,0},{4,5},{5,6},{6,7},{7,4},{8,9},{9,10},{10,1... | collective-permute-start | bytes 393224 | tf_op jit(solution)/shard_map/ppermute | solution.py:307

commit v2 on v1

v2 whole, which is shorter than its diff:
```python
import functools
import math

import jax
import jax.numpy as jnp
from jax import lax
from jax.experimental import pallas as pl
from jax.experimental.pallas import tpu as pltpu
from jax.sharding import PartitionSpec as P

HEAD = 128
PLANE = 8
MOST = 8
f32 = jnp.float32
bf16 = jnp.bfloat16
i32 = jnp.int32
NT = (((1,), (1,)), ((), ()))
MIB = 1024 * 1024


FREE = pl.CostEstimate(flops=0, bytes_accessed=0, transcendentals=0)


def params(mib=12):
    return pltpu.CompilerParams(vmem_limit_bytes=mib * MIB)


def iota(shape, dim):
    return lax.broadcasted_iota(i32, shape, dim)


def segment_rows(meta):
    slots, groups = meta.slots, meta.groups
    adapters = meta.adapters
    listed = meta.ref[pl.ds(lax.axis_index("rows"), 1), :slots]
    hit = (iota((adapters, slots), 0) == listed).astype(f32)
    table = jnp.broadcast_to(meta.table().astype(f32), (8, adapters))
    position = jnp.dot(table, hit, preferred_element_type=f32)[:1]
    owner = jnp.right_shift(position.astype(i32), 1).astype(f32)
    lens = meta.ref[groups + 1 : groups + 2, :slots].astype(f32)
    before = (iota((slots, slots), 0) < iota((slots, slots), 1)).astype(f32)
    start = jnp.dot(jnp.broadcast_to(lens, (8, slots)), before, preferred_element_type=f32)[:1]
    return owner, start, lens


class Meta:
    def __init__(self, ref, groups, slots, adapters):
        self.ref, self.groups, self.slots, self.adapters = ref, groups, slots, adapters

    def table(self):
        return self.ref[self.groups : self.groups + 1, : self.adapters]


def column(plane):
    rows = lax.axis_index("rows")
    at = lax.rem(rows, plane)
    return lax.div(rows, plane), lax.div(at, 2), lax.rem(at, 2)


def owner_at(z, k, y, core, plane):
    half = plane // 2
    owner_y = lax.rem(lax.rem(k, half) + y, half)
    owner_core = lax.rem(lax.div(k, half) + core, 2)
    return z * plane + owner_y * 2 + owner_core


def slot_owner(slot, y, core, plane):
    k = lax.rem(jnp.right_shift(slot, 3), plane)
    return owner_at(lax.div(slot, plane * MOST), k, y, core, plane)


def place_kernel(plane, sizes, meta_ref, x_ref, out_ref, token_ref):
    count = out_ref.shape[0]
    rows = x_ref.shape[0]
    token_ref[...] = jnp.zeros_like(token_ref)
    owner, start, lengths = segment_rows(Meta(meta_ref, *sizes))
    _, y, core = column(plane)
    slot = iota((count, 1), 0)
    mine = owner == slot_owner(slot, y, core, plane).astype(f32)
    begin = jnp.sum(jnp.where(mine, start, 0.0), axis=1, keepdims=True)
    length = jnp.sum(jnp.where(mine, lengths, 0.0), axis=1, keepdims=True)
    within = jnp.bitwise_and(slot, MOST - 1).astype(f32)
    source = jnp.where(within < length, begin + within, -1.0)
    placing = (iota((count, rows), 1).astype(f32) == source).astype(bf16)
    out_ref[...] = jnp.dot(placing, x_ref[...], preferred_element_type=f32).astype(bf16)


def place(sizes, meta, x_part, count):
    part = x_part.shape[1]
    vmem = pl.BlockSpec(memory_space=pltpu.VMEM)
    return pl.pallas_call(
        functools.partial(place_kernel, PLANE, sizes),
        out_shape=(
            jax.ShapeDtypeStruct((count, part), bf16),
            jax.ShapeDtypeStruct((8, 128), i32),
        ),
        in_specs=[vmem, vmem],
        out_specs=(vmem, vmem),
        compiler_params=params(),
    )(meta, x_part)


def unplace_kernel(plane, sizes, meta_ref, token_ref, out_ref):
    rows, count = out_ref.shape
    owner, start, lens = segment_rows(Meta(meta_ref, *sizes))
    _, y, core = column(plane)
    row = iota((rows, 1), 0).astype(f32)
    inside = (row >= start) & (row < start + lens)
    target = jnp.sum(jnp.where(inside, owner * MOST + row - start, 0.0), axis=1, keepdims=True)
    slot = iota((1, count), 1)
    meant = slot_owner(slot, y, core, plane) * MOST + jnp.bitwise_and(slot, MOST - 1)
    out_ref[...] = (meant.astype(f32) == target).astype(bf16)


def choose_kernel(plane, sizes, meta_ref, token_ref, out_ref):
    meta = Meta(meta_ref, *sizes)
    count = out_ref.shape[0]
    planes = meta.groups // plane
    z, y, core = column(plane)
    at = lax.rem(lax.axis_index("rows"), plane)
    listed = jnp.concatenate(
        [meta_ref[pl.ds(p * plane + at, 1), : meta.slots] for p in range(planes)], axis=0
    )
    table = meta.table()
    ids = iota((1, meta.adapters), 1)
    lane = iota((planes, 128), 1)
    uses = jnp.zeros((planes, 128), f32)
    for k in range(plane):
        owner = owner_at(z, k, y, core, plane)
        second = jnp.max(jnp.where(table == 2 * owner + 1, ids, -1), axis=1, keepdims=True)
        hit = jnp.max((listed == second).astype(f32), axis=1, keepdims=True)
        uses = jnp.where(lane == k, hit, uses)
    row = iota((count, 1), 0)
    both = 2 * MOST
    k_of = lax.div(row, both * planes) * 2 + jnp.bitwise_and(jnp.right_shift(row, 3), 1)
    from_z = lax.rem(lax.div(row, both), planes)
    spread = (from_z == iota((count, planes), 1)).astype(f32)
    wide = jnp.dot(spread, uses, preferred_element_type=f32)
    mine = iota((count, 128), 1) == k_of
    out_ref[...] = jnp.broadcast_to(
        jnp.sum(jnp.where(mine, wide, 0.0), axis=1, keepdims=True), out_ref.shape
    )


def low_kernel(plane, choice_ref, x_ref, near_ref, far_ref, out_ref):
    count, part = x_ref.shape
    half, both = out_ref.shape
    rank = both // 2
    tile = 2 * MOST
    stride = plane * MOST
    pairs = []
    for pair in range(plane // 2):
        ref = near_ref if pair < plane // 4 else far_ref
        first = pair % (plane // 4) * 2
        a = jnp.concatenate([ref[first, :part], ref[first + 1, :part]], axis=1)
        x = jnp.concatenate(
            [x_ref[at : at + tile, :] for at in range(pair * tile, count, stride)], axis=0
        )
        each = jnp.dot(x, a, preferred_element_type=f32)
        odd = jnp.bitwise_and(iota((each.shape[0], both), 0), MOST) > 0
        pairs.append(jnp.where(odd, each[:, both:], each[:, :both]))
    total = jnp.concatenate(pairs, axis=0)
    second = choice_ref[...] > 0.5
    turned = pltpu.roll(total, rank, 1)
    left = jnp.where(second, turned, total)
    right = jnp.where(second, total, turned)
    out_ref[...] = jnp.where(iota((half, both), 1) < rank, left[:half], right[half:])


def delta_kernel(plane, choice_ref, p0, p1, p2, p3, maps_ref, out_ref):
    count, width = out_ref.shape
    half, both = p0.shape
    rank = both // 2
    tile = 2 * MOST
    stride = plane * MOST
    low = (p0[...] + p1[...]) + (p2[...] + p3[...])
    turned = pltpu.roll(low, rank, 1)
    lane = iota((half, both), 1) < rank
    twice = jnp.concatenate([jnp.where(lane, low, turned), jnp.where(lane, turned, low)], axis=0)
    keep = (iota((count, both), 1) >= rank) == (choice_ref[...] > 0.5)
    low = jnp.where(keep, twice, 0.0)
    odd = jnp.bitwise_and(iota((count, both), 0), MOST) > 0
    spread = jnp.concatenate(
        [jnp.where(odd, 0.0, low), jnp.where(odd, low, 0.0)], axis=1
    ).astype(bf16)
    many = count // (plane // 2)
    for pair in range(plane // 2):
        wide = [
            jnp.concatenate([maps_ref[k, at : at + both] for at in range(0, width, both)], axis=1)
            for k in (2 * pair, 2 * pair + 1)
        ]
        got = jnp.dot(
            spread[pair * many : (pair + 1) * many],
            jnp.concatenate(wide, axis=0),
            preferred_element_type=f32,
        ).astype(bf16)
        for i in range(many // tile):
            at = i * stride + pair * tile
            out_ref[at : at + tile, :] = got[i * tile : (i + 1) * tile]


def vmem_call(kernel, shape, dtype, *args):
    return pl.pallas_call(
        kernel,
        out_shape=jax.ShapeDtypeStruct(shape, dtype),
        in_specs=[pl.BlockSpec(memory_space=pltpu.VMEM)] * len(args),
        out_specs=pl.BlockSpec(memory_space=pltpu.VMEM),
        cost_estimate=FREE,
        compiler_params=params(),
    )(*args)


def attend_kernel(scale, q_ref, nk_ref, k_ref, v_ref, len_ref, ctx_ref, own_ref):
    rows, cache, width = k_ref.shape
    kv_heads = width // HEAD
    group = q_ref.shape[1] // width
    many = 8 * group
    row = jnp.bitwise_and(iota((many, 128), 0), 7)
    lane = iota((many, 128), 1)
    upper = row >= 4
    place_ok = jnp.right_shift(lane, 5) == jnp.bitwise_and(row, 3)
    cell = jnp.bitwise_and(lane, cache - 1)
    lane8 = iota((8, 128), 1)
    for pair in range(rows // 16):
        q16 = q_ref[pl.ds(pair * 16, 16), :].astype(f32)
        nk16 = nk_ref[pl.ds(pair * 16, 16), :].astype(f32)
        for sub in range(2):
            base = pair * 16 + sub * 8
            q8 = q16[sub * 8 : sub * 8 + 8]
            nk8 = nk16[sub * 8 : sub * 8 + 8]
            keys = k_ref[pl.ds(base, 8)].reshape(8 * cache, width)
            values = v_ref[pl.ds(base, 8)].reshape(8 * cache, width)
            lens = jnp.concatenate([len_ref[pl.ds(base, 8), :]] * group, axis=0)
            valid = place_ok & (cell < lens)
            own_tile = jnp.zeros((8, 128), f32)
            for h in range(kv_heads):
                cut = slice(h * HEAD, (h + 1) * HEAD)
                q = jnp.concatenate(
                    [q8[:, (h * group + g) * HEAD : (h * group + g + 1) * HEAD] for g in range(group)],
                    axis=0,
                )
                score = lax.dot_general(
                    q.astype(bf16), keys[:, cut], NT, preferred_element_type=f32
                )
                score = jnp.where(upper, score[:, 128:], score[:, :128]) * scale
                score = jnp.where(valid, score, -1e30)
                own = jnp.sum(
                    q * jnp.concatenate([nk8[:, cut]] * group, axis=0), axis=1, keepdims=True
                ) * scale
                top = jnp.maximum(jnp.max(score, axis=1, keepdims=True), own)
                weight = jnp.where(valid, jnp.exp(score - top), 0.0)
                e_own = jnp.exp(own - top)
                inv = 1.0 / (jnp.sum(weight, axis=1, keepdims=True) + e_own)
                split = jnp.concatenate(
                    [jnp.where(upper, 0.0, weight), jnp.where(upper, weight, 0.0)], axis=1
                ).astype(bf16)
                ctx = jnp.dot(split, values[:, cut], preferred_element_type=f32) * inv
                w_own = e_own.astype(bf16).astype(f32) * inv
                for g in range(group):
                    head = h * group + g
                    ctx_ref[pl.ds(base, 8), head * HEAD : (head + 1) * HEAD] = ctx[g * 8 : g * 8 + 8]
                    own_tile = jnp.where(lane8 == head, w_own[g * 8 : g * 8 + 8], own_tile)
            own_ref[pl.ds(base, 8), :] = own_tile


def attend(queries, new_key, cache_keys, cache_values, lengths):
    rows, wide = queries.shape
    cache, width = cache_keys.shape[1:]
    step = 32
    return pl.pallas_call(
        functools.partial(attend_kernel, 1.0 / math.sqrt(HEAD)),
        out_shape=(
            jax.ShapeDtypeStruct((rows, wide), f32),
            jax.ShapeDtypeStruct((rows, 128), f32),
        ),
        grid=(rows // step,),
        in_specs=[
            pl.BlockSpec((step, wide), lambda i: (i, 0)),
            pl.BlockSpec((step, width), lambda i: (i, 0)),
            pl.BlockSpec((step, cache, width), lambda i: (i, 0, 0)),
            pl.BlockSpec((step, cache, width), lambda i: (i, 0, 0)),
            pl.BlockSpec((step, 1), lambda i: (i, 0)),
        ],
        out_specs=(
            pl.BlockSpec((step, wide), lambda i: (i, 0)),
            pl.BlockSpec((step, 128), lambda i: (i, 0)),
        ),
        cost_estimate=FREE,
        compiler_params=params(),
    )(queries, new_key, cache_keys, cache_values, lengths)


def finish_kernel(un_ref, delta_ref, base_ref, ctx_ref, own_ref, value_ref, out_ref):
    heads = out_ref.shape[1] // HEAD
    group = out_ref.shape[1] // value_ref.shape[1]
    delta = jnp.dot(un_ref[...], delta_ref[...], preferred_element_type=f32)
    value = (base_ref[...] + delta).astype(bf16)
    value_ref[...] = value
    value = value.astype(f32)
    for head in range(heads):
        kv = head // group
        cut = slice(head * HEAD, (head + 1) * HEAD)
        out_ref[:, cut] = (
            ctx_ref[:, cut] + own_ref[:, head : head + 1] * value[:, kv * HEAD : (kv + 1) * HEAD]
        ).astype(bf16)


def finish(un, delta, base, ctx, own):
    rows, wide = ctx.shape
    step = 64
    by_row = lambda n: pl.BlockSpec((step, n), lambda i: (i, 0))
    whole = lambda a: pl.BlockSpec(a.shape, lambda i: (0, 0))
    return pl.pallas_call(
        finish_kernel,
        out_shape=(
            jax.ShapeDtypeStruct(base.shape, bf16),
            jax.ShapeDtypeStruct((rows, wide), bf16),
        ),
        grid=(rows // step,),
        in_specs=[
            by_row(un.shape[1]),
            whole(delta),
            by_row(base.shape[1]),
            by_row(wide),
            by_row(128),
        ],
        out_specs=(by_row(base.shape[1]), by_row(wide)),
        compiler_params=params(),
    )(un, delta, base, ctx, own)


def body(
    normed_rows,
    value_weight,
    adapter_a,
    adapter_b,
    page_table,
    group_list,
    seg_len,
    kv_len,
    queries,
    new_key,
    cache_keys,
    cache_values,
):
    tp = lax.axis_size("tp")
    groups = lax.axis_size("rows")
    planes = groups // PLANE
    rows = normed_rows.shape[0]
    part = normed_rows.shape[1] // tp
    per_owner, _, rank = adapter_a.shape
    width = adapter_b.shape[2]
    count = groups * MOST
    slots, adapters = group_list.shape[1], page_table.shape[0]
    sizes = (groups, slots, adapters)
    wide = lambda x: jnp.pad(x, ((0, 0), (0, 128 - x.shape[1])))
    meta = jnp.concatenate([wide(group_list), wide(page_table.reshape(1, -1)), wide(seg_len)], axis=0)
    columns = [[z * PLANE + at for z in range(planes)] for at in range(PLANE)]
    ring = PLANE // 2

    def shift_y(x, dy):
        pairs = []
        for r in range(groups):
            z, y, c = r // PLANE, r % PLANE // 2, r % 2
            pairs.append((z * PLANE + (y + dy) % ring * 2 + c, r))
        return lax.ppermute(x, "rows", pairs)

    def over_z(x):
        wide = x.shape[1]
        x = lax.all_to_all(
            x.reshape(planes, count // planes, wide),
            "rows",
            split_axis=0,
            concat_axis=0,
            axis_index_groups=columns,
            tiled=True,
        )
        return x.reshape(count, wide)

    x_part = lax.dynamic_slice_in_dim(normed_rows, lax.axis_index("tp") * part, part, 1)
    placed, token = place(sizes, meta, x_part, count)
    arrived = over_z(placed)

    token, meta, adapter_a, adapter_b, normed_rows = lax.optimization_barrier(
        (token, meta, adapter_a, adapter_b, normed_rows)
    )
    both = per_owner * rank
    choice = vmem_call(
        functools.partial(choose_kernel, PLANE, sizes), (count, both), f32, meta, token
    )
    un = vmem_call(functools.partial(unplace_kernel, PLANE, sizes), (rows, count), bf16, meta, token)
    packed = jnp.concatenate(
        [jnp.swapaxes(adapter_a, 0, 1).reshape(part, both)]
        + [adapter_b.reshape(both, width)[:, at : at + both] for at in range(0, width, both)],
        axis=0,
    )
    near = [packed] + [shift_y(packed, dy) for dy in range(1, ring)]
    packed, un, choice, queries = lax.optimization_barrier((packed, un, choice, queries))
    ctx, own = attend(queries, new_key, cache_keys, cache_values, kv_len.reshape(-1, 1))
    *near, ctx, own = lax.optimization_barrier((*near, ctx, own))
    near = jnp.stack(near)
    far = lax.ppermute(near, "rows", [(r ^ 1, r) for r in range(groups)])
    base = jnp.dot(normed_rows, value_weight, preferred_element_type=f32)
    b_maps = jnp.concatenate([near[:, part:], far[:, part:]], axis=0)
    arrived, un, base, ctx, own, choice, near, far, b_maps = lax.optimization_barrier(
        (arrived, un, base, ctx, own, choice, near, far, b_maps)
    )

    partial = vmem_call(
        functools.partial(low_kernel, PLANE), (count // 2, both), f32, choice, arrived, near, far
    )
    others = [
        lax.ppermute(partial, "tp", [(j, (j + k) % tp) for j in range(tp)]) for k in range(1, tp)
    ]
    out = vmem_call(
        functools.partial(delta_kernel, PLANE),
        (count, width),
        bf16,
        choice,
        partial,
        *others,
        b_maps,
    )
    return finish(un, over_z(out), base, ctx, own)


def solution(mesh):
    return jax.shard_map(
        body,
        mesh=mesh,
        in_specs=(
            P("rows", None),
            P(None, "tp"),
            P("rows", "tp", None),
            P("rows", None, "tp"),
            P(),
            P(),
            P("rows", None),
            P("rows", None),
            P("rows", "tp"),
            P("rows", "tp"),
            P("rows", None, "tp"),
            P("rows", None, "tp"),
        ),
        out_specs=(P("rows", "tp"), P("rows", "tp")),
        check_vma=False,
    )
```

time: 108 us -> 97.8 us (0.906)
  waiting for transfers between devices: 30.7 us -> 18 us
  blocking collectives: 22.8 us -> 17.8 us
  starting transfers between devices: 16.8 us -> 19.9 us
  other arithmetic: 0.08 us -> 2.9 us
  Pallas kernels: 27.4 us -> 24.6 us
  local copies, waits for them, and re-layouts: 8.01 us -> 10.7 us
    all_to_all x1, waiting for transfers between devices: 25.1 us -> 9.29 us  [over_z(): lax.all_to_all(x.reshape(planes, count // planes, wide), 'rows', split_ax...]
    ppermute x0 -> x4, starting transfers between devices: none -> 7.02 us  [the longest x3 5.06 us: shift_y(): return lax.ppermute(x, 'rows', pairs)]
    all_to_all x1, blocking collectives: 22.8 us -> 17.8 us  [over_z(): lax.all_to_all(x.reshape(planes, count // planes, wide), 'rows', split_ax...]
    all_to_all x1, starting transfers between devices: 13.2 us -> 9.15 us  [over_z(): lax.all_to_all(x.reshape(planes, count // planes, wide), 'rows', split_ax...]
    ppermute x0 -> x4, waiting for transfers between devices: none -> 3.11 us  [the longest x1 2.19 us: body(): far = lax.ppermute(near, 'rows', [(r ^ 1, r) for r in range(groups)])]
    another operation x1, other arithmetic: 0.08 us -> 2.04 us  [body(): near = jnp.stack(near)]
    unnamed x38 -> x32, local copies, waits for them, and re-layouts: 7.21 us -> 8.91 us
    pallas_call x1, Pallas kernels: 17.8 us -> 16.4 us  [attend(): pl.pallas_call(functools.partial(attend_kernel, 1.0 / math.sqrt(HEAD)), o...]
  transfers between devices with their start and end apart: 4 -> 8, of which waited for: 4 -> 6; matrix products, arithmetic and copies ran while one was open for 2% -> 5% of each run, Pallas kernels for 17% -> 18%
where the time goes in v2:
time: 97.8 us; the launch traced here: 96.6 us
  Pallas kernels  24.6 us (25%)
  starting transfers between devices  19.9 us (20%)
  waiting for transfers between devices  18 us (18%)
  blocking collectives  17.8 us (18%)
  local copies, waits for them, and re-layouts  10.7 us (11%)
  other arithmetic  2.9 us (3%)
  matrix products  1.95 us (2%)
    all_to_all x1, blocking collectives, over_z(): lax.all_to_all(x.reshape(planes, count // planes, wide), 'rows', split_ax...  17.8 us
    pallas_call x1, Pallas kernels, attend(): pl.pallas_call(functools.partial(attend_kernel, 1.0 / math.sqrt(HEAD)), o...  16.4 us
    all_to_all x1, waiting for transfers between devices, over_z(): lax.all_to_all(x.reshape(planes, count // planes, wide), 'rows', split_ax...  9.29 us
    all_to_all x1, starting transfers between devices, over_z(): lax.all_to_all(x.reshape(planes, count // planes, wide), 'rows', split_ax...  9.15 us
    unnamed x32, local copies, waits for them, and re-layouts  8.91 us
    ppermute x3, waiting for transfers between devices, body(): lax.ppermute(partial, 'tp', [(j, (j + k) % tp) for j in range(tp)])  5.6 us
    ppermute x3, starting transfers between devices, shift_y(): return lax.ppermute(x, 'rows', pairs)  5.06 us
    ppermute x3, starting transfers between devices, body(): lax.ppermute(partial, 'tp', [(j, (j + k) % tp) for j in range(tp)])  3.68 us
  transfers between devices with their start and end apart: 8, of which 6 were waited for; matrix products, arithmetic and copies ran while one was open for 5% of the time, Pallas kernels for 18%

profile of v2, /device:TPU:1, one launch (start us, length us, event | category | flops | bytes accessed | tf_op | source)
XLA Modules:
  0.0 96.6 jit_solution(7269504705814809369)
XLA Ops:
  0.6 1.3 %constant_dynamic-slice_fusion.x_ref = bf16[256,2048]{1,0:T(8,128)(2,1)S(1)} fusion(bf16[256,8192]{1,0:T(8,128)(2,1)} %param.12, s32[]{:T(128)S(6)} %select_n.3), kind=kLoop, calls=%fused_computation.5 | loop fusion | bytes 2097156 | tf_op jit(solution)/shard_map/dynamic_slice | solution.py:380
  1.9 0.8 pad_add_fusion.meta_ref
  2.7 2.5 %shard_map.131 = (bf16[512,2048]{1,0:T(8,128)(2,1)}, s32[8,128]{1,0:T(8,128)S(1)}) custom-call(s32[66,128]{1,0:T(8,128)S(1)} %pad_add_fusion.meta_ref, bf16[256,2048]{1,0:T(8,128)(2,1)S(1)} %constant_dynamic-slice_fusion.x_ref), custom_call_target="tpu_custom_call" | custom-call | tf_op jit(solution)/shard_map/pallas_call | solution.py:91
  5.2 9.2 %all-to-all-start = ((bf16[8,64,2048]{2,1,0:T(8,128)(2,1)}), bf16[8,64,2048]{2,1,0:T(8,128)(2,1)}, u32[]{:S(2)}, u32[]{:S(2)}) async-start(bf16[8,64,2048]{2,1,0:T(8,128)(2,1)} %bitcast.1), calls=%async_computation | async-start | bytes 4194304 | tf_op jit(solution)/shard_map/all_to_all | solution.py:370
  14.4 0.0 copy-start.6
  14.4 0.0 copy-start.8
  14.4 0.0 copy-done.13
  14.4 0.0 copy-done.11
  14.4 0.3 copy.15
  14.7 0.0 copy-start.9
  14.8 1.4 %collective-permute-start.2 = (bf16[2304,128]{1,0:T(8,128)(2,1)S(1)}, bf16[2304,128]{1,0:T(8,128)(2,1)S(1)}, u32[]{:S(2)}, u32[]{:S(2)}) collective-permute-start(bf16[2304,128]{1,0:T(8,128)(2,1)S(1)} %pad_maximum_fusion.1), channel_id=1, source_target_pairs={{24,0},{28,4},{0,8},{4,12},{8,16},{12,20},{16,24},{20,28},{56,32},... | collective-permute-start | bytes 1769480 | tf_op jit(solution)/shard_map/ppermute | solution.py:366
  16.1 2.6 %collective-permute-start.1 = (bf16[2304,128]{1,0:T(8,128)(2,1)S(1)}, bf16[2304,128]{1,0:T(8,128)(2,1)}, u32[]{:S(2)}, u32[]{:S(2)}) collective-permute-start(bf16[2304,128]{1,0:T(8,128)(2,1)S(1)} %pad_maximum_fusion.1), channel_id=1, source_target_pairs={{16,0},{20,4},{24,8},{28,12},{0,16},{4,20},{8,24},{12,28},{48,32},... | collective-permute-start | bytes 1769480 | tf_op jit(solution)/shard_map/ppermute | solution.py:366
  18.8 1.1 %collective-permute-start = (bf16[2304,128]{1,0:T(8,128)(2,1)S(1)}, bf16[2304,128]{1,0:T(8,128)(2,1)}, u32[]{:S(2)}, u32[]{:S(2)}) collective-permute-start(bf16[2304,128]{1,0:T(8,128)(2,1)S(1)} %pad_maximum_fusion.1), channel_id=1, source_target_pairs={{8,0},{12,4},{16,8},{20,12},{24,16},{28,20},{0,24},{4,28},{40,32},... | collective-permute-start | bytes 1769480 | tf_op jit(solution)/shard_map/ppermute | solution.py:366
  19.8 0.5 shard_map.133.choice_ref
  20.3 0.3 shard_map.132.un_ref
  20.6 0.0 copy-done.14
  20.6 0.1 copy.16.len_ref
  20.8 0.0 copy-done.6
  20.8 0.0 copy-done.8
  20.8 0.0 copy-start
  20.8 2.2 %copy-done = bf16[256,32,256]{2,1,0:T(8,128)(2,1)S(1)} copy-done((bf16[256,32,256]{2,1,0:T(8,128)(2,1)S(1)}, bf16[256,32,256]{2,1,0:T(8,128)(2,1)}, u32[]{:S(2)}) %copy-start) | copy-done | bytes 4194328
  23.0 2.2 %copy-done.1 = bf16[256,32,256]{2,1,0:T(8,128)(2,1)S(1)} copy-done((bf16[256,32,256]{2,1,0:T(8,128)(2,1)S(1)}, bf16[256,32,256]{2,1,0:T(8,128)(2,1)}, u32[]{:S(2)}) %copy-start.1) | copy-done | bytes 4194328
  25.2 16.4 %shard_map.134 = (f32[256,2048]{1,0:T(8,128)S(1)}, f32[256,128]{1,0:T(8,128)S(1)}) custom-call(bf16[256,2048]{1,0:T(8,128)(2,1)S(1)} %copy-done.6, bf16[256,256]{1,0:T(8,128)(2,1)S(1)} %copy-done.8, bf16[256,32,256]{2,1,0:T(8,128)(2,1)S(1)} %copy-done, bf16[256,32,256]{2,1,0:T(8,128)(2,1)S(1)} %copy-done.1, s32[256,1]{1,0:T(8,128)S(1)} %copy.16.len_ref), custom_call_target="tpu_custom_call" | custom-call | tf_op jit(solution)/shard_map/pallas_call | solution.py:270
  41.6 0.0 copy-done.9
  41.6 0.0 copy-start.4
  41.6 1.4 %copy-done.4 = f32[256,2048]{1,0:T(8,128)} copy-done((f32[256,2048]{1,0:T(8,128)}, f32[256,2048]{1,0:T(8,128)S(1)}, u32[]{:S(2)}) %copy-start.4) | copy-done | bytes 2097176
  43.0 0.0 collective-permute-done.2
  43.0 0.9 collective-permute-done.1
  43.9 0.0 collective-permute-done
  43.9 2.0 %pad_maximum_fusion.near_ref = bf16[4,2304,128]{2,1,0:T(8,128)(2,1)S(1)} fusion(bf16[1,2304,128]{2,1,0:T(8,128)(2,1)} %bitcast.19, bf16[1,2304,128]{2,1,0:T(8,128)(2,1)} %bitcast.9, bf16[1,2304,128]{2,1,0:T(8,128)(2,1)} %bitcast.8, bf16[1,2304,128]{2,1,0:T(8,128)(2,1)} %bitcast.18), kind=kLoop, calls=%fused_computation | loop fusion | flops 3538944 | bytes 4718592 | tf_op jit(solution)/shard_map/stack | solution.py:401
  46.0 2.0 %collective-permute-start.3 = (bf16[4,2304,128]{2,1,0:T(8,128)(2,1)S(1)}, bf16[4,2304,128]{2,1,0:T(8,128)(2,1)S(1)}, u32[]{:S(2)}, u32[]{:S(2)}) collective-permute-start(bf16[4,2304,128]{2,1,0:T(8,128)(2,1)S(1)} %pad_maximum_fusion.near_ref), channel_id=1, source_target_pairs={{4,0},{0,4},{12,8},{8,12},{20,16},{16,20},{28,24},{24,28},{36,32},... | collective-permute-start | bytes 7077896 | tf_op jit(solution)/shard_map/ppermute | solution.py:402
  47.9 1.9 %fusion.1.base_ref = f32[256,256]{1,0:T(8,128)} fusion(bf16[256,8192]{1,0:T(8,128)(2,1)S(1)} %copy-done.12, bf16[8192,256]{1,0:T(8,128)(2,1)S(1)} %copy-done.15), kind=kOutput, calls=%fused_computation.7 | convolution fusion | flops 1073741824 | bytes 8650752 | tf_op jit(solution)/shard_map/dot_general | solution.py:403
  49.9 2.2 %collective-permute-done.3.far_ref = bf16[4,2304,128]{2,1,0:T(8,128)(2,1)S(1)} collective-permute-done((bf16[4,2304,128]{2,1,0:T(8,128)(2,1)S(1)}, bf16[4,2304,128]{2,1,0:T(8,128)(2,1)S(1)}, u32[]{:S(2)}, u32[]{:S(2)}) %collective-permute-start.3) | collective-permute-done | bytes 2359328 | tf_op jit(solution)/shard_map/ppermute | solution.py:402
  52.1 1.4 %copy-done.2 = bf16[4,2304,128]{2,1,0:T(8,128)(2,1)} copy-done((bf16[4,2304,128]{2,1,0:T(8,128)(2,1)}, bf16[4,2304,128]{2,1,0:T(8,128)(2,1)S(1)}, u32[]{:S(2)}) %copy-start.2) | copy-done | bytes 2359320
  53.6 9.3 %all-to-all-done = bf16[8,64,2048]{2,1,0:T(8,128)(2,1)} async-done(((bf16[8,64,2048]{2,1,0:T(8,128)(2,1)}), bf16[8,64,2048]{2,1,0:T(8,128)(2,1)}, u32[]{:S(2)}, u32[]{:S(2)}) %all-to-all-start) | async-done | bytes 2097184 | tf_op jit(solution)/shard_map/all_to_all | solution.py:370
  62.9 1.7 %copy-done.3 = bf16[4,2304,128]{2,1,0:T(8,128)(2,1)S(1)} copy-done((bf16[4,2304,128]{2,1,0:T(8,128)(2,1)S(1)}, bf16[4,2304,128]{2,1,0:T(8,128)(2,1)}, u32[]{:S(2)}) %copy-start.3) | copy-done | bytes 2359320
  64.6 2.4 %shard_map.135.p0 = f32[256,128]{1,0:T(8,128)S(1)} custom-call(f32[512,128]{1,0:T(8,128)S(1)} %shard_map.133.choice_ref, bf16[512,2048]{1,0:T(8,128)(2,1)} %bitcast.2.x_ref, bf16[4,2304,128]{2,1,0:T(8,128)(2,1)S(1)} %pad_maximum_fusion.near_ref, bf16[4,2304,128]{2,1,0:T(8,128)(2,1)S(1)} %copy-done.3), custom_call_target="tpu_custom_call" | custom-call | tf_op jit(solution)/shard_map/pallas_call | solution.py:203
  67.0 0.0 copy-start.5
  67.0 2.6 %collective-permute-start.6 = (f32[256,128]{1,0:T(8,128)S(1)}, f32[256,128]{1,0:T(8,128)S(1)}, u32[]{:S(2)}, u32[]{:S(2)}) collective-permute-start(f32[256,128]{1,0:T(8,128)S(1)} %shard_map.135.p0), channel_id=1, source_target_pairs={{0,3},{1,0},{2,1},{3,2},{4,7},{5,4},{6,5},{7,6},{8,11},{9,8},{10,9... | collective-permute-start | bytes 393224 | tf_op jit(solution)/shard_map/ppermute | solution.py:413
  69.6 0.5 collective-permute-start.5
  70.1 0.6 collective-permute-start.4
  70.7 2.2 %collective-permute-done.6.p3 = f32[256,128]{1,0:T(8,128)S(1)} collective-permute-done((f32[256,128]{1,0:T(8,128)S(1)}, f32[256,128]{1,0:T(8,128)S(1)}, u32[]{:S(2)}, u32[]{:S(2)}) %collective-permute-start.6) | collective-permute-done | bytes 131104 | tf_op jit(solution)/shard_map/ppermute | solution.py:413
  72.9 2.1 %collective-permute-done.5.p2 = f32[256,128]{1,0:T(8,128)S(1)} collective-permute-done((f32[256,128]{1,0:T(8,128)S(1)}, f32[256,128]{1,0:T(8,128)S(1)}, u32[]{:S(2)}, u32[]{:S(2)}) %collective-permute-start.5) | collective-permute-done | bytes 131104 | tf_op jit(solution)/shard_map/ppermute | solution.py:413
  75.0 1.3 %collective-permute-done.4.p1 = f32[256,128]{1,0:T(8,128)S(1)} collective-permute-done((f32[256,128]{1,0:T(8,128)S(1)}, f32[256,128]{1,0:T(8,128)S(1)}, u32[]{:S(2)}, u32[]{:S(2)}) %collective-permute-start.4) | collective-permute-done | bytes 131104 | tf_op jit(solution)/shard_map/ppermute | solution.py:413
  76.3 0.3 shard_map.136
  76.6 17.8 %all_to_all.10 = bf16[8,64,256]{2,1,0:T(8,128)(2,1)S(1)} all-to-all(bf16[8,64,256]{2,1,0:T(8,128)(2,1)S(1)} %bitcast.17), channel_id=1, replica_groups={{0,32,64,96,128,160,192,224},{4,36,68,100,132,164,196,228},{8,40,72,104..., dimensions={0} | all-to-all | bytes 524288 | tf_op jit(solution)/shard_map/all_to_all | solution.py:370
  94.4 0.0 copy-done.5
  94.4 2.2 %shard_map.137 = (bf16[256,256]{1,0:T(8,128)(2,1)}, bf16[256,2048]{1,0:T(8,128)(2,1)}) custom-call(bf16[256,512]{1,0:T(8,128)(2,1)S(1)} %shard_map.132.un_ref, bf16[512,256]{1,0:T(8,128)(2,1)S(1)} %bitcast.16, f32[256,256]{1,0:T(8,128)S(1)} %copy-done.7, f32[256,2048]{1,0:T(8,128)S(1)} %copy-done.5, f32[256,128]{1,0:T(8,128)S(1)} %get-tuple-element.55.own_ref), custom_call_target="tpu_custom_call" | custom-call | tf_op jit(solution)/shard_map/pallas_call | solution.py:313
  (19 shorter events, 0.2 us)
Async XLA Ops:
  5.2 9.2 %copy-start.13 = (bf16[2,64,256]{2,1,0:T(8,128)(2,1)S(1)}, bf16[2,64,256]{2,1,0:T(8,128)(2,1)}, u32[]{:S(2)}) copy-start(bf16[2,64,256]{2,1,0:T(8,128)(2,1)} %param.15) | copy-start | bytes 196612
  5.2 9.2 %copy-start.11 = (bf16[2,2048,64]{1,2,0:T(8,128)(2,1)S(1)}, bf16[2,2048,64]{1,2,0:T(8,128)(2,1)}, u32[]{:S(2)}) copy-start(bf16[2,2048,64]{1,2,0:T(8,128)(2,1)} %param.14) | copy-start | bytes 1572868
  5.2 57.7 %all-to-all-start = ((bf16[8,64,2048]{2,1,0:T(8,128)(2,1)}), bf16[8,64,2048]{2,1,0:T(8,128)(2,1)}, u32[]{:S(2)}, u32[]{:S(2)}) async-start(bf16[8,64,2048]{2,1,0:T(8,128)(2,1)} %bitcast.1), calls=%async_computation | async-start | bytes 4194304 | tf_op jit(solution)/shard_map/all_to_all | solution.py:370
  14.4 6.3 %copy-start.14 = (s32[1,256]{1,0:T(1,128)S(1)}, s32[1,256]{1,0:T(1,128)}, u32[]{:S(2)}) copy-start(s32[1,256]{1,0:T(1,128)} %param.19) | copy-start | bytes 3076
  14.4 6.4 %copy-start.6 = (bf16[256,2048]{1,0:T(8,128)(2,1)S(1)}, bf16[256,2048]{1,0:T(8,128)(2,1)}, u32[]{:S(2)}) copy-start(bf16[256,2048]{1,0:T(8,128)(2,1)} %q_ref) | copy-start | bytes 3145732
  14.4 6.4 %copy-start.8 = (bf16[256,256]{1,0:T(8,128)(2,1)S(1)}, bf16[256,256]{1,0:T(8,128)(2,1)}, u32[]{:S(2)}) copy-start(bf16[256,256]{1,0:T(8,128)(2,1)} %nk_ref.1) | copy-start | bytes 393220
  14.7 26.8 %copy-start.9 = (bf16[2304,128]{1,0:T(8,128)(2,1)}, bf16[2304,128]{1,0:T(8,128)(2,1)S(1)}, u32[]{:S(2)}) copy-start(bf16[2304,128]{1,0:T(8,128)(2,1)S(1)} %pad_maximum_fusion.1) | copy-start | bytes 1769476
  14.8 28.2 %collective-permute-start.2 = (bf16[2304,128]{1,0:T(8,128)(2,1)S(1)}, bf16[2304,128]{1,0:T(8,128)(2,1)S(1)}, u32[]{:S(2)}, u32[]{:S(2)}) collective-permute-start(bf16[2304,128]{1,0:T(8,128)(2,1)S(1)} %pad_maximum_fusion.1), channel_id=1, source_target_pairs={{24,0},{28,4},{0,8},{4,12},{8,16},{12,20},{16,24},{20,28},{56,32},... | collective-permute-start | bytes 1769480 | tf_op jit(solution)/shard_map/ppermute | solution.py:366
  16.1 27.8 %collective-permute-start.1 = (bf16[2304,128]{1,0:T(8,128)(2,1)S(1)}, bf16[2304,128]{1,0:T(8,128)(2,1)}, u32[]{:S(2)}, u32[]{:S(2)}) collective-permute-start(bf16[2304,128]{1,0:T(8,128)(2,1)S(1)} %pad_maximum_fusion.1), channel_id=1, source_target_pairs={{16,0},{20,4},{24,8},{28,12},{0,16},{4,20},{8,24},{12,28},{48,32},... | collective-permute-start | bytes 1769480 | tf_op jit(solution)/shard_map/ppermute | solution.py:366
  18.8 25.2 %collective-permute-start = (bf16[2304,128]{1,0:T(8,128)(2,1)S(1)}, bf16[2304,128]{1,0:T(8,128)(2,1)}, u32[]{:S(2)}, u32[]{:S(2)}) collective-permute-start(bf16[2304,128]{1,0:T(8,128)(2,1)S(1)} %pad_maximum_fusion.1), channel_id=1, source_target_pairs={{8,0},{12,4},{16,8},{20,12},{24,16},{28,20},{0,24},{4,28},{40,32},... | collective-permute-start | bytes 1769480 | tf_op jit(solution)/shard_map/ppermute | solution.py:366
  20.8 2.2 %copy-start = (bf16[256,32,256]{2,1,0:T(8,128)(2,1)S(1)}, bf16[256,32,256]{2,1,0:T(8,128)(2,1)}, u32[]{:S(2)}) copy-start(bf16[256,32,256]{2,1,0:T(8,128)(2,1)} %k_ref.1) | copy-start | bytes 12582916
  23.0 2.2 %copy-start.1 = (bf16[256,32,256]{2,1,0:T(8,128)(2,1)S(1)}, bf16[256,32,256]{2,1,0:T(8,128)(2,1)}, u32[]{:S(2)}) copy-start(bf16[256,32,256]{2,1,0:T(8,128)(2,1)} %v_ref.1) | copy-start | bytes 12582916
  25.2 22.8 %copy-start.15 = (bf16[8192,256]{1,0:T(8,128)(2,1)S(1)}, bf16[8192,256]{1,0:T(8,128)(2,1)}, u32[]{:S(2)}) copy-start(bf16[8192,256]{1,0:T(8,128)(2,1)} %param.13) | copy-start | bytes 12582916
  41.6 1.4 %copy-start.4 = (f32[256,2048]{1,0:T(8,128)}, f32[256,2048]{1,0:T(8,128)S(1)}, u32[]{:S(2)}) copy-start(f32[256,2048]{1,0:T(8,128)S(1)} %get-tuple-element.54.ctx_ref) | copy-start | bytes 6291460
  43.0 0.9 copy-start.10
  43.9 4.0 %copy-start.12 = (bf16[256,8192]{1,0:T(8,128)(2,1)S(1)}, bf16[256,8192]{1,0:T(8,128)(2,1)}, u32[]{:S(2)}) copy-start(bf16[256,8192]{1,0:T(8,128)(2,1)} %param.12) | copy-start | bytes 12582916
  46.0 6.1 %collective-permute-start.3 = (bf16[4,2304,128]{2,1,0:T(8,128)(2,1)S(1)}, bf16[4,2304,128]{2,1,0:T(8,128)(2,1)S(1)}, u32[]{:S(2)}, u32[]{:S(2)}) collective-permute-start(bf16[4,2304,128]{2,1,0:T(8,128)(2,1)S(1)} %pad_maximum_fusion.near_ref), channel_id=1, source_target_pairs={{4,0},{0,4},{12,8},{8,12},{20,16},{16,20},{28,24},{24,28},{36,32},... | collective-permute-start | bytes 7077896 | tf_op jit(solution)/shard_map/ppermute | solution.py:402
  52.1 1.4 %copy-start.2 = (bf16[4,2304,128]{2,1,0:T(8,128)(2,1)}, bf16[4,2304,128]{2,1,0:T(8,128)(2,1)S(1)}, u32[]{:S(2)}) copy-start(bf16[4,2304,128]{2,1,0:T(8,128)(2,1)S(1)} %collective-permute-done.3.far_ref) | copy-start | bytes 7077892
  62.9 1.7 %copy-start.3 = (bf16[4,2304,128]{2,1,0:T(8,128)(2,1)S(1)}, bf16[4,2304,128]{2,1,0:T(8,128)(2,1)}, u32[]{:S(2)}) copy-start(bf16[4,2304,128]{2,1,0:T(8,128)(2,1)} %copy-done.2) | copy-start | bytes 7077892
  64.6 29.8 %copy-start.7 = (f32[256,256]{1,0:T(8,128)S(1)}, f32[256,256]{1,0:T(8,128)}, u32[]{:S(2)}) copy-start(f32[256,256]{1,0:T(8,128)} %fusion.1.base_ref) | copy-start | bytes 786436
  67.0 27.4 %copy-start.5 = (f32[256,2048]{1,0:T(8,128)S(1)}, f32[256,2048]{1,0:T(8,128)}, u32[]{:S(2)}) copy-start(f32[256,2048]{1,0:T(8,128)} %copy-done.4) | copy-start | bytes 6291460
  67.0 5.9 %collective-permute-start.6 = (f32[256,128]{1,0:T(8,128)S(1)}, f32[256,128]{1,0:T(8,128)S(1)}, u32[]{:S(2)}, u32[]{:S(2)}) collective-permute-start(f32[256,128]{1,0:T(8,128)S(1)} %shard_map.135.p0), channel_id=1, source_target_pairs={{0,3},{1,0},{2,1},{3,2},{4,7},{5,4},{6,5},{7,6},{8,11},{9,8},{10,9... | collective-permute-start | bytes 393224 | tf_op jit(solution)/shard_map/ppermute | solution.py:413
  69.6 5.4 %collective-permute-start.5 = (f32[256,128]{1,0:T(8,128)S(1)}, f32[256,128]{1,0:T(8,128)S(1)}, u32[]{:S(2)}, u32[]{:S(2)}) collective-permute-start(f32[256,128]{1,0:T(8,128)S(1)} %shard_map.135.p0), channel_id=1, source_target_pairs={{0,2},{1,3},{2,0},{3,1},{4,6},{5,7},{6,4},{7,5},{8,10},{9,11},{10,... | collective-permute-start | bytes 393224 | tf_op jit(solution)/shard_map/ppermute | solution.py:413
  70.1 6.2 %collective-permute-start.4 = (f32[256,128]{1,0:T(8,128)S(1)}, f32[256,128]{1,0:T(8,128)S(1)}, u32[]{:S(2)}, u32[]{:S(2)}) collective-permute-start(f32[256,128]{1,0:T(8,128)S(1)} %shard_map.135.p0), channel_id=1, source_target_pairs={{0,1},{1,2},{2,3},{3,0},{4,5},{5,6},{6,7},{7,4},{8,9},{9,10},{10,1... | collective-permute-start | bytes 393224 | tf_op jit(solution)/shard_map/ppermute | solution.py:413

commit v3 on v2

--- a/solution.py
+++ b/solution.py
@@ -51,22 +51,16 @@
         return self.ref[self.groups : self.groups + 1, : self.adapters]
 
 
-def column(plane):
-    rows = lax.axis_index("rows")
-    at = lax.rem(rows, plane)
-    return lax.div(rows, plane), lax.div(at, 2), lax.rem(at, 2)
-
-
-def owner_at(z, k, y, core, plane):
-    half = plane // 2
-    owner_y = lax.rem(lax.rem(k, half) + y, half)
-    owner_core = lax.rem(lax.div(k, half) + core, 2)
-    return z * plane + owner_y * 2 + owner_core
-
-
-def slot_owner(slot, y, core, plane):
-    k = lax.rem(jnp.right_shift(slot, 3), plane)
-    return owner_at(lax.div(slot, plane * MOST), k, y, core, plane)
+def ahead(q):
+    i = jnp.right_shift(q, 1)
+    odd = jnp.bitwise_and(q, 1) == 1
+    return jnp.where(odd, jnp.where(i == 0, 4, 8 - i), i)
+
+
+def slot_owner(slot, plane):
+    z = lax.div(lax.axis_index("rows"), plane)
+    q = jnp.bitwise_and(jnp.right_shift(slot, 3), 7)
+    return jnp.bitwise_and(z + ahead(q), 7) * plane + jnp.right_shift(slot, 6)
 
 
 def place_kernel(plane, sizes, meta_ref, x_ref, out_ref, token_ref):
@@ -74,9 +68,8 @@
     rows = x_ref.shape[0]
     token_ref[...] = jnp.zeros_like(token_ref)
     owner, start, lengths = segment_rows(Meta(meta_ref, *sizes))
-    _, y, core = column(plane)
     slot = iota((count, 1), 0)
-    mine = owner == slot_owner(slot, y, core, plane).astype(f32)
+    mine = owner == slot_owner(slot, plane).astype(f32)
     begin = jnp.sum(jnp.where(mine, start, 0.0), axis=1, keepdims=True)
     length = jnp.sum(jnp.where(mine, lengths, 0.0), axis=1, keepdims=True)
     within = jnp.bitwise_and(slot, MOST - 1).astype(f32)
@@ -103,76 +96,89 @@
 def unplace_kernel(plane, sizes, meta_ref, token_ref, out_ref):
     rows, count = out_ref.shape
     owner, start, lens = segment_rows(Meta(meta_ref, *sizes))
-    _, y, core = column(plane)
     row = iota((rows, 1), 0).astype(f32)
     inside = (row >= start) & (row < start + lens)
     target = jnp.sum(jnp.where(inside, owner * MOST + row - start, 0.0), axis=1, keepdims=True)
     slot = iota((1, count), 1)
-    meant = slot_owner(slot, y, core, plane) * MOST + jnp.bitwise_and(slot, MOST - 1)
+    meant = slot_owner(slot, plane) * MOST + jnp.bitwise_and(slot, MOST - 1)
     out_ref[...] = (meant.astype(f32) == target).astype(bf16)
 
 
 def choose_kernel(plane, sizes, meta_ref, token_ref, out_ref):
     meta = Meta(meta_ref, *sizes)
     count = out_ref.shape[0]
-    planes = meta.groups // plane
-    z, y, core = column(plane)
-    at = lax.rem(lax.axis_index("rows"), plane)
-    listed = jnp.concatenate(
-        [meta_ref[pl.ds(p * plane + at, 1), : meta.slots] for p in range(planes)], axis=0
-    )
+    rows = lax.axis_index("rows")
+    z, at = lax.div(rows, plane), lax.rem(rows, plane)
+    listed = meta_ref[pl.ds(pl.multiple_of(z * plane, plane), plane), : meta.slots]
     table = meta.table()
     ids = iota((1, meta.adapters), 1)
-    lane = iota((planes, 128), 1)
-    uses = jnp.zeros((planes, 128), f32)
-    for k in range(plane):
-        owner = owner_at(z, k, y, core, plane)
+    lane = iota((plane, 128), 1)
+    uses = jnp.zeros((plane, 128), f32)
+    for q in range(8):
+        step = (0, 4, 1, 7, 2, 6, 3, 5)[q]
+        owner = jnp.bitwise_and(z + step, 7) * plane + at
         second = jnp.max(jnp.where(table == 2 * owner + 1, ids, -1), axis=1, keepdims=True)
         hit = jnp.max((listed == second).astype(f32), axis=1, keepdims=True)
-        uses = jnp.where(lane == k, hit, uses)
+        uses = jnp.where(lane == q, hit, uses)
     row = iota((count, 1), 0)
     both = 2 * MOST
-    k_of = lax.div(row, both * planes) * 2 + jnp.bitwise_and(jnp.right_shift(row, 3), 1)
-    from_z = lax.rem(lax.div(row, both), planes)
-    spread = (from_z == iota((count, planes), 1)).astype(f32)
+    q_of = lax.div(row, both * plane) * 2 + jnp.bitwise_and(jnp.right_shift(row, 3), 1)
+    source = lax.rem(lax.div(row, both), plane)
+    spread = (source == iota((count, plane), 1)).astype(f32)
     wide = jnp.dot(spread, uses, preferred_element_type=f32)
-    mine = iota((count, 128), 1) == k_of
+    mine = iota((count, 128), 1) == q_of
     out_ref[...] = jnp.broadcast_to(
         jnp.sum(jnp.where(mine, wide, 0.0), axis=1, keepdims=True), out_ref.shape
     )
 
 
-def low_kernel(plane, choice_ref, x_ref, near_ref, far_ref, out_ref):
-    count, part = x_ref.shape
-    half, both = out_ref.shape
-    rank = both // 2
+def pair_rows(x_ref, pair):
     tile = 2 * MOST
-    stride = plane * MOST
-    pairs = []
-    for pair in range(plane // 2):
-        ref = near_ref if pair < plane // 4 else far_ref
-        first = pair % (plane // 4) * 2
-        a = jnp.concatenate([ref[first, :part], ref[first + 1, :part]], axis=1)
-        x = jnp.concatenate(
-            [x_ref[at : at + tile, :] for at in range(pair * tile, count, stride)], axis=0
-        )
-        each = jnp.dot(x, a, preferred_element_type=f32)
-        odd = jnp.bitwise_and(iota((each.shape[0], both), 0), MOST) > 0
-        pairs.append(jnp.where(odd, each[:, both:], each[:, :both]))
-    total = jnp.concatenate(pairs, axis=0)
-    second = choice_ref[...] > 0.5
-    turned = pltpu.roll(total, rank, 1)
-    left = jnp.where(second, turned, total)
-    right = jnp.where(second, total, turned)
-    out_ref[...] = jnp.where(iota((half, both), 1) < rank, left[:half], right[half:])
-
-
-def delta_kernel(plane, choice_ref, p0, p1, p2, p3, maps_ref, out_ref):
+    return jnp.concatenate(
+        [x_ref[at : at + tile, :] for at in range(pair * tile, x_ref.shape[0], 8 * MOST)], axis=0
+    )
+
+
+def turn(low, second):
+    turned = pltpu.roll(low, low.shape[1] // 2, 1)
+    return jnp.where(second, turned, low), jnp.where(second, low, turned)
+
+
+def early_kernel(choice_ref, x_ref, own_ref, d1, u1, d2, u2, d3, u3, out_ref, kept_ref):
+    part = x_ref.shape[1]
+    many, both = out_ref.shape[0] // 2, out_ref.shape[1]
+    odd = jnp.bitwise_and(iota((many, both), 0), MOST) > 0
+    second = [choice_ref[i * many : (i + 1) * many, :] > 0.5 for i in range(4)]
+    kept = pair_rows(x_ref, 0)
+    kept_ref[...] = kept
+    sides = [turn(jnp.dot(kept, own_ref[:part], preferred_element_type=f32), second[0])]
+    for i, (even_map, odd_map) in enumerate(((d1, u1), (d2, u2), (d3, u3))):
+        a = jnp.concatenate([even_map[:part], odd_map[:part]], axis=1)
+        each = jnp.dot(pair_rows(x_ref, i + 1), a, preferred_element_type=f32)
+        sides.append(turn(jnp.where(odd, each[:, both:], each[:, :both]), second[i + 1]))
+    left = iota((many, both), 1) < both // 2
+    out_ref[:many] = jnp.where(left, sides[0][0], sides[2][1])
+    out_ref[many:] = jnp.where(left, sides[1][0], sides[3][1])
+
+
+def final_kernel(choice_ref, kept_ref, a_ref, b_ref, early_ref, out_ref):
+    many, part = kept_ref.shape
+    both = out_ref.shape[1]
+    cut = a_ref.shape[0]
+    low = jnp.dot(kept_ref[:, :cut], a_ref[...], preferred_element_type=f32)
+    low = low + jnp.dot(kept_ref[:, cut:], b_ref[: part - cut], preferred_element_type=f32)
+    low = turn(low, choice_ref[:many, :] > 0.5)[0]
+    odd = jnp.bitwise_and(iota((many, both), 0), MOST) > 0
+    mine = odd & (iota((many, both), 1) < both // 2)
+    out_ref[:many] = jnp.where(mine, low, early_ref[:many])
+    out_ref[many:] = early_ref[many:]
+
+
+def delta_kernel(choice_ref, p0, p1, p2, p3, own, last, d1, u1, d2, u2, d3, u3, out_ref):
     count, width = out_ref.shape
     half, both = p0.shape
     rank = both // 2
     tile = 2 * MOST
-    stride = plane * MOST
     low = (p0[...] + p1[...]) + (p2[...] + p3[...])
     turned = pltpu.roll(low, rank, 1)
     lane = iota((half, both), 1) < rank
@@ -183,34 +189,80 @@
     spread = jnp.concatenate(
         [jnp.where(odd, 0.0, low), jnp.where(odd, low, 0.0)], axis=1
     ).astype(bf16)
-    many = count // (plane // 2)
-    for pair in range(plane // 2):
-        wide = [
-            jnp.concatenate([maps_ref[k, at : at + both] for at in range(0, width, both)], axis=1)
-            for k in (2 * pair, 2 * pair + 1)
-        ]
+    many = count // 4
+    for pair, refs in enumerate(((own, last), (d1, u1), (d2, u2), (d3, u3))):
+        wide = []
+        for ref in refs:
+            first = ref.shape[0] - width
+            wide.append(
+                jnp.concatenate(
+                    [ref[first + at : first + at + both] for at in range(0, width, both)], axis=1
+                )
+            )
         got = jnp.dot(
             spread[pair * many : (pair + 1) * many],
             jnp.concatenate(wide, axis=0),
             preferred_element_type=f32,
         ).astype(bf16)
         for i in range(many // tile):
-            at = i * stride + pair * tile
+            at = i * 8 * MOST + pair * tile
             out_ref[at : at + tile, :] = got[i * tile : (i + 1) * tile]
 
 
-def vmem_call(kernel, shape, dtype, *args):
+def vmem_spec():
+    return pl.BlockSpec(memory_space=pltpu.VMEM)
+
+
+def halves_kernel(a_ref, b_ref, a_out, b_out):
+    a_out[...] = a_ref[...]
+    b_out[...] = b_ref[...]
+
+
+def halves(a, b):
+    shape = (a.shape[0] // 2, a.shape[1])
+    return pl.pallas_call(
+        halves_kernel,
+        out_shape=(jax.ShapeDtypeStruct(shape, a.dtype),) * 2,
+        grid=(1,),
+        in_specs=[pl.BlockSpec(shape, lambda i: (0, 0)), pl.BlockSpec(shape, lambda i: (1, 0))],
+        out_specs=(pl.BlockSpec(shape, lambda i: (0, 0)),) * 2,
+        cost_estimate=FREE,
+        compiler_params=params(),
+    )(a, b)
+
+
+def delta_call(choice, parts, maps, count, width):
+    def whole(a):
+        return pl.BlockSpec(a.shape, lambda i: (0, 0))
+
+    def tail(a):
+        last = a.shape[0] // width - 1
+        return pl.BlockSpec((width, a.shape[1]), lambda i: (last, 0))
+
+    return pl.pallas_call(
+        delta_kernel,
+        out_shape=jax.ShapeDtypeStruct((count, width), bf16),
+        grid=(1,),
+        in_specs=[whole(a) for a in (choice, *parts)]
+        + [tail(a) if a.shape[0] % width == 0 else whole(a) for a in maps],
+        out_specs=pl.BlockSpec((count, width), lambda i: (0, 0)),
+        compiler_params=params(),
+    )(choice, *parts, *maps)
+
+
+def vmem_call(kernel, outs, *args):
     return pl.pallas_call(
         kernel,
-        out_shape=jax.ShapeDtypeStruct(shape, dtype),
-        in_specs=[pl.BlockSpec(memory_space=pltpu.VMEM)] * len(args),
-        out_specs=pl.BlockSpec(memory_space=pltpu.VMEM),
+        out_shape=tuple(jax.ShapeDtypeStruct(shape, dtype) for shape, dtype in outs),
+        in_specs=[vmem_spec()] * len(args),
+        out_specs=(vmem_spec(),) * len(outs),
         cost_estimate=FREE,
         compiler_params=params(),
     )(*args)
 
 
-def attend_kernel(scale, q_ref, nk_ref, k_ref, v_ref, len_ref, ctx_ref, own_ref):
+def attend_kernel(scale, q_ref, nk_ref, k_ref, v_ref, len_ref, *refs):
+    ctx_ref, own_ref = refs[-2:]
     rows, cache, width = k_ref.shape
     kv_heads = width // HEAD
     group = q_ref.shape[1] // width
@@ -263,7 +315,7 @@
             own_ref[pl.ds(base, 8), :] = own_tile
 
 
-def attend(queries, new_key, cache_keys, cache_values, lengths):
+def attend(first, steps, queries, new_key, cache_keys, cache_values, lengths, before=()):
     rows, wide = queries.shape
     cache, width = cache_keys.shape[1:]
     step = 32
@@ -273,21 +325,23 @@
             jax.ShapeDtypeStruct((rows, wide), f32),
             jax.ShapeDtypeStruct((rows, 128), f32),
         ),
-        grid=(rows // step,),
+        grid=(steps,),
         in_specs=[
-            pl.BlockSpec((step, wide), lambda i: (i, 0)),
-            pl.BlockSpec((step, width), lambda i: (i, 0)),
-            pl.BlockSpec((step, cache, width), lambda i: (i, 0, 0)),
-            pl.BlockSpec((step, cache, width), lambda i: (i, 0, 0)),
-            pl.BlockSpec((step, 1), lambda i: (i, 0)),
-        ],
+            pl.BlockSpec((step, wide), lambda i: (i + first, 0)),
+            pl.BlockSpec((step, width), lambda i: (i + first, 0)),
+            pl.BlockSpec((step, cache, width), lambda i: (i + first, 0, 0)),
+            pl.BlockSpec((step, cache, width), lambda i: (i + first, 0, 0)),
+            pl.BlockSpec((step, 1), lambda i: (i + first, 0)),
+        ]
+        + [pl.BlockSpec(memory_space=pl.ANY)] * len(before),
         out_specs=(
-            pl.BlockSpec((step, wide), lambda i: (i, 0)),
-            pl.BlockSpec((step, 128), lambda i: (i, 0)),
+            pl.BlockSpec((step, wide), lambda i: (i + first, 0)),
+            pl.BlockSpec((step, 128), lambda i: (i + first, 0)),
         ),
+        input_output_aliases={5 + i: i for i in range(len(before))},
         cost_estimate=FREE,
-        compiler_params=params(),
-    )(queries, new_key, cache_keys, cache_values, lengths)
+        compiler_params=params(60),
+    )(queries, new_key, cache_keys, cache_values, lengths, *before)
 
 
 def finish_kernel(un_ref, delta_ref, base_ref, ctx_ref, own_ref, value_ref, out_ref):
@@ -355,73 +409,81 @@
     sizes = (groups, slots, adapters)
     wide = lambda x: jnp.pad(x, ((0, 0), (0, 128 - x.shape[1])))
     meta = jnp.concatenate([wide(group_list), wide(page_table.reshape(1, -1)), wide(seg_len)], axis=0)
-    columns = [[z * PLANE + at for z in range(planes)] for at in range(PLANE)]
-    ring = PLANE // 2
-
-    def shift_y(x, dy):
-        pairs = []
-        for r in range(groups):
-            z, y, c = r // PLANE, r % PLANE // 2, r % 2
-            pairs.append((z * PLANE + (y + dy) % ring * 2 + c, r))
-        return lax.ppermute(x, "rows", pairs)
-
-    def over_z(x):
-        wide = x.shape[1]
+    planes_of = [[z * PLANE + at for at in range(PLANE)] for z in range(planes)]
+    both = per_owner * rank
+    lengths = kv_len.reshape(-1, 1)
+
+    def shift_z(x, by):
+        return lax.ppermute(
+            x, "rows", [(r, (r + by * PLANE) % groups) for r in range(groups)]
+        )
+
+    def over_plane(x):
+        size, wide = x.shape
         x = lax.all_to_all(
-            x.reshape(planes, count // planes, wide),
+            x.reshape(PLANE, size // PLANE, wide),
             "rows",
             split_axis=0,
             concat_axis=0,
-            axis_index_groups=columns,
+            axis_index_groups=planes_of,
             tiled=True,
         )
-        return x.reshape(count, wide)
-
-    x_part = lax.dynamic_slice_in_dim(normed_rows, lax.axis_index("tp") * part, part, 1)
-    placed, token = place(sizes, meta, x_part, count)
-    arrived = over_z(placed)
-
-    token, meta, adapter_a, adapter_b, normed_rows = lax.optimization_barrier(
-        (token, meta, adapter_a, adapter_b, normed_rows)
-    )
-    both = per_owner * rank
-    choice = vmem_call(
-        functools.partial(choose_kernel, PLANE, sizes), (count, both), f32, meta, token
-    )
-    un = vmem_call(functools.partial(unplace_kernel, PLANE, sizes), (rows, count), bf16, meta, token)
+        return x.reshape(size, wide)
+
     packed = jnp.concatenate(
         [jnp.swapaxes(adapter_a, 0, 1).reshape(part, both)]
         + [adapter_b.reshape(both, width)[:, at : at + both] for at in range(0, width, both)],
         axis=0,
     )
-    near = [packed] + [shift_y(packed, dy) for dy in range(1, ring)]
-    packed, un, choice, queries = lax.optimization_barrier((packed, un, choice, queries))
-    ctx, own = attend(queries, new_key, cache_keys, cache_values, kv_len.reshape(-1, 1))
-    *near, ctx, own = lax.optimization_barrier((*near, ctx, own))
-    near = jnp.stack(near)
-    far = lax.ppermute(near, "rows", [(r ^ 1, r) for r in range(groups)])
-    base = jnp.dot(normed_rows, value_weight, preferred_element_type=f32)
-    b_maps = jnp.concatenate([near[:, part:], far[:, part:]], axis=0)
-    arrived, un, base, ctx, own, choice, near, far, b_maps = lax.optimization_barrier(
-        (arrived, un, base, ctx, own, choice, near, far, b_maps)
-    )
-
-    partial = vmem_call(
-        functools.partial(low_kernel, PLANE), (count // 2, both), f32, choice, arrived, near, far
+    up, down = [shift_z(packed, 1)], [shift_z(packed, -1)]
+
+    packed, normed_rows, meta = lax.optimization_barrier((packed, normed_rows, meta))
+    x_part = lax.dynamic_slice_in_dim(normed_rows, lax.axis_index("tp") * part, part, 1)
+    placed, token = place(sizes, meta, x_part, count)
+    arrived = over_plane(placed)
+    (choice,) = vmem_call(
+        functools.partial(choose_kernel, PLANE, sizes), [((count, both), f32)], meta, token
+    )
+    up[0], choice, lengths = lax.optimization_barrier((up[0], choice, lengths))
+    up.append(shift_z(up[0], 1))
+    down[0], choice, lengths = lax.optimization_barrier((down[0], choice, lengths))
+    down.append(shift_z(down[0], -1))
+    up[0], down[0], queries = lax.optimization_barrier((up[0], down[0], queries))
+    steps = rows // 64
+    done = attend(0, steps, queries, new_key, cache_keys, cache_values, lengths)
+    up[1], done = lax.optimization_barrier((up[1], done))
+    up.append(shift_z(up[1], 1))
+    down[1], done = lax.optimization_barrier((down[1], done))
+    down.append(shift_z(down[1], -1))
+    up[1], down[1], queries = lax.optimization_barrier((up[1], down[1], queries))
+    ctx, own = attend(steps, steps, queries, new_key, cache_keys, cache_values, lengths, done)
+    up[2], down[2], ctx, own, meta = lax.optimization_barrier((up[2], down[2], ctx, own, meta))
+    half_up, half_down = halves(up[2], down[2])
+    last_a, last_b = shift_z(half_up, 1), shift_z(half_down, -1)
+    (un,) = vmem_call(
+        functools.partial(unplace_kernel, PLANE, sizes), [((rows, count), bf16)], meta, token
+    )
+    maps = [m for pair in zip(down, up) for m in pair]
+    early, kept = vmem_call(
+        early_kernel,
+        [((count // 2, both), f32), ((count // 4, part), bf16)],
+        choice,
+        arrived,
+        packed,
+        *maps,
+    )
+    last_a, last_b, early, kept, un = lax.optimization_barrier((last_a, last_b, early, kept, un))
+    (partial,) = vmem_call(
+        final_kernel, [((count // 2, both), f32)], choice, kept, last_a, last_b, early
     )
     others = [
         lax.ppermute(partial, "tp", [(j, (j + k) % tp) for j in range(tp)]) for k in range(1, tp)
     ]
-    out = vmem_call(
-        functools.partial(delta_kernel, PLANE),
-        (count, width),
-        bf16,
-        choice,
-        partial,
-        *others,
-        b_maps,
-    )
-    return finish(un, over_z(out), base, ctx, own)
+    partial, normed_rows = lax.optimization_barrier((partial, normed_rows))
+    base = jnp.dot(normed_rows, value_weight, preferred_element_type=f32)
+    *others, base = lax.optimization_barrier((*others, base))
+    out = delta_call(choice, [partial, *others], [packed, last_b, *maps], count, width)
+    return finish(un, over_plane(out), base, ctx, own)
 
 
 def solution(mesh):

time: 97.8 us -> 95.6 us (0.978)
  waiting for transfers between devices: 18 us -> 9.61 us
  Pallas kernels: 24.6 us -> 31.6 us
  starting transfers between devices: 19.9 us -> 23.1 us
  local copies, waits for them, and re-layouts: 10.7 us -> 8.15 us
  other arithmetic: 2.9 us -> 0.81 us
  matrix products: 1.95 us -> 3.5 us
    all_to_all x1, waiting for transfers between devices: 9.29 us -> 0.01 us  [over_plane(): lax.all_to_all(x.reshape(PLANE, size // PLANE, wide), 'rows', split_axis=...]
    ppermute x4 -> x8, starting transfers between devices: 7.02 us -> 14 us  [shift_z(): lax.ppermute(x, 'rows', [(r, (r + by * PLANE) % groups) for r in range(gr...]
    unnamed x32 -> x26, local copies, waits for them, and re-layouts: 8.91 us -> 3.95 us
    ppermute x4 -> x8, waiting for transfers between devices: 3.11 us -> 7.55 us  [shift_z(): lax.ppermute(x, 'rows', [(r, (r + by * PLANE) % groups) for r in range(gr...]
    pallas_call x4 -> x6, Pallas kernels: 3.51 us -> 7.89 us  [the longest x4 4.76 us: vmem_call(): pl.pallas_call(kernel, out_shape=tuple((jax.ShapeDtypeStruct(shape, dtype...]
    pallas_call x1 -> x2, Pallas kernels: 16.4 us -> 20.5 us  [attend(): pl.pallas_call(functools.partial(attend_kernel, 1.0 / math.sqrt(HEAD)), o...]
    all_to_all x1, starting transfers between devices: 9.15 us -> 5.42 us  [over_plane(): lax.all_to_all(x.reshape(PLANE, size // PLANE, wide), 'rows', split_axis=...]
    ppermute x3, waiting for transfers between devices: 5.6 us -> 2.05 us  [body(): lax.ppermute(partial, 'tp', [(j, (j + k) % tp) for j in range(tp)])]
  transfers between devices with their start and end apart: 8 -> 12, of which waited for: 6 -> 5; matrix products, arithmetic and copies ran while one was open for 5% -> 7% of each run, Pallas kernels for 18% -> 28%
where the time goes in v3:
time: 95.6 us; the launch traced here: 94.9 us
  Pallas kernels  31.6 us (33%)
  starting transfers between devices  23.1 us (24%)
  blocking collectives  17.3 us (18%)
  waiting for transfers between devices  9.61 us (10%)
  local copies, waits for them, and re-layouts  8.15 us (9%)
  matrix products  3.5 us (4%)
    pallas_call x2, Pallas kernels, attend(): pl.pallas_call(functools.partial(attend_kernel, 1.0 / math.sqrt(HEAD)), o...  20.5 us
    all_to_all x1, blocking collectives, over_plane(): lax.all_to_all(x.reshape(PLANE, size // PLANE, wide), 'rows', split_axis=...  17.3 us
    ppermute x8, starting transfers between devices, shift_z(): lax.ppermute(x, 'rows', [(r, (r + by * PLANE) % groups) for r in range(gr...  14 us
    ppermute x8, waiting for transfers between devices, shift_z(): lax.ppermute(x, 'rows', [(r, (r + by * PLANE) % groups) for r in range(gr...  7.55 us
    all_to_all x1, starting transfers between devices, over_plane(): lax.all_to_all(x.reshape(PLANE, size // PLANE, wide), 'rows', split_axis=...  5.42 us
    pallas_call x4, Pallas kernels, vmem_call(): pl.pallas_call(kernel, out_shape=tuple((jax.ShapeDtypeStruct(shape, dtype...  4.76 us
    unnamed x26, local copies, waits for them, and re-layouts  3.95 us
    ppermute x3, starting transfers between devices, body(): lax.ppermute(partial, 'tp', [(j, (j + k) % tp) for j in range(tp)])  3.68 us
  transfers between devices with their start and end apart: 12, of which 5 were waited for; matrix products, arithmetic and copies ran while one was open for 7% of the time, Pallas kernels for 28%

profile of v3, /device:TPU:1, one launch (start us, length us, event | category | flops | bytes accessed | tf_op | source)
XLA Modules:
  0.0 94.9 jit_solution(14718847412689035480)
XLA Ops:
  0.6 0.8 fusion
  1.4 1.3 %copy.17 = bf16[2048,128]{1,0:T(8,128)(2,1)S(1)} copy(bf16[2048,128]{0,1:T(8,128)(2,1)} %bitcast.16) | data formatting | bytes 1048576 | tf_op jit(solution)/shard_map/reshape | solution.py:434
  2.7 0.0 copy-start.12
  2.8 6.5 %collective-permute-start.2 = (bf16[2304,128]{1,0:T(8,128)(2,1)S(1)}, bf16[2304,128]{1,0:T(8,128)(2,1)S(1)}, u32[]{:S(2)}, u32[]{:S(2)}) collective-permute-start(bf16[2304,128]{1,0:T(8,128)(2,1)S(1)} %pad_maximum_fusion.own_ref.own), channel_id=1, source_target_pairs={{0,224},{4,228},{8,232},{12,236},{16,240},{20,244},{24,248},{28,25... | collective-permute-start | bytes 1769480 | tf_op jit(solution)/shard_map/ppermute | solution.py:417
  9.3 0.0 collective-permute-start
  9.3 0.8 pad_add_fusion.meta_ref
  10.0 1.3 %constant_dynamic-slice_fusion.x_ref = bf16[256,2048]{1,0:T(8,128)(2,1)S(1)} fusion(bf16[256,8192]{1,0:T(8,128)(2,1)} %param.12, s32[]{:T(128)S(6)} %select_n.3), kind=kLoop, calls=%fused_computation.3 | loop fusion | bytes 2097156 | tf_op jit(solution)/shard_map/dynamic_slice | solution.py:441
  11.4 1.0 %shard_map.131 = (bf16[512,2048]{1,0:T(8,128)(2,1)S(1)}, s32[8,128]{1,0:T(8,128)S(1)}) custom-call(s32[66,128]{1,0:T(8,128)S(1)} %pad_add_fusion.meta_ref, bf16[256,2048]{1,0:T(8,128)(2,1)S(1)} %constant_dynamic-slice_fusion.x_ref), custom_call_target="tpu_custom_call" | custom-call | tf_op jit(solution)/shard_map/pallas_call | solution.py:84
  12.3 1.3 %copy-done.4 = bf16[512,2048]{1,0:T(8,128)(2,1)} copy-done((bf16[512,2048]{1,0:T(8,128)(2,1)}, bf16[512,2048]{1,0:T(8,128)(2,1)S(1)}, u32[]{:S(2)}) %copy-start.4) | copy-done | bytes 2097176
  13.7 5.4 %all-to-all-start = ((bf16[8,64,2048]{2,1,0:T(8,128)(2,1)}), bf16[8,64,2048]{2,1,0:T(8,128)(2,1)S(1)}, u32[]{:S(2)}, u32[]{:S(2)}) async-start(bf16[8,64,2048]{2,1,0:T(8,128)(2,1)} %bitcast.13), calls=%async_computation | async-start | bytes 4194304 | tf_op jit(solution)/shard_map/all_to_all | solution.py:423
  19.1 0.8 copy-done.8
  19.9 0.5 shard_map.132.choice_ref
  20.4 4.1 %collective-permute-done.u1 = bf16[2304,128]{1,0:T(8,128)(2,1)} collective-permute-done((bf16[2304,128]{1,0:T(8,128)(2,1)S(1)}, bf16[2304,128]{1,0:T(8,128)(2,1)}, u32[]{:S(2)}, u32[]{:S(2)}) %collective-permute-start) | collective-permute-done | bytes 589856 | tf_op jit(solution)/shard_map/ppermute | solution.py:417
  24.5 0.0 collective-permute-start.1
  24.5 0.0 collective-permute-done.2.d1
  24.5 2.7 %collective-permute-start.4 = (bf16[2304,128]{1,0:T(8,128)(2,1)S(1)}, bf16[2304,128]{1,0:T(8,128)(2,1)}, u32[]{:S(2)}, u32[]{:S(2)}) collective-permute-start(bf16[2304,128]{1,0:T(8,128)(2,1)S(1)} %collective-permute-done.2.d1), channel_id=1, source_target_pairs={{0,224},{4,228},{8,232},{12,236},{16,240},{20,244},{24,248},{28,25... | collective-permute-start | bytes 1769480 | tf_op jit(solution)/shard_map/ppermute | solution.py:417
  27.1 0.8 copy.18.len_ref
  28.0 10.3 %shard_map.133 = (f32[256,2048]{1,0:T(8,128)}, f32[256,128]{1,0:T(8,128)}) custom-call(bf16[256,2048]{1,0:T(8,128)(2,1)} %q_ref.1, bf16[256,256]{1,0:T(8,128)(2,1)} %nk_ref.3, bf16[256,32,256]{2,1,0:T(8,128)(2,1)} %k_ref.3, bf16[256,32,256]{2,1,0:T(8,128)(2,1)} %v_ref.3, s32[256,1]{1,0:T(8,128)} %copy.18.len_ref), custom_call_target="tpu_custom_call" | custom-call | tf_op jit(solution)/shard_map/pallas_call | solution.py:322
  38.2 0.0 copy-done.1
  38.2 0.7 collective-permute-done.1.u2
  39.0 0.0 collective-permute-done.4.d2
  39.0 2.2 %collective-permute-start.5 = (bf16[2304,128]{1,0:T(8,128)(2,1)}, bf16[2304,128]{1,0:T(8,128)(2,1)S(1)}, u32[]{:S(2)}, u32[]{:S(2)}) collective-permute-start(bf16[2304,128]{1,0:T(8,128)(2,1)} %collective-permute-done.4.d2), channel_id=1, source_target_pairs={{0,224},{4,228},{8,232},{12,236},{16,240},{20,244},{24,248},{28,25... | collective-permute-start | bytes 1769480 | tf_op jit(solution)/shard_map/ppermute | solution.py:417
  41.1 0.0 collective-permute-start.3
  41.1 10.3 %shard_map.134 = (f32[256,2048]{1,0:T(8,128)}, f32[256,128]{1,0:T(8,128)}) custom-call(bf16[256,2048]{1,0:T(8,128)(2,1)} %q_ref.1, bf16[256,256]{1,0:T(8,128)(2,1)} %nk_ref.3, bf16[256,32,256]{2,1,0:T(8,128)(2,1)} %k_ref.3, bf16[256,32,256]{2,1,0:T(8,128)(2,1)} %v_ref.3, s32[256,1]{1,0:T(8,128)} %copy.18.len_ref, ...), custom_call_target="tpu_custom_call", output_to_operand_aliasing={{0}: (5, {}), {1}: (6, {})} | custom-call | tf_op jit(solution)/shard_map/pallas_call | solution.py:322
  51.4 0.0 collective-permute-done.5.b_ref.d3
  51.4 2.7 %collective-permute-done.3.a_ref.u3 = bf16[2304,128]{1,0:T(8,128)(2,1)} collective-permute-done((bf16[2304,128]{1,0:T(8,128)(2,1)}, bf16[2304,128]{1,0:T(8,128)(2,1)}, u32[]{:S(2)}, u32[]{:S(2)}) %collective-permute-start.3) | collective-permute-done | bytes 589856 | tf_op jit(solution)/shard_map/ppermute | solution.py:417
  54.1 1.8 %shard_map.135 = (bf16[1152,128]{1,0:T(8,128)(2,1)}, bf16[1152,128]{1,0:T(8,128)(2,1)}) custom-call(bf16[2304,128]{1,0:T(8,128)(2,1)} %collective-permute-done.3.a_ref.u3, bf16[2304,128]{1,0:T(8,128)(2,1)S(1)} %collective-permute-done.5.b_ref.d3), custom_call_target="tpu_custom_call" | custom-call | tf_op jit(solution)/shard_map/pallas_call | solution.py:223
  55.9 0.0 collective-permute-start.6
  55.9 2.7 %collective-permute-start.7 = (bf16[1152,128]{1,0:T(8,128)(2,1)}, bf16[1152,128]{1,0:T(8,128)(2,1)}, u32[]{:S(2)}, u32[]{:S(2)}) collective-permute-start(bf16[1152,128]{1,0:T(8,128)(2,1)} %get-tuple-element.72), channel_id=1, source_target_pairs={{0,224},{4,228},{8,232},{12,236},{16,240},{20,244},{24,248},{28,25... | collective-permute-start | bytes 884744 | tf_op jit(solution)/shard_map/ppermute | solution.py:417
  58.6 0.3 shard_map.137.un_ref
  58.9 0.7 copy-done.5
  59.6 0.0 all-to-all-done
  59.6 1.1 %copy-done.2 = bf16[2304,128]{1,0:T(8,128)(2,1)S(1)} copy-done((bf16[2304,128]{1,0:T(8,128)(2,1)S(1)}, bf16[2304,128]{1,0:T(8,128)(2,1)}, u32[]{:S(2)}) %copy-start.2) | copy-done | bytes 589848
  60.7 2.6 %shard_map.136 = (f32[256,128]{1,0:T(8,128)S(1)}, bf16[128,2048]{1,0:T(8,128)(2,1)S(1)}) custom-call(f32[512,128]{1,0:T(8,128)S(1)} %shard_map.132.choice_ref, bf16[512,2048]{1,0:T(8,128)(2,1)S(1)} %bitcast.12, bf16[2304,128]{1,0:T(8,128)(2,1)S(1)} %pad_maximum_fusion.own_ref.own, bf16[2304,128]{1,0:T(8,128)(2,1)S(1)} %copy-done.2, ...), custom_call_target="tpu_custom_call" | custom-call | tf_op jit(solution)/shard_map/pallas_call | solution.py:254
  63.3 0.0 collective-permute-done.6.a_ref
  63.3 0.0 collective-permute-done.7.b_ref.last
  63.3 1.4 %shard_map.138.p0 = f32[256,128]{1,0:T(8,128)S(1)} custom-call(f32[512,128]{1,0:T(8,128)S(1)} %shard_map.132.choice_ref, bf16[128,2048]{1,0:T(8,128)(2,1)S(1)} %get-tuple-element.84.kept_ref, bf16[1152,128]{1,0:T(8,128)(2,1)} %collective-permute-done.6.a_ref, bf16[1152,128]{1,0:T(8,128)(2,1)} %collective-permute-done.7.b_ref.last, ...), custom_call_target="tpu_custom_call" | custom-call | tf_op jit(solution)/shard_map/pallas_call | solution.py:254
  64.7 0.0 copy-start.3
  64.7 2.6 %collective-permute-start.10 = (f32[256,128]{1,0:T(8,128)S(1)}, f32[256,128]{1,0:T(8,128)S(1)}, u32[]{:S(2)}, u32[]{:S(2)}) collective-permute-start(f32[256,128]{1,0:T(8,128)S(1)} %shard_map.138.p0), channel_id=1, source_target_pairs={{0,3},{1,0},{2,1},{3,2},{4,7},{5,4},{6,5},{7,6},{8,11},{9,8},{10,9... | collective-permute-start | bytes 393224 | tf_op jit(solution)/shard_map/ppermute | solution.py:480
  67.3 0.5 collective-permute-start.9
  67.8 0.6 collective-permute-start.8
  68.4 3.5 %fusion.1.base_ref = f32[256,256]{1,0:T(8,128)S(1)} fusion(bf16[256,8192]{1,0:T(8,128)(2,1)S(1)} %copy-done.11, bf16[8192,256]{1,0:T(8,128)(2,1)} %param.13), kind=kOutput, calls=%fused_computation.5 | convolution fusion | flops 1073741824 | bytes 8650752 | tf_op jit(solution)/shard_map/dot_general | solution.py:483
  72.0 0.0 collective-permute-done.10.p3
  72.0 0.7 collective-permute-done.9.p2
  72.7 1.3 %collective-permute-done.8.p1 = f32[256,128]{1,0:T(8,128)S(1)} collective-permute-done((f32[256,128]{1,0:T(8,128)S(1)}, f32[256,128]{1,0:T(8,128)S(1)}, u32[]{:S(2)}, u32[]{:S(2)}) %collective-permute-start.8) | collective-permute-done | bytes 131104 | tf_op jit(solution)/shard_map/ppermute | solution.py:480
  74.0 1.3 %shard_map.139 = bf16[512,256]{1,0:T(8,128)(2,1)S(1)} custom-call(f32[512,128]{1,0:T(8,128)S(1)} %shard_map.132.choice_ref, f32[256,128]{1,0:T(8,128)S(1)} %shard_map.138.p0, f32[256,128]{1,0:T(8,128)S(1)} %collective-permute-done.8.p1, f32[256,128]{1,0:T(8,128)S(1)} %collective-permute-done.9.p2, f32[256,128]{1,0:T(8,128)S(1)} %collective-permute-done.10.p3, ...), custom_call_target="tpu_custom_call" | custom-call | tf_op jit(solution)/shard_map/pallas_call | solution.py:242
  75.4 17.3 %all_to_all.10 = bf16[8,64,256]{2,1,0:T(8,128)(2,1)S(1)} all-to-all(bf16[8,64,256]{2,1,0:T(8,128)(2,1)S(1)} %bitcast.15), channel_id=1, replica_groups={{0,4,8,12,16,20,24,28},{32,36,40,44,48,52,56,60},{64,68,72,76,80,84,88,..., dimensions={0} | all-to-all | bytes 524288 | tf_op jit(solution)/shard_map/all_to_all | solution.py:423
  92.7 2.2 %shard_map.140 = (bf16[256,256]{1,0:T(8,128)(2,1)}, bf16[256,2048]{1,0:T(8,128)(2,1)}) custom-call(bf16[256,512]{1,0:T(8,128)(2,1)S(1)} %copy-done.6, bf16[512,256]{1,0:T(8,128)(2,1)S(1)} %bitcast.14, f32[256,256]{1,0:T(8,128)S(1)} %fusion.1.base_ref, f32[256,2048]{1,0:T(8,128)S(1)} %copy-done, f32[256,128]{1,0:T(8,128)S(1)} %copy-done.10), custom_call_target="tpu_custom_call" | custom-call | tf_op jit(solution)/shard_map/pallas_call | solution.py:367
  (20 shorter events, 0.1 us)
Async XLA Ops:
  2.7 24.4 %copy-start.12 = (s32[1,256]{1,0:T(1,128)S(1)}, s32[1,256]{1,0:T(1,128)}, u32[]{:S(2)}) copy-start(s32[1,256]{1,0:T(1,128)} %param.19) | copy-start | bytes 3076
  2.8 21.7 %collective-permute-start.2 = (bf16[2304,128]{1,0:T(8,128)(2,1)S(1)}, bf16[2304,128]{1,0:T(8,128)(2,1)S(1)}, u32[]{:S(2)}, u32[]{:S(2)}) collective-permute-start(bf16[2304,128]{1,0:T(8,128)(2,1)S(1)} %pad_maximum_fusion.own_ref.own), channel_id=1, source_target_pairs={{0,224},{4,228},{8,232},{12,236},{16,240},{20,244},{24,248},{28,25... | collective-permute-start | bytes 1769480 | tf_op jit(solution)/shard_map/ppermute | solution.py:417
  9.3 15.2 %collective-permute-start = (bf16[2304,128]{1,0:T(8,128)(2,1)S(1)}, bf16[2304,128]{1,0:T(8,128)(2,1)}, u32[]{:S(2)}, u32[]{:S(2)}) collective-permute-start(bf16[2304,128]{1,0:T(8,128)(2,1)S(1)} %pad_maximum_fusion.own_ref.own), channel_id=1, source_target_pairs={{0,32},{4,36},{8,40},{12,44},{16,48},{20,52},{24,56},{28,60},{32,6... | collective-permute-start | bytes 1769480 | tf_op jit(solution)/shard_map/ppermute | solution.py:417
  10.0 9.1 %copy-start.7 = (s32[66,128]{1,0:T(8,128)}, s32[66,128]{1,0:T(8,128)S(1)}, u32[]{:S(2)}) copy-start(s32[66,128]{1,0:T(8,128)S(1)} %pad_add_fusion.meta_ref) | copy-start | bytes 101380
  12.3 1.3 %copy-start.4 = (bf16[512,2048]{1,0:T(8,128)(2,1)}, bf16[512,2048]{1,0:T(8,128)(2,1)S(1)}, u32[]{:S(2)}) copy-start(bf16[512,2048]{1,0:T(8,128)(2,1)S(1)} %get-tuple-element.74) | copy-start | bytes 6291460
  13.7 46.0 %all-to-all-start = ((bf16[8,64,2048]{2,1,0:T(8,128)(2,1)}), bf16[8,64,2048]{2,1,0:T(8,128)(2,1)S(1)}, u32[]{:S(2)}, u32[]{:S(2)}) async-start(bf16[8,64,2048]{2,1,0:T(8,128)(2,1)} %bitcast.13), calls=%async_computation | async-start | bytes 4194304 | tf_op jit(solution)/shard_map/all_to_all | solution.py:423
  19.1 0.8 copy-start.8
  24.5 14.5 %collective-permute-start.1 = (bf16[2304,128]{1,0:T(8,128)(2,1)}, bf16[2304,128]{1,0:T(8,128)(2,1)}, u32[]{:S(2)}, u32[]{:S(2)}) collective-permute-start(bf16[2304,128]{1,0:T(8,128)(2,1)} %collective-permute-done.u1), channel_id=1, source_target_pairs={{0,32},{4,36},{8,40},{12,44},{16,48},{20,52},{24,56},{28,60},{32,6... | collective-permute-start | bytes 1769480 | tf_op jit(solution)/shard_map/ppermute | solution.py:417
  24.5 13.7 %copy-start.1 = (bf16[2304,128]{1,0:T(8,128)(2,1)}, bf16[2304,128]{1,0:T(8,128)(2,1)S(1)}, u32[]{:S(2)}) copy-start(bf16[2304,128]{1,0:T(8,128)(2,1)S(1)} %collective-permute-done.2.d1) | copy-start | bytes 1769476
  24.5 14.5 %collective-permute-start.4 = (bf16[2304,128]{1,0:T(8,128)(2,1)S(1)}, bf16[2304,128]{1,0:T(8,128)(2,1)}, u32[]{:S(2)}, u32[]{:S(2)}) collective-permute-start(bf16[2304,128]{1,0:T(8,128)(2,1)S(1)} %collective-permute-done.2.d1), channel_id=1, source_target_pairs={{0,224},{4,228},{8,232},{12,236},{16,240},{20,244},{24,248},{28,25... | collective-permute-start | bytes 1769480 | tf_op jit(solution)/shard_map/ppermute | solution.py:417
  38.9 19.7 %copy-start.9 = (s32[66,128]{1,0:T(8,128)S(1)}, s32[66,128]{1,0:T(8,128)}, u32[]{:S(2)}) copy-start(s32[66,128]{1,0:T(8,128)} %copy-done.7) | copy-start | bytes 101380
  39.0 12.5 %collective-permute-start.5 = (bf16[2304,128]{1,0:T(8,128)(2,1)}, bf16[2304,128]{1,0:T(8,128)(2,1)S(1)}, u32[]{:S(2)}, u32[]{:S(2)}) collective-permute-start(bf16[2304,128]{1,0:T(8,128)(2,1)} %collective-permute-done.4.d2), channel_id=1, source_target_pairs={{0,224},{4,228},{8,232},{12,236},{16,240},{20,244},{24,248},{28,25... | collective-permute-start | bytes 1769480 | tf_op jit(solution)/shard_map/ppermute | solution.py:417
  41.1 13.0 %collective-permute-start.3 = (bf16[2304,128]{1,0:T(8,128)(2,1)}, bf16[2304,128]{1,0:T(8,128)(2,1)}, u32[]{:S(2)}, u32[]{:S(2)}) collective-permute-start(bf16[2304,128]{1,0:T(8,128)(2,1)} %collective-permute-done.1.u2), channel_id=1, source_target_pairs={{0,32},{4,36},{8,40},{12,44},{16,48},{20,52},{24,56},{28,60},{32,6... | collective-permute-start | bytes 1769480 | tf_op jit(solution)/shard_map/ppermute | solution.py:417
  55.9 7.4 %collective-permute-start.6 = (bf16[1152,128]{1,0:T(8,128)(2,1)}, bf16[1152,128]{1,0:T(8,128)(2,1)}, u32[]{:S(2)}, u32[]{:S(2)}) collective-permute-start(bf16[1152,128]{1,0:T(8,128)(2,1)} %get-tuple-element.71), channel_id=1, source_target_pairs={{0,32},{4,36},{8,40},{12,44},{16,48},{20,52},{24,56},{28,60},{32,6... | collective-permute-start | bytes 884744 | tf_op jit(solution)/shard_map/ppermute | solution.py:417
  55.9 7.4 %collective-permute-start.7 = (bf16[1152,128]{1,0:T(8,128)(2,1)}, bf16[1152,128]{1,0:T(8,128)(2,1)}, u32[]{:S(2)}, u32[]{:S(2)}) collective-permute-start(bf16[1152,128]{1,0:T(8,128)(2,1)} %get-tuple-element.72), channel_id=1, source_target_pairs={{0,224},{4,228},{8,232},{12,236},{16,240},{20,244},{24,248},{28,25... | collective-permute-start | bytes 884744 | tf_op jit(solution)/shard_map/ppermute | solution.py:417
  58.9 0.7 copy-start.5
  59.6 1.1 %copy-start.2 = (bf16[2304,128]{1,0:T(8,128)(2,1)S(1)}, bf16[2304,128]{1,0:T(8,128)(2,1)}, u32[]{:S(2)}) copy-start(bf16[2304,128]{1,0:T(8,128)(2,1)} %copy-done.1) | copy-start | bytes 1769476
  60.7 7.7 %copy-start.11 = (bf16[256,8192]{1,0:T(8,128)(2,1)S(1)}, bf16[256,8192]{1,0:T(8,128)(2,1)}, u32[]{:S(2)}) copy-start(bf16[256,8192]{1,0:T(8,128)(2,1)} %param.12) | copy-start | bytes 12582916
  64.7 9.3 %copy-start.3 = (bf16[2304,128]{1,0:T(8,128)(2,1)S(1)}, bf16[2304,128]{1,0:T(8,128)(2,1)}, u32[]{:S(2)}) copy-start(bf16[2304,128]{1,0:T(8,128)(2,1)} %copy-done.1) | copy-start | bytes 1769476
  64.7 7.2 %collective-permute-start.10 = (f32[256,128]{1,0:T(8,128)S(1)}, f32[256,128]{1,0:T(8,128)S(1)}, u32[]{:S(2)}, u32[]{:S(2)}) collective-permute-start(f32[256,128]{1,0:T(8,128)S(1)} %shard_map.138.p0), channel_id=1, source_target_pairs={{0,3},{1,0},{2,1},{3,2},{4,7},{5,4},{6,5},{7,6},{8,11},{9,8},{10,9... | collective-permute-start | bytes 393224 | tf_op jit(solution)/shard_map/ppermute | solution.py:480
  67.3 5.4 %collective-permute-start.9 = (f32[256,128]{1,0:T(8,128)S(1)}, f32[256,128]{1,0:T(8,128)S(1)}, u32[]{:S(2)}, u32[]{:S(2)}) collective-permute-start(f32[256,128]{1,0:T(8,128)S(1)} %shard_map.138.p0), channel_id=1, source_target_pairs={{0,2},{1,3},{2,0},{3,1},{4,6},{5,7},{6,4},{7,5},{8,10},{9,11},{10,... | collective-permute-start | bytes 393224 | tf_op jit(solution)/shard_map/ppermute | solution.py:480
  67.8 6.2 %collective-permute-start.8 = (f32[256,128]{1,0:T(8,128)S(1)}, f32[256,128]{1,0:T(8,128)S(1)}, u32[]{:S(2)}, u32[]{:S(2)}) collective-permute-start(f32[256,128]{1,0:T(8,128)S(1)} %shard_map.138.p0), channel_id=1, source_target_pairs={{0,1},{1,2},{2,3},{3,0},{4,5},{5,6},{6,7},{7,4},{8,9},{9,10},{10,1... | collective-permute-start | bytes 393224 | tf_op jit(solution)/shard_map/ppermute | solution.py:480
  71.9 20.8 %copy-start = (f32[256,2048]{1,0:T(8,128)S(1)}, f32[256,2048]{1,0:T(8,128)}, u32[]{:S(2)}) copy-start(f32[256,2048]{1,0:T(8,128)} %get-tuple-element.94.ctx_ref) | copy-start | bytes 6291460
  71.9 20.8 %copy-start.6 = (bf16[256,512]{1,0:T(8,128)(2,1)S(1)}, bf16[256,512]{1,0:T(8,128)(2,1)}, u32[]{:S(2)}) copy-start(bf16[256,512]{1,0:T(8,128)(2,1)} %copy-done.5) | copy-start | bytes 786436
  72.0 20.8 %copy-start.10 = (f32[256,128]{1,0:T(8,128)S(1)}, f32[256,128]{1,0:T(8,128)}, u32[]{:S(2)}) copy-start(f32[256,128]{1,0:T(8,128)} %get-tuple-element.95.own_ref) | copy-start | bytes 393220

commit v4 on v3

--- a/solution.py
+++ b/solution.py
@@ -361,7 +361,7 @@
 
 def finish(un, delta, base, ctx, own):
     rows, wide = ctx.shape
-    step = 64
+    step = 128
     by_row = lambda n: pl.BlockSpec((step, n), lambda i: (i, 0))
     whole = lambda a: pl.BlockSpec(a.shape, lambda i: (0, 0))
     return pl.pallas_call(
@@ -444,18 +444,16 @@
     (choice,) = vmem_call(
         functools.partial(choose_kernel, PLANE, sizes), [((count, both), f32)], meta, token
     )
-    up[0], choice, lengths = lax.optimization_barrier((up[0], choice, lengths))
+    up[0], down[0], choice, queries, lengths = lax.optimization_barrier(
+        (up[0], down[0], choice, queries, lengths)
+    )
     up.append(shift_z(up[0], 1))
-    down[0], choice, lengths = lax.optimization_barrier((down[0], choice, lengths))
     down.append(shift_z(down[0], -1))
-    up[0], down[0], queries = lax.optimization_barrier((up[0], down[0], queries))
     steps = rows // 64
     done = attend(0, steps, queries, new_key, cache_keys, cache_values, lengths)
-    up[1], done = lax.optimization_barrier((up[1], done))
+    up[1], down[1], done, queries = lax.optimization_barrier((up[1], down[1], done, queries))
     up.append(shift_z(up[1], 1))
-    down[1], done = lax.optimization_barrier((down[1], done))
     down.append(shift_z(down[1], -1))
-    up[1], down[1], queries = lax.optimization_barrier((up[1], down[1], queries))
     ctx, own = attend(steps, steps, queries, new_key, cache_keys, cache_values, lengths, done)
     up[2], down[2], ctx, own, meta = lax.optimization_barrier((up[2], down[2], ctx, own, meta))
     half_up, half_down = halves(up[2], down[2])

time: 95.6 us -> 92.7 us (0.970)
  waiting for transfers between devices: 9.61 us -> 7.4 us
    ppermute x8, waiting for transfers between devices: 7.55 us -> 5.36 us  [shift_z(): lax.ppermute(x, 'rows', [(r, (r + by * PLANE) % groups) for r in range(gr...]
  transfers between devices with their start and end apart: 12 -> 12, of which waited for: 5 -> 6; matrix products, arithmetic and copies ran while one was open for 7% -> 7% of each run, Pallas kernels for 28% -> 29%
where the time goes in v4:
time: 92.7 us; the launch traced here: 92 us
  Pallas kernels  31 us (33%)
  starting transfers between devices  23.6 us (25%)
  blocking collectives  16.8 us (18%)
  local copies, waits for them, and re-layouts  8.15 us (9%)
  waiting for transfers between devices  7.4 us (8%)
  matrix products  3.5 us (4%)
    pallas_call x2, Pallas kernels, attend(): pl.pallas_call(functools.partial(attend_kernel, 1.0 / math.sqrt(HEAD)), o...  20.5 us
    all_to_all x1, blocking collectives, over_plane(): lax.all_to_all(x.reshape(PLANE, size // PLANE, wide), 'rows', split_axis=...  16.8 us
    ppermute x8, starting transfers between devices, shift_z(): lax.ppermute(x, 'rows', [(r, (r + by * PLANE) % groups) for r in range(gr...  14.5 us
    all_to_all x1, starting transfers between devices, over_plane(): lax.all_to_all(x.reshape(PLANE, size // PLANE, wide), 'rows', split_axis=...  5.42 us
    ppermute x8, waiting for transfers between devices, shift_z(): lax.ppermute(x, 'rows', [(r, (r + by * PLANE) % groups) for r in range(gr...  5.36 us
    pallas_call x4, Pallas kernels, vmem_call(): pl.pallas_call(kernel, out_shape=tuple((jax.ShapeDtypeStruct(shape, dtype...  4.76 us
    unnamed x26, local copies, waits for them, and re-layouts  3.95 us
    ppermute x3, starting transfers between devices, body(): lax.ppermute(partial, 'tp', [(j, (j + k) % tp) for j in range(tp)])  3.68 us
  transfers between devices with their start and end apart: 12, of which 6 were waited for; matrix products, arithmetic and copies ran while one was open for 7% of the time, Pallas kernels for 29%

profile of v4, /device:TPU:1, one launch (start us, length us, event | category | flops | bytes accessed | tf_op | source)
XLA Modules:
  0.0 92.0 jit_solution(10036747602375918273)
XLA Ops:
  0.6 0.8 fusion
  1.4 1.3 %copy.17 = bf16[2048,128]{1,0:T(8,128)(2,1)S(1)} copy(bf16[2048,128]{0,1:T(8,128)(2,1)} %bitcast.16) | data formatting | bytes 1048576 | tf_op jit(solution)/shard_map/reshape | solution.py:434
  2.7 0.0 copy-start.12
  2.8 6.5 %collective-permute-start.1 = (bf16[2304,128]{1,0:T(8,128)(2,1)S(1)}, bf16[2304,128]{1,0:T(8,128)(2,1)S(1)}, u32[]{:S(2)}, u32[]{:S(2)}) collective-permute-start(bf16[2304,128]{1,0:T(8,128)(2,1)S(1)} %pad_maximum_fusion.own_ref.own), channel_id=1, source_target_pairs={{0,224},{4,228},{8,232},{12,236},{16,240},{20,244},{24,248},{28,25... | collective-permute-start | bytes 1769480 | tf_op jit(solution)/shard_map/ppermute | solution.py:417
  9.3 0.0 collective-permute-start
  9.3 0.8 pad_add_fusion.meta_ref
  10.0 1.3 %constant_dynamic-slice_fusion.x_ref = bf16[256,2048]{1,0:T(8,128)(2,1)S(1)} fusion(bf16[256,8192]{1,0:T(8,128)(2,1)} %param.12, s32[]{:T(128)S(6)} %select_n.3), kind=kLoop, calls=%fused_computation.3 | loop fusion | bytes 2097156 | tf_op jit(solution)/shard_map/dynamic_slice | solution.py:441
  11.4 1.0 %shard_map.131 = (bf16[512,2048]{1,0:T(8,128)(2,1)S(1)}, s32[8,128]{1,0:T(8,128)S(1)}) custom-call(s32[66,128]{1,0:T(8,128)S(1)} %pad_add_fusion.meta_ref, bf16[256,2048]{1,0:T(8,128)(2,1)S(1)} %constant_dynamic-slice_fusion.x_ref), custom_call_target="tpu_custom_call" | custom-call | tf_op jit(solution)/shard_map/pallas_call | solution.py:84
  12.3 0.0 copy-start.4
  12.3 1.3 %copy-done.4 = bf16[512,2048]{1,0:T(8,128)(2,1)} copy-done((bf16[512,2048]{1,0:T(8,128)(2,1)}, bf16[512,2048]{1,0:T(8,128)(2,1)S(1)}, u32[]{:S(2)}) %copy-start.4) | copy-done | bytes 2097176
  13.7 5.4 %all-to-all-start = ((bf16[8,64,2048]{2,1,0:T(8,128)(2,1)}), bf16[8,64,2048]{2,1,0:T(8,128)(2,1)S(1)}, u32[]{:S(2)}, u32[]{:S(2)}) async-start(bf16[8,64,2048]{2,1,0:T(8,128)(2,1)} %bitcast.13), calls=%async_computation | async-start | bytes 4194304 | tf_op jit(solution)/shard_map/all_to_all | solution.py:423
  19.1 0.8 copy-done.8
  19.9 0.5 shard_map.132.choice_ref
  20.4 0.9 collective-permute-done.1.d1
  21.3 3.2 %collective-permute-done.u1 = bf16[2304,128]{1,0:T(8,128)(2,1)} collective-permute-done((bf16[2304,128]{1,0:T(8,128)(2,1)S(1)}, bf16[2304,128]{1,0:T(8,128)(2,1)}, u32[]{:S(2)}, u32[]{:S(2)}) %collective-permute-start) | collective-permute-done | bytes 589856 | tf_op jit(solution)/shard_map/ppermute | solution.py:417
  24.5 0.0 collective-permute-start.2
  24.5 2.7 %collective-permute-start.3 = (bf16[2304,128]{1,0:T(8,128)(2,1)S(1)}, bf16[2304,128]{1,0:T(8,128)(2,1)}, u32[]{:S(2)}, u32[]{:S(2)}) collective-permute-start(bf16[2304,128]{1,0:T(8,128)(2,1)S(1)} %collective-permute-done.1.d1), channel_id=1, source_target_pairs={{0,224},{4,228},{8,232},{12,236},{16,240},{20,244},{24,248},{28,25... | collective-permute-start | bytes 1769480 | tf_op jit(solution)/shard_map/ppermute | solution.py:417
  27.1 0.8 copy.18.len_ref
  27.9 10.3 %shard_map.133 = (f32[256,2048]{1,0:T(8,128)}, f32[256,128]{1,0:T(8,128)}) custom-call(bf16[256,2048]{1,0:T(8,128)(2,1)} %q_ref.1, bf16[256,256]{1,0:T(8,128)(2,1)} %nk_ref.3, bf16[256,32,256]{2,1,0:T(8,128)(2,1)} %k_ref.3, bf16[256,32,256]{2,1,0:T(8,128)(2,1)} %v_ref.3, s32[256,1]{1,0:T(8,128)} %copy.18.len_ref), custom_call_target="tpu_custom_call" | custom-call | tf_op jit(solution)/shard_map/pallas_call | solution.py:322
  38.2 0.7 collective-permute-done.2.u2
  38.9 0.0 collective-permute-done.3.d2
  39.0 0.0 collective-permute-start.4
  39.0 2.7 %collective-permute-start.5 = (bf16[2304,128]{1,0:T(8,128)(2,1)}, bf16[2304,128]{1,0:T(8,128)(2,1)}, u32[]{:S(2)}, u32[]{:S(2)}) collective-permute-start(bf16[2304,128]{1,0:T(8,128)(2,1)} %collective-permute-done.3.d2), channel_id=1, source_target_pairs={{0,224},{4,228},{8,232},{12,236},{16,240},{20,244},{24,248},{28,25... | collective-permute-start | bytes 1769480 | tf_op jit(solution)/shard_map/ppermute | solution.py:417
  41.6 10.3 %shard_map.134 = (f32[256,2048]{1,0:T(8,128)}, f32[256,128]{1,0:T(8,128)}) custom-call(bf16[256,2048]{1,0:T(8,128)(2,1)} %q_ref.1, bf16[256,256]{1,0:T(8,128)(2,1)} %nk_ref.3, bf16[256,32,256]{2,1,0:T(8,128)(2,1)} %k_ref.3, bf16[256,32,256]{2,1,0:T(8,128)(2,1)} %v_ref.3, s32[256,1]{1,0:T(8,128)} %copy.18.len_ref, ...), custom_call_target="tpu_custom_call", output_to_operand_aliasing={{0}: (5, {}), {1}: (6, {})} | custom-call | tf_op jit(solution)/shard_map/pallas_call | solution.py:322
  51.9 0.5 collective-permute-done.4.a_ref.u3
  52.4 0.0 collective-permute-done.5.b_ref.d3
  52.4 1.8 %shard_map.135 = (bf16[1152,128]{1,0:T(8,128)(2,1)}, bf16[1152,128]{1,0:T(8,128)(2,1)}) custom-call(bf16[2304,128]{1,0:T(8,128)(2,1)S(1)} %collective-permute-done.4.a_ref.u3, bf16[2304,128]{1,0:T(8,128)(2,1)} %collective-permute-done.5.b_ref.d3), custom_call_target="tpu_custom_call" | custom-call | tf_op jit(solution)/shard_map/pallas_call | solution.py:223
  54.2 0.0 collective-permute-start.6
  54.2 2.7 %collective-permute-start.7 = (bf16[1152,128]{1,0:T(8,128)(2,1)}, bf16[1152,128]{1,0:T(8,128)(2,1)}, u32[]{:S(2)}, u32[]{:S(2)}) collective-permute-start(bf16[1152,128]{1,0:T(8,128)(2,1)} %get-tuple-element.60), channel_id=1, source_target_pairs={{0,224},{4,228},{8,232},{12,236},{16,240},{20,244},{24,248},{28,25... | collective-permute-start | bytes 884744 | tf_op jit(solution)/shard_map/ppermute | solution.py:417
  56.9 0.3 shard_map.137.un_ref
  57.2 0.7 copy-done.5
  57.9 0.0 all-to-all-done
  57.9 1.1 %copy-done.2 = bf16[2304,128]{1,0:T(8,128)(2,1)S(1)} copy-done((bf16[2304,128]{1,0:T(8,128)(2,1)S(1)}, bf16[2304,128]{1,0:T(8,128)(2,1)}, u32[]{:S(2)}) %copy-start.2) | copy-done | bytes 589848
  59.0 2.6 %shard_map.136 = (f32[256,128]{1,0:T(8,128)S(1)}, bf16[128,2048]{1,0:T(8,128)(2,1)S(1)}) custom-call(f32[512,128]{1,0:T(8,128)S(1)} %shard_map.132.choice_ref, bf16[512,2048]{1,0:T(8,128)(2,1)S(1)} %bitcast.12, bf16[2304,128]{1,0:T(8,128)(2,1)S(1)} %pad_maximum_fusion.own_ref.own, bf16[2304,128]{1,0:T(8,128)(2,1)S(1)} %copy-done.2, ...), custom_call_target="tpu_custom_call" | custom-call | tf_op jit(solution)/shard_map/pallas_call | solution.py:254
  61.5 0.0 collective-permute-done.6.a_ref
  61.6 0.0 collective-permute-done.7.b_ref.last
  61.6 1.4 %shard_map.138.p0 = f32[256,128]{1,0:T(8,128)S(1)} custom-call(f32[512,128]{1,0:T(8,128)S(1)} %shard_map.132.choice_ref, bf16[128,2048]{1,0:T(8,128)(2,1)S(1)} %get-tuple-element.68.kept_ref, bf16[1152,128]{1,0:T(8,128)(2,1)} %collective-permute-done.6.a_ref, bf16[1152,128]{1,0:T(8,128)(2,1)} %collective-permute-done.7.b_ref.last, ...), custom_call_target="tpu_custom_call" | custom-call | tf_op jit(solution)/shard_map/pallas_call | solution.py:254
  63.0 0.0 copy-start.3
  63.0 2.5 %collective-permute-start.10 = (f32[256,128]{1,0:T(8,128)S(1)}, f32[256,128]{1,0:T(8,128)S(1)}, u32[]{:S(2)}, u32[]{:S(2)}) collective-permute-start(f32[256,128]{1,0:T(8,128)S(1)} %shard_map.138.p0), channel_id=1, source_target_pairs={{0,3},{1,0},{2,1},{3,2},{4,7},{5,4},{6,5},{7,6},{8,11},{9,8},{10,9... | collective-permute-start | bytes 393224 | tf_op jit(solution)/shard_map/ppermute | solution.py:478
  65.5 0.5 collective-permute-start.9
  66.1 0.6 collective-permute-start.8
  66.7 3.5 %fusion.1.base_ref = f32[256,256]{1,0:T(8,128)S(1)} fusion(bf16[256,8192]{1,0:T(8,128)(2,1)S(1)} %copy-done.11, bf16[8192,256]{1,0:T(8,128)(2,1)} %param.13), kind=kOutput, calls=%fused_computation.5 | convolution fusion | flops 1073741824 | bytes 8650752 | tf_op jit(solution)/shard_map/dot_general | solution.py:481
  70.2 0.0 collective-permute-done.10.p3
  70.2 0.7 collective-permute-done.9.p2
  71.0 1.3 %collective-permute-done.8.p1 = f32[256,128]{1,0:T(8,128)S(1)} collective-permute-done((f32[256,128]{1,0:T(8,128)S(1)}, f32[256,128]{1,0:T(8,128)S(1)}, u32[]{:S(2)}, u32[]{:S(2)}) %collective-permute-start.8) | collective-permute-done | bytes 131104 | tf_op jit(solution)/shard_map/ppermute | solution.py:478
  72.3 1.3 %shard_map.139 = bf16[512,256]{1,0:T(8,128)(2,1)S(1)} custom-call(f32[512,128]{1,0:T(8,128)S(1)} %shard_map.132.choice_ref, f32[256,128]{1,0:T(8,128)S(1)} %shard_map.138.p0, f32[256,128]{1,0:T(8,128)S(1)} %collective-permute-done.8.p1, f32[256,128]{1,0:T(8,128)S(1)} %collective-permute-done.9.p2, f32[256,128]{1,0:T(8,128)S(1)} %collective-permute-done.10.p3, ...), custom_call_target="tpu_custom_call" | custom-call | tf_op jit(solution)/shard_map/pallas_call | solution.py:242
  73.6 16.8 %all_to_all.10 = bf16[8,64,256]{2,1,0:T(8,128)(2,1)S(1)} all-to-all(bf16[8,64,256]{2,1,0:T(8,128)(2,1)S(1)} %bitcast.15), channel_id=1, replica_groups={{0,4,8,12,16,20,24,28},{32,36,40,44,48,52,56,60},{64,68,72,76,80,84,88,..., dimensions={0} | all-to-all | bytes 524288 | tf_op jit(solution)/shard_map/all_to_all | solution.py:423
  90.4 1.6 %shard_map.140 = (bf16[256,256]{1,0:T(8,128)(2,1)}, bf16[256,2048]{1,0:T(8,128)(2,1)}) custom-call(bf16[256,512]{1,0:T(8,128)(2,1)S(1)} %copy-done.6, bf16[512,256]{1,0:T(8,128)(2,1)S(1)} %bitcast.14, f32[256,256]{1,0:T(8,128)S(1)} %fusion.1.base_ref, f32[256,2048]{1,0:T(8,128)S(1)} %copy-done, f32[256,128]{1,0:T(8,128)S(1)} %copy-done.10), custom_call_target="tpu_custom_call" | custom-call | tf_op jit(solution)/shard_map/pallas_call | solution.py:367
  (20 shorter events, 0.1 us)
Async XLA Ops:
  2.7 24.4 %copy-start.12 = (s32[1,256]{1,0:T(1,128)S(1)}, s32[1,256]{1,0:T(1,128)}, u32[]{:S(2)}) copy-start(s32[1,256]{1,0:T(1,128)} %param.19) | copy-start | bytes 3076
  2.8 18.5 %collective-permute-start.1 = (bf16[2304,128]{1,0:T(8,128)(2,1)S(1)}, bf16[2304,128]{1,0:T(8,128)(2,1)S(1)}, u32[]{:S(2)}, u32[]{:S(2)}) collective-permute-start(bf16[2304,128]{1,0:T(8,128)(2,1)S(1)} %pad_maximum_fusion.own_ref.own), channel_id=1, source_target_pairs={{0,224},{4,228},{8,232},{12,236},{16,240},{20,244},{24,248},{28,25... | collective-permute-start | bytes 1769480 | tf_op jit(solution)/shard_map/ppermute | solution.py:417
  9.3 15.2 %collective-permute-start = (bf16[2304,128]{1,0:T(8,128)(2,1)S(1)}, bf16[2304,128]{1,0:T(8,128)(2,1)}, u32[]{:S(2)}, u32[]{:S(2)}) collective-permute-start(bf16[2304,128]{1,0:T(8,128)(2,1)S(1)} %pad_maximum_fusion.own_ref.own), channel_id=1, source_target_pairs={{0,32},{4,36},{8,40},{12,44},{16,48},{20,52},{24,56},{28,60},{32,6... | collective-permute-start | bytes 1769480 | tf_op jit(solution)/shard_map/ppermute | solution.py:417
  10.0 9.0 %copy-start.7 = (s32[66,128]{1,0:T(8,128)}, s32[66,128]{1,0:T(8,128)S(1)}, u32[]{:S(2)}) copy-start(s32[66,128]{1,0:T(8,128)S(1)} %pad_add_fusion.meta_ref) | copy-start | bytes 101380
  12.3 1.3 %copy-start.4 = (bf16[512,2048]{1,0:T(8,128)(2,1)}, bf16[512,2048]{1,0:T(8,128)(2,1)S(1)}, u32[]{:S(2)}) copy-start(bf16[512,2048]{1,0:T(8,128)(2,1)S(1)} %get-tuple-element.62) | copy-start | bytes 6291460
  13.7 44.2 %all-to-all-start = ((bf16[8,64,2048]{2,1,0:T(8,128)(2,1)}), bf16[8,64,2048]{2,1,0:T(8,128)(2,1)S(1)}, u32[]{:S(2)}, u32[]{:S(2)}) async-start(bf16[8,64,2048]{2,1,0:T(8,128)(2,1)} %bitcast.13), calls=%async_computation | async-start | bytes 4194304 | tf_op jit(solution)/shard_map/all_to_all | solution.py:423
  19.1 0.8 copy-start.8
  21.3 16.9 %copy-start.1 = (bf16[2304,128]{1,0:T(8,128)(2,1)}, bf16[2304,128]{1,0:T(8,128)(2,1)S(1)}, u32[]{:S(2)}) copy-start(bf16[2304,128]{1,0:T(8,128)(2,1)S(1)} %collective-permute-done.1.d1) | copy-start | bytes 1769476
  24.5 14.5 %collective-permute-start.2 = (bf16[2304,128]{1,0:T(8,128)(2,1)}, bf16[2304,128]{1,0:T(8,128)(2,1)}, u32[]{:S(2)}, u32[]{:S(2)}) collective-permute-start(bf16[2304,128]{1,0:T(8,128)(2,1)} %collective-permute-done.u1), channel_id=1, source_target_pairs={{0,32},{4,36},{8,40},{12,44},{16,48},{20,52},{24,56},{28,60},{32,6... | collective-permute-start | bytes 1769480 | tf_op jit(solution)/shard_map/ppermute | solution.py:417
  24.5 14.5 %collective-permute-start.3 = (bf16[2304,128]{1,0:T(8,128)(2,1)S(1)}, bf16[2304,128]{1,0:T(8,128)(2,1)}, u32[]{:S(2)}, u32[]{:S(2)}) collective-permute-start(bf16[2304,128]{1,0:T(8,128)(2,1)S(1)} %collective-permute-done.1.d1), channel_id=1, source_target_pairs={{0,224},{4,228},{8,232},{12,236},{16,240},{20,244},{24,248},{28,25... | collective-permute-start | bytes 1769480 | tf_op jit(solution)/shard_map/ppermute | solution.py:417
  39.0 17.9 %copy-start.9 = (s32[66,128]{1,0:T(8,128)S(1)}, s32[66,128]{1,0:T(8,128)}, u32[]{:S(2)}) copy-start(s32[66,128]{1,0:T(8,128)} %copy-done.7) | copy-start | bytes 101380
  39.0 13.5 %collective-permute-start.4 = (bf16[2304,128]{1,0:T(8,128)(2,1)}, bf16[2304,128]{1,0:T(8,128)(2,1)S(1)}, u32[]{:S(2)}, u32[]{:S(2)}) collective-permute-start(bf16[2304,128]{1,0:T(8,128)(2,1)} %collective-permute-done.2.u2), channel_id=1, source_target_pairs={{0,32},{4,36},{8,40},{12,44},{16,48},{20,52},{24,56},{28,60},{32,6... | collective-permute-start | bytes 1769480 | tf_op jit(solution)/shard_map/ppermute | solution.py:417
  39.0 13.5 %collective-permute-start.5 = (bf16[2304,128]{1,0:T(8,128)(2,1)}, bf16[2304,128]{1,0:T(8,128)(2,1)}, u32[]{:S(2)}, u32[]{:S(2)}) collective-permute-start(bf16[2304,128]{1,0:T(8,128)(2,1)} %collective-permute-done.3.d2), channel_id=1, source_target_pairs={{0,224},{4,228},{8,232},{12,236},{16,240},{20,244},{24,248},{28,25... | collective-permute-start | bytes 1769480 | tf_op jit(solution)/shard_map/ppermute | solution.py:417
  54.2 7.4 %collective-permute-start.6 = (bf16[1152,128]{1,0:T(8,128)(2,1)}, bf16[1152,128]{1,0:T(8,128)(2,1)}, u32[]{:S(2)}, u32[]{:S(2)}) collective-permute-start(bf16[1152,128]{1,0:T(8,128)(2,1)} %get-tuple-element.59), channel_id=1, source_target_pairs={{0,32},{4,36},{8,40},{12,44},{16,48},{20,52},{24,56},{28,60},{32,6... | collective-permute-start | bytes 884744 | tf_op jit(solution)/shard_map/ppermute | solution.py:417
  54.2 7.4 %collective-permute-start.7 = (bf16[1152,128]{1,0:T(8,128)(2,1)}, bf16[1152,128]{1,0:T(8,128)(2,1)}, u32[]{:S(2)}, u32[]{:S(2)}) collective-permute-start(bf16[1152,128]{1,0:T(8,128)(2,1)} %get-tuple-element.60), channel_id=1, source_target_pairs={{0,224},{4,228},{8,232},{12,236},{16,240},{20,244},{24,248},{28,25... | collective-permute-start | bytes 884744 | tf_op jit(solution)/shard_map/ppermute | solution.py:417
  57.1 0.7 copy-start.5
  57.9 1.1 %copy-start.2 = (bf16[2304,128]{1,0:T(8,128)(2,1)S(1)}, bf16[2304,128]{1,0:T(8,128)(2,1)}, u32[]{:S(2)}) copy-start(bf16[2304,128]{1,0:T(8,128)(2,1)} %copy-done.1) | copy-start | bytes 1769476
  59.0 7.7 %copy-start.11 = (bf16[256,8192]{1,0:T(8,128)(2,1)S(1)}, bf16[256,8192]{1,0:T(8,128)(2,1)}, u32[]{:S(2)}) copy-start(bf16[256,8192]{1,0:T(8,128)(2,1)} %param.12) | copy-start | bytes 12582916
  63.0 9.3 %copy-start.3 = (bf16[2304,128]{1,0:T(8,128)(2,1)S(1)}, bf16[2304,128]{1,0:T(8,128)(2,1)}, u32[]{:S(2)}) copy-start(bf16[2304,128]{1,0:T(8,128)(2,1)} %copy-done.1) | copy-start | bytes 1769476
  63.0 7.2 %collective-permute-start.10 = (f32[256,128]{1,0:T(8,128)S(1)}, f32[256,128]{1,0:T(8,128)S(1)}, u32[]{:S(2)}, u32[]{:S(2)}) collective-permute-start(f32[256,128]{1,0:T(8,128)S(1)} %shard_map.138.p0), channel_id=1, source_target_pairs={{0,3},{1,0},{2,1},{3,2},{4,7},{5,4},{6,5},{7,6},{8,11},{9,8},{10,9... | collective-permute-start | bytes 393224 | tf_op jit(solution)/shard_map/ppermute | solution.py:478
  65.5 5.4 %collective-permute-start.9 = (f32[256,128]{1,0:T(8,128)S(1)}, f32[256,128]{1,0:T(8,128)S(1)}, u32[]{:S(2)}, u32[]{:S(2)}) collective-permute-start(f32[256,128]{1,0:T(8,128)S(1)} %shard_map.138.p0), channel_id=1, source_target_pairs={{0,2},{1,3},{2,0},{3,1},{4,6},{5,7},{6,4},{7,5},{8,10},{9,11},{10,... | collective-permute-start | bytes 393224 | tf_op jit(solution)/shard_map/ppermute | solution.py:478
  66.1 6.2 %collective-permute-start.8 = (f32[256,128]{1,0:T(8,128)S(1)}, f32[256,128]{1,0:T(8,128)S(1)}, u32[]{:S(2)}, u32[]{:S(2)}) collective-permute-start(f32[256,128]{1,0:T(8,128)S(1)} %shard_map.138.p0), channel_id=1, source_target_pairs={{0,1},{1,2},{2,3},{3,0},{4,5},{5,6},{6,7},{7,4},{8,9},{9,10},{10,1... | collective-permute-start | bytes 393224 | tf_op jit(solution)/shard_map/ppermute | solution.py:478
  70.2 20.2 %copy-start = (f32[256,2048]{1,0:T(8,128)S(1)}, f32[256,2048]{1,0:T(8,128)}, u32[]{:S(2)}) copy-start(f32[256,2048]{1,0:T(8,128)} %get-tuple-element.78.ctx_ref) | copy-start | bytes 6291460
  70.2 20.2 %copy-start.6 = (bf16[256,512]{1,0:T(8,128)(2,1)S(1)}, bf16[256,512]{1,0:T(8,128)(2,1)}, u32[]{:S(2)}) copy-start(bf16[256,512]{1,0:T(8,128)(2,1)} %copy-done.5) | copy-start | bytes 786436
  70.2 20.2 %copy-start.10 = (f32[256,128]{1,0:T(8,128)S(1)}, f32[256,128]{1,0:T(8,128)}, u32[]{:S(2)}) copy-start(f32[256,128]{1,0:T(8,128)} %get-tuple-element.79.own_ref) | copy-start | bytes 393220

commit v5 on v4

--- a/solution.py
+++ b/solution.py
@@ -144,7 +144,7 @@
     return jnp.where(second, turned, low), jnp.where(second, low, turned)
 
 
-def early_kernel(choice_ref, x_ref, own_ref, d1, u1, d2, u2, d3, u3, out_ref, kept_ref):
+def early_kernel(choice_ref, x_ref, own_ref, d1, u1, d2, u2, d3, u3, out_ref, kept_ref, b_ref):
     part = x_ref.shape[1]
     many, both = out_ref.shape[0] // 2, out_ref.shape[1]
     odd = jnp.bitwise_and(iota((many, both), 0), MOST) > 0
@@ -156,6 +156,8 @@
         a = jnp.concatenate([even_map[:part], odd_map[:part]], axis=1)
         each = jnp.dot(pair_rows(x_ref, i + 1), a, preferred_element_type=f32)
         sides.append(turn(jnp.where(odd, each[:, both:], each[:, :both]), second[i + 1]))
+    for i, ref in enumerate((own_ref, d1, u1, d2, u2, d3, u3)):
+        b_ref[i] = ref[part:]
     left = iota((many, both), 1) < both // 2
     out_ref[:many] = jnp.where(left, sides[0][0], sides[2][1])
     out_ref[many:] = jnp.where(left, sides[1][0], sides[3][1])
@@ -174,7 +176,7 @@
     out_ref[many:] = early_ref[many:]
 
 
-def delta_kernel(choice_ref, p0, p1, p2, p3, own, last, d1, u1, d2, u2, d3, u3, out_ref):
+def delta_kernel(choice_ref, p0, p1, p2, p3, maps_ref, last, out_ref):
     count, width = out_ref.shape
     half, both = p0.shape
     rank = both // 2
@@ -190,15 +192,13 @@
         [jnp.where(odd, 0.0, low), jnp.where(odd, low, 0.0)], axis=1
     ).astype(bf16)
     many = count // 4
-    for pair, refs in enumerate(((own, last), (d1, u1), (d2, u2), (d3, u3))):
-        wide = []
-        for ref in refs:
-            first = ref.shape[0] - width
-            wide.append(
-                jnp.concatenate(
-                    [ref[first + at : first + at + both] for at in range(0, width, both)], axis=1
-                )
-            )
+    tail = last[last.shape[0] - width :]
+    for pair in range(4):
+        maps = (maps_ref[0], tail) if pair == 0 else (maps_ref[2 * pair - 1], maps_ref[2 * pair])
+        wide = [
+            jnp.concatenate([b[at : at + both] for at in range(0, width, both)], axis=1)
+            for b in maps
+        ]
         got = jnp.dot(
             spread[pair * many : (pair + 1) * many],
             jnp.concatenate(wide, axis=0),
@@ -229,25 +229,6 @@
         cost_estimate=FREE,
         compiler_params=params(),
     )(a, b)
-
-
-def delta_call(choice, parts, maps, count, width):
-    def whole(a):
-        return pl.BlockSpec(a.shape, lambda i: (0, 0))
-
-    def tail(a):
-        last = a.shape[0] // width - 1
-        return pl.BlockSpec((width, a.shape[1]), lambda i: (last, 0))
-
-    return pl.pallas_call(
-        delta_kernel,
-        out_shape=jax.ShapeDtypeStruct((count, width), bf16),
-        grid=(1,),
-        in_specs=[whole(a) for a in (choice, *parts)]
-        + [tail(a) if a.shape[0] % width == 0 else whole(a) for a in maps],
-        out_specs=pl.BlockSpec((count, width), lambda i: (0, 0)),
-        compiler_params=params(),
-    )(choice, *parts, *maps)
 
 
 def vmem_call(kernel, outs, *args):
@@ -462,15 +443,17 @@
         functools.partial(unplace_kernel, PLANE, sizes), [((rows, count), bf16)], meta, token
     )
     maps = [m for pair in zip(down, up) for m in pair]
-    early, kept = vmem_call(
+    early, kept, b_maps = vmem_call(
         early_kernel,
-        [((count // 2, both), f32), ((count // 4, part), bf16)],
+        [((count // 2, both), f32), ((count // 4, part), bf16), ((7, width, both), bf16)],
         choice,
         arrived,
         packed,
         *maps,
     )
-    last_a, last_b, early, kept, un = lax.optimization_barrier((last_a, last_b, early, kept, un))
+    last_a, last_b, early, kept, b_maps, un = lax.optimization_barrier(
+        (last_a, last_b, early, kept, b_maps, un)
+    )
     (partial,) = vmem_call(
         final_kernel, [((count // 2, both), f32)], choice, kept, last_a, last_b, early
     )
@@ -480,7 +463,9 @@
     partial, normed_rows = lax.optimization_barrier((partial, normed_rows))
     base = jnp.dot(normed_rows, value_weight, preferred_element_type=f32)
     *others, base = lax.optimization_barrier((*others, base))
-    out = delta_call(choice, [partial, *others], [packed, last_b, *maps], count, width)
+    (out,) = vmem_call(
+        delta_kernel, [((count, width), bf16)], choice, partial, *others, b_maps, last_b
+    )
     return finish(un, over_plane(out), base, ctx, own)
 
 

time: 92.7 us -> 92.7 us (level)
    pallas_call x1 -> x0, Pallas kernels: 1.34 us -> none  [delta_call(): pl.pallas_call(delta_kernel, out_shape=jax.ShapeDtypeStruct((count, width...]
    pallas_call x4 -> x5, Pallas kernels: 4.76 us -> 6.03 us  [vmem_call(): pl.pallas_call(kernel, out_shape=tuple((jax.ShapeDtypeStruct(shape, dtype...]
    unnamed x26 -> x24, local copies, waits for them, and re-layouts: 3.95 us -> 3.95 us
where the time goes in v5:
time: 92.7 us; the launch traced here: 92 us
  Pallas kernels  30.9 us (33%)
  starting transfers between devices  23.6 us (25%)
  blocking collectives  16.8 us (18%)
  local copies, waits for them, and re-layouts  8.16 us (9%)
  waiting for transfers between devices  7.44 us (8%)
  matrix products  3.51 us (4%)
    pallas_call x2, Pallas kernels, attend(): pl.pallas_call(functools.partial(attend_kernel, 1.0 / math.sqrt(HEAD)), o...  20.5 us
    all_to_all x1, blocking collectives, over_plane(): lax.all_to_all(x.reshape(PLANE, size // PLANE, wide), 'rows', split_axis=...  16.8 us
    ppermute x8, starting transfers between devices, shift_z(): lax.ppermute(x, 'rows', [(r, (r + by * PLANE) % groups) for r in range(gr...  14.5 us
    pallas_call x5, Pallas kernels, vmem_call(): pl.pallas_call(kernel, out_shape=tuple((jax.ShapeDtypeStruct(shape, dtype...  6.03 us
    all_to_all x1, starting transfers between devices, over_plane(): lax.all_to_all(x.reshape(PLANE, size // PLANE, wide), 'rows', split_axis=...  5.42 us
    ppermute x8, waiting for transfers between devices, shift_z(): lax.ppermute(x, 'rows', [(r, (r + by * PLANE) % groups) for r in range(gr...  5.36 us
    unnamed x24, local copies, waits for them, and re-layouts  3.95 us
    ppermute x3, starting transfers between devices, body(): lax.ppermute(partial, 'tp', [(j, (j + k) % tp) for j in range(tp)])  3.69 us
  transfers between devices with their start and end apart: 12, of which 6 were waited for; matrix products, arithmetic and copies ran while one was open for 7% of the time, Pallas kernels for 29%

profile of v5, /device:TPU:1, one launch (start us, length us, event | category | flops | bytes accessed | tf_op | source)
XLA Modules:
  0.0 92.0 jit_solution(11286858585773344835)
XLA Ops:
  0.6 0.8 fusion
  1.4 1.3 %copy.17 = bf16[2048,128]{1,0:T(8,128)(2,1)S(1)} copy(bf16[2048,128]{0,1:T(8,128)(2,1)} %bitcast.16) | data formatting | bytes 1048576 | tf_op jit(solution)/shard_map/reshape | solution.py:415
  2.7 0.0 copy-start.11
  2.8 6.5 %collective-permute-start.1 = (bf16[2304,128]{1,0:T(8,128)(2,1)S(1)}, bf16[2304,128]{1,0:T(8,128)(2,1)S(1)}, u32[]{:S(2)}, u32[]{:S(2)}) collective-permute-start(bf16[2304,128]{1,0:T(8,128)(2,1)S(1)} %pad_maximum_fusion.own_ref), channel_id=1, source_target_pairs={{0,224},{4,228},{8,232},{12,236},{16,240},{20,244},{24,248},{28,25... | collective-permute-start | bytes 1769480 | tf_op jit(solution)/shard_map/ppermute | solution.py:398
  9.3 0.0 collective-permute-start
  9.3 0.8 pad_add_fusion.meta_ref
  10.0 1.3 %constant_dynamic-slice_fusion.x_ref = bf16[256,2048]{1,0:T(8,128)(2,1)S(1)} fusion(bf16[256,8192]{1,0:T(8,128)(2,1)} %param.12, s32[]{:T(128)S(6)} %select_n.3), kind=kLoop, calls=%fused_computation.3 | loop fusion | bytes 2097156 | tf_op jit(solution)/shard_map/dynamic_slice | solution.py:422
  11.4 1.0 %shard_map.131 = (bf16[512,2048]{1,0:T(8,128)(2,1)S(1)}, s32[8,128]{1,0:T(8,128)S(1)}) custom-call(s32[66,128]{1,0:T(8,128)S(1)} %pad_add_fusion.meta_ref, bf16[256,2048]{1,0:T(8,128)(2,1)S(1)} %constant_dynamic-slice_fusion.x_ref), custom_call_target="tpu_custom_call" | custom-call | tf_op jit(solution)/shard_map/pallas_call | solution.py:84
  12.3 0.0 copy-start.1
  12.3 1.3 %copy-done.1 = bf16[512,2048]{1,0:T(8,128)(2,1)} copy-done((bf16[512,2048]{1,0:T(8,128)(2,1)}, bf16[512,2048]{1,0:T(8,128)(2,1)S(1)}, u32[]{:S(2)}) %copy-start.1) | copy-done | bytes 2097176
  13.7 5.4 %all-to-all-start = ((bf16[8,64,2048]{2,1,0:T(8,128)(2,1)}), bf16[8,64,2048]{2,1,0:T(8,128)(2,1)S(1)}, u32[]{:S(2)}, u32[]{:S(2)}) async-start(bf16[8,64,2048]{2,1,0:T(8,128)(2,1)} %bitcast.13), calls=%async_computation | async-start | bytes 4194304 | tf_op jit(solution)/shard_map/all_to_all | solution.py:404
  19.1 0.8 copy-done.7
  19.9 0.5 shard_map.132.choice_ref
  20.4 0.9 collective-permute-done.1.d1
  21.3 3.2 %collective-permute-done.u1 = bf16[2304,128]{1,0:T(8,128)(2,1)} collective-permute-done((bf16[2304,128]{1,0:T(8,128)(2,1)S(1)}, bf16[2304,128]{1,0:T(8,128)(2,1)}, u32[]{:S(2)}, u32[]{:S(2)}) %collective-permute-start) | collective-permute-done | bytes 589856 | tf_op jit(solution)/shard_map/ppermute | solution.py:398
  24.5 0.0 collective-permute-start.2
  24.5 2.7 %collective-permute-start.3 = (bf16[2304,128]{1,0:T(8,128)(2,1)S(1)}, bf16[2304,128]{1,0:T(8,128)(2,1)}, u32[]{:S(2)}, u32[]{:S(2)}) collective-permute-start(bf16[2304,128]{1,0:T(8,128)(2,1)S(1)} %collective-permute-done.1.d1), channel_id=1, source_target_pairs={{0,224},{4,228},{8,232},{12,236},{16,240},{20,244},{24,248},{28,25... | collective-permute-start | bytes 1769480 | tf_op jit(solution)/shard_map/ppermute | solution.py:398
  27.1 0.8 copy.18.len_ref
  27.9 10.2 %shard_map.133 = (f32[256,2048]{1,0:T(8,128)}, f32[256,128]{1,0:T(8,128)}) custom-call(bf16[256,2048]{1,0:T(8,128)(2,1)} %q_ref.1, bf16[256,256]{1,0:T(8,128)(2,1)} %nk_ref.3, bf16[256,32,256]{2,1,0:T(8,128)(2,1)} %k_ref.3, bf16[256,32,256]{2,1,0:T(8,128)(2,1)} %v_ref.3, s32[256,1]{1,0:T(8,128)} %copy.18.len_ref), custom_call_target="tpu_custom_call" | custom-call | tf_op jit(solution)/shard_map/pallas_call | solution.py:303
  38.2 0.7 collective-permute-done.2.u2
  38.9 0.0 collective-permute-done.3.d2
  39.0 0.0 collective-permute-start.4
  39.0 2.7 %collective-permute-start.5 = (bf16[2304,128]{1,0:T(8,128)(2,1)}, bf16[2304,128]{1,0:T(8,128)(2,1)}, u32[]{:S(2)}, u32[]{:S(2)}) collective-permute-start(bf16[2304,128]{1,0:T(8,128)(2,1)} %collective-permute-done.3.d2), channel_id=1, source_target_pairs={{0,224},{4,228},{8,232},{12,236},{16,240},{20,244},{24,248},{28,25... | collective-permute-start | bytes 1769480 | tf_op jit(solution)/shard_map/ppermute | solution.py:398
  41.6 10.3 %shard_map.134 = (f32[256,2048]{1,0:T(8,128)}, f32[256,128]{1,0:T(8,128)}) custom-call(bf16[256,2048]{1,0:T(8,128)(2,1)} %q_ref.1, bf16[256,256]{1,0:T(8,128)(2,1)} %nk_ref.3, bf16[256,32,256]{2,1,0:T(8,128)(2,1)} %k_ref.3, bf16[256,32,256]{2,1,0:T(8,128)(2,1)} %v_ref.3, s32[256,1]{1,0:T(8,128)} %copy.18.len_ref, ...), custom_call_target="tpu_custom_call", output_to_operand_aliasing={{0}: (5, {}), {1}: (6, {})} | custom-call | tf_op jit(solution)/shard_map/pallas_call | solution.py:303
  51.9 0.5 collective-permute-done.4.a_ref.u3
  52.4 0.0 collective-permute-done.5.b_ref.d3
  52.4 1.8 %shard_map.135 = (bf16[1152,128]{1,0:T(8,128)(2,1)}, bf16[1152,128]{1,0:T(8,128)(2,1)}) custom-call(bf16[2304,128]{1,0:T(8,128)(2,1)S(1)} %collective-permute-done.4.a_ref.u3, bf16[2304,128]{1,0:T(8,128)(2,1)} %collective-permute-done.5.b_ref.d3), custom_call_target="tpu_custom_call" | custom-call | tf_op jit(solution)/shard_map/pallas_call | solution.py:223
  54.2 0.0 collective-permute-start.6
  54.2 2.7 %collective-permute-start.7 = (bf16[1152,128]{1,0:T(8,128)(2,1)}, bf16[1152,128]{1,0:T(8,128)(2,1)}, u32[]{:S(2)}, u32[]{:S(2)}) collective-permute-start(bf16[1152,128]{1,0:T(8,128)(2,1)} %get-tuple-element.62), channel_id=1, source_target_pairs={{0,224},{4,228},{8,232},{12,236},{16,240},{20,244},{24,248},{28,25... | collective-permute-start | bytes 884744 | tf_op jit(solution)/shard_map/ppermute | solution.py:398
  56.9 0.0 copy-done.8
  56.9 0.3 shard_map.137.un_ref
  57.2 0.7 copy-done.2
  57.9 0.0 all-to-all-done
  57.9 1.1 %copy-done.5 = bf16[2304,128]{1,0:T(8,128)(2,1)S(1)} copy-done((bf16[2304,128]{1,0:T(8,128)(2,1)S(1)}, bf16[2304,128]{1,0:T(8,128)(2,1)}, u32[]{:S(2)}) %copy-start.5) | copy-done | bytes 589848
  59.0 2.6 %shard_map.136 = (f32[256,128]{1,0:T(8,128)S(1)}, bf16[128,2048]{1,0:T(8,128)(2,1)S(1)}, bf16[7,256,128]{2,1,0:T(8,128)(2,1)S(1)}) custom-call(f32[512,128]{1,0:T(8,128)S(1)} %shard_map.132.choice_ref, bf16[512,2048]{1,0:T(8,128)(2,1)S(1)} %bitcast.12, bf16[2304,128]{1,0:T(8,128)(2,1)S(1)} %pad_maximum_fusion.own_ref, bf16[2304,128]{1,0:T(8,128)(2,1)S(1)} %copy-done.5, ...), custom_call_target="tpu_custom_call" | custom-call | tf_op jit(solution)/shard_map/pallas_call | solution.py:235
  61.6 0.0 collective-permute-done.6.a_ref
  61.6 0.0 collective-permute-done.7.b_ref.last
  61.6 1.4 %shard_map.138.p0 = f32[256,128]{1,0:T(8,128)S(1)} custom-call(f32[512,128]{1,0:T(8,128)S(1)} %shard_map.132.choice_ref, bf16[128,2048]{1,0:T(8,128)(2,1)S(1)} %get-tuple-element.71.kept_ref, bf16[1152,128]{1,0:T(8,128)(2,1)} %collective-permute-done.6.a_ref, bf16[1152,128]{1,0:T(8,128)(2,1)} %collective-permute-done.7.b_ref.last, ...), custom_call_target="tpu_custom_call" | custom-call | tf_op jit(solution)/shard_map/pallas_call | solution.py:235
  63.0 2.6 %collective-permute-start.10 = (f32[256,128]{1,0:T(8,128)S(1)}, f32[256,128]{1,0:T(8,128)S(1)}, u32[]{:S(2)}, u32[]{:S(2)}) collective-permute-start(f32[256,128]{1,0:T(8,128)S(1)} %shard_map.138.p0), channel_id=1, source_target_pairs={{0,3},{1,0},{2,1},{3,2},{4,7},{5,4},{6,5},{7,6},{8,11},{9,8},{10,9... | collective-permute-start | bytes 393224 | tf_op jit(solution)/shard_map/ppermute | solution.py:461
  65.6 0.5 collective-permute-start.9
  66.1 0.6 collective-permute-start.8
  66.7 3.5 %fusion.1.base_ref = f32[256,256]{1,0:T(8,128)S(1)} fusion(bf16[256,8192]{1,0:T(8,128)(2,1)S(1)} %copy-done.10, bf16[8192,256]{1,0:T(8,128)(2,1)} %param.13), kind=kOutput, calls=%fused_computation.5 | convolution fusion | flops 1073741824 | bytes 8650752 | tf_op jit(solution)/shard_map/dot_general | solution.py:464
  70.2 0.0 collective-permute-done.10.p3
  70.2 0.8 collective-permute-done.9.p2
  71.0 1.3 %collective-permute-done.8.p1 = f32[256,128]{1,0:T(8,128)S(1)} collective-permute-done((f32[256,128]{1,0:T(8,128)S(1)}, f32[256,128]{1,0:T(8,128)S(1)}, u32[]{:S(2)}, u32[]{:S(2)}) %collective-permute-start.8) | collective-permute-done | bytes 131104 | tf_op jit(solution)/shard_map/ppermute | solution.py:461
  72.3 1.3 %shard_map.139 = bf16[512,256]{1,0:T(8,128)(2,1)S(1)} custom-call(f32[512,128]{1,0:T(8,128)S(1)} %shard_map.132.choice_ref, f32[256,128]{1,0:T(8,128)S(1)} %shard_map.138.p0, f32[256,128]{1,0:T(8,128)S(1)} %collective-permute-done.8.p1, f32[256,128]{1,0:T(8,128)S(1)} %collective-permute-done.9.p2, f32[256,128]{1,0:T(8,128)S(1)} %collective-permute-done.10.p3, ...), custom_call_target="tpu_custom_call" | custom-call | tf_op jit(solution)/shard_map/pallas_call | solution.py:235
  73.6 16.8 %all_to_all.10 = bf16[8,64,256]{2,1,0:T(8,128)(2,1)S(1)} all-to-all(bf16[8,64,256]{2,1,0:T(8,128)(2,1)S(1)} %bitcast.14), channel_id=1, replica_groups={{0,4,8,12,16,20,24,28},{32,36,40,44,48,52,56,60},{64,68,72,76,80,84,88,..., dimensions={0} | all-to-all | bytes 524288 | tf_op jit(solution)/shard_map/all_to_all | solution.py:404
  90.4 1.7 %shard_map.140 = (bf16[256,256]{1,0:T(8,128)(2,1)}, bf16[256,2048]{1,0:T(8,128)(2,1)}) custom-call(bf16[256,512]{1,0:T(8,128)(2,1)S(1)} %copy-done.3, bf16[512,256]{1,0:T(8,128)(2,1)S(1)} %bitcast.15, f32[256,256]{1,0:T(8,128)S(1)} %fusion.1.base_ref, f32[256,2048]{1,0:T(8,128)S(1)} %copy-done, f32[256,128]{1,0:T(8,128)S(1)} %copy-done.9), custom_call_target="tpu_custom_call" | custom-call | tf_op jit(solution)/shard_map/pallas_call | solution.py:348
  (18 shorter events, 0.1 us)
Async XLA Ops:
  2.7 24.4 %copy-start.11 = (s32[1,256]{1,0:T(1,128)S(1)}, s32[1,256]{1,0:T(1,128)}, u32[]{:S(2)}) copy-start(s32[1,256]{1,0:T(1,128)} %param.19) | copy-start | bytes 3076
  2.8 18.5 %collective-permute-start.1 = (bf16[2304,128]{1,0:T(8,128)(2,1)S(1)}, bf16[2304,128]{1,0:T(8,128)(2,1)S(1)}, u32[]{:S(2)}, u32[]{:S(2)}) collective-permute-start(bf16[2304,128]{1,0:T(8,128)(2,1)S(1)} %pad_maximum_fusion.own_ref), channel_id=1, source_target_pairs={{0,224},{4,228},{8,232},{12,236},{16,240},{20,244},{24,248},{28,25... | collective-permute-start | bytes 1769480 | tf_op jit(solution)/shard_map/ppermute | solution.py:398
  9.3 15.2 %collective-permute-start = (bf16[2304,128]{1,0:T(8,128)(2,1)S(1)}, bf16[2304,128]{1,0:T(8,128)(2,1)}, u32[]{:S(2)}, u32[]{:S(2)}) collective-permute-start(bf16[2304,128]{1,0:T(8,128)(2,1)S(1)} %pad_maximum_fusion.own_ref), channel_id=1, source_target_pairs={{0,32},{4,36},{8,40},{12,44},{16,48},{20,52},{24,56},{28,60},{32,6... | collective-permute-start | bytes 1769480 | tf_op jit(solution)/shard_map/ppermute | solution.py:398
  10.0 9.1 %copy-start.6 = (s32[66,128]{1,0:T(8,128)}, s32[66,128]{1,0:T(8,128)S(1)}, u32[]{:S(2)}) copy-start(s32[66,128]{1,0:T(8,128)S(1)} %pad_add_fusion.meta_ref) | copy-start | bytes 101380
  12.3 1.4 %copy-start.1 = (bf16[512,2048]{1,0:T(8,128)(2,1)}, bf16[512,2048]{1,0:T(8,128)(2,1)S(1)}, u32[]{:S(2)}) copy-start(bf16[512,2048]{1,0:T(8,128)(2,1)S(1)} %get-tuple-element.64) | copy-start | bytes 6291460
  13.7 44.2 %all-to-all-start = ((bf16[8,64,2048]{2,1,0:T(8,128)(2,1)}), bf16[8,64,2048]{2,1,0:T(8,128)(2,1)S(1)}, u32[]{:S(2)}, u32[]{:S(2)}) async-start(bf16[8,64,2048]{2,1,0:T(8,128)(2,1)} %bitcast.13), calls=%async_computation | async-start | bytes 4194304 | tf_op jit(solution)/shard_map/all_to_all | solution.py:404
  19.1 0.8 copy-start.7
  21.3 16.9 %copy-start.4 = (bf16[2304,128]{1,0:T(8,128)(2,1)}, bf16[2304,128]{1,0:T(8,128)(2,1)S(1)}, u32[]{:S(2)}) copy-start(bf16[2304,128]{1,0:T(8,128)(2,1)S(1)} %collective-permute-done.1.d1) | copy-start | bytes 1769476
  24.5 14.5 %collective-permute-start.2 = (bf16[2304,128]{1,0:T(8,128)(2,1)}, bf16[2304,128]{1,0:T(8,128)(2,1)}, u32[]{:S(2)}, u32[]{:S(2)}) collective-permute-start(bf16[2304,128]{1,0:T(8,128)(2,1)} %collective-permute-done.u1), channel_id=1, source_target_pairs={{0,32},{4,36},{8,40},{12,44},{16,48},{20,52},{24,56},{28,60},{32,6... | collective-permute-start | bytes 1769480 | tf_op jit(solution)/shard_map/ppermute | solution.py:398
  24.5 14.5 %collective-permute-start.3 = (bf16[2304,128]{1,0:T(8,128)(2,1)S(1)}, bf16[2304,128]{1,0:T(8,128)(2,1)}, u32[]{:S(2)}, u32[]{:S(2)}) collective-permute-start(bf16[2304,128]{1,0:T(8,128)(2,1)S(1)} %collective-permute-done.1.d1), channel_id=1, source_target_pairs={{0,224},{4,228},{8,232},{12,236},{16,240},{20,244},{24,248},{28,25... | collective-permute-start | bytes 1769480 | tf_op jit(solution)/shard_map/ppermute | solution.py:398
  39.0 17.9 %copy-start.8 = (s32[66,128]{1,0:T(8,128)S(1)}, s32[66,128]{1,0:T(8,128)}, u32[]{:S(2)}) copy-start(s32[66,128]{1,0:T(8,128)} %copy-done.6) | copy-start | bytes 101380
  39.0 13.5 %collective-permute-start.4 = (bf16[2304,128]{1,0:T(8,128)(2,1)}, bf16[2304,128]{1,0:T(8,128)(2,1)S(1)}, u32[]{:S(2)}, u32[]{:S(2)}) collective-permute-start(bf16[2304,128]{1,0:T(8,128)(2,1)} %collective-permute-done.2.u2), channel_id=1, source_target_pairs={{0,32},{4,36},{8,40},{12,44},{16,48},{20,52},{24,56},{28,60},{32,6... | collective-permute-start | bytes 1769480 | tf_op jit(solution)/shard_map/ppermute | solution.py:398
  39.0 13.5 %collective-permute-start.5 = (bf16[2304,128]{1,0:T(8,128)(2,1)}, bf16[2304,128]{1,0:T(8,128)(2,1)}, u32[]{:S(2)}, u32[]{:S(2)}) collective-permute-start(bf16[2304,128]{1,0:T(8,128)(2,1)} %collective-permute-done.3.d2), channel_id=1, source_target_pairs={{0,224},{4,228},{8,232},{12,236},{16,240},{20,244},{24,248},{28,25... | collective-permute-start | bytes 1769480 | tf_op jit(solution)/shard_map/ppermute | solution.py:398
  54.2 7.4 %collective-permute-start.6 = (bf16[1152,128]{1,0:T(8,128)(2,1)}, bf16[1152,128]{1,0:T(8,128)(2,1)}, u32[]{:S(2)}, u32[]{:S(2)}) collective-permute-start(bf16[1152,128]{1,0:T(8,128)(2,1)} %get-tuple-element.61), channel_id=1, source_target_pairs={{0,32},{4,36},{8,40},{12,44},{16,48},{20,52},{24,56},{28,60},{32,6... | collective-permute-start | bytes 884744 | tf_op jit(solution)/shard_map/ppermute | solution.py:398
  54.2 7.4 %collective-permute-start.7 = (bf16[1152,128]{1,0:T(8,128)(2,1)}, bf16[1152,128]{1,0:T(8,128)(2,1)}, u32[]{:S(2)}, u32[]{:S(2)}) collective-permute-start(bf16[1152,128]{1,0:T(8,128)(2,1)} %get-tuple-element.62), channel_id=1, source_target_pairs={{0,224},{4,228},{8,232},{12,236},{16,240},{20,244},{24,248},{28,25... | collective-permute-start | bytes 884744 | tf_op jit(solution)/shard_map/ppermute | solution.py:398
  57.1 0.8 copy-start.2
  57.9 1.1 %copy-start.5 = (bf16[2304,128]{1,0:T(8,128)(2,1)S(1)}, bf16[2304,128]{1,0:T(8,128)(2,1)}, u32[]{:S(2)}) copy-start(bf16[2304,128]{1,0:T(8,128)(2,1)} %copy-done.4) | copy-start | bytes 1769476
  59.0 7.8 %copy-start.10 = (bf16[256,8192]{1,0:T(8,128)(2,1)S(1)}, bf16[256,8192]{1,0:T(8,128)(2,1)}, u32[]{:S(2)}) copy-start(bf16[256,8192]{1,0:T(8,128)(2,1)} %param.12) | copy-start | bytes 12582916
  63.0 27.3 %copy-start = (f32[256,2048]{1,0:T(8,128)S(1)}, f32[256,2048]{1,0:T(8,128)}, u32[]{:S(2)}) copy-start(f32[256,2048]{1,0:T(8,128)} %get-tuple-element.82.ctx_ref) | copy-start | bytes 6291460
  63.0 27.3 %copy-start.3 = (bf16[256,512]{1,0:T(8,128)(2,1)S(1)}, bf16[256,512]{1,0:T(8,128)(2,1)}, u32[]{:S(2)}) copy-start(bf16[256,512]{1,0:T(8,128)(2,1)} %copy-done.2) | copy-start | bytes 786436
  63.0 27.3 %copy-start.9 = (f32[256,128]{1,0:T(8,128)S(1)}, f32[256,128]{1,0:T(8,128)}, u32[]{:S(2)}) copy-start(f32[256,128]{1,0:T(8,128)} %get-tuple-element.83.own_ref) | copy-start | bytes 393220
  63.0 7.2 %collective-permute-start.10 = (f32[256,128]{1,0:T(8,128)S(1)}, f32[256,128]{1,0:T(8,128)S(1)}, u32[]{:S(2)}, u32[]{:S(2)}) collective-permute-start(f32[256,128]{1,0:T(8,128)S(1)} %shard_map.138.p0), channel_id=1, source_target_pairs={{0,3},{1,0},{2,1},{3,2},{4,7},{5,4},{6,5},{7,6},{8,11},{9,8},{10,9... | collective-permute-start | bytes 393224 | tf_op jit(solution)/shard_map/ppermute | solution.py:461
  65.6 5.4 %collective-permute-start.9 = (f32[256,128]{1,0:T(8,128)S(1)}, f32[256,128]{1,0:T(8,128)S(1)}, u32[]{:S(2)}, u32[]{:S(2)}) collective-permute-start(f32[256,128]{1,0:T(8,128)S(1)} %shard_map.138.p0), channel_id=1, source_target_pairs={{0,2},{1,3},{2,0},{3,1},{4,6},{5,7},{6,4},{7,5},{8,10},{9,11},{10,... | collective-permute-start | bytes 393224 | tf_op jit(solution)/shard_map/ppermute | solution.py:461
  66.1 6.2 %collective-permute-start.8 = (f32[256,128]{1,0:T(8,128)S(1)}, f32[256,128]{1,0:T(8,128)S(1)}, u32[]{:S(2)}, u32[]{:S(2)}) collective-permute-start(f32[256,128]{1,0:T(8,128)S(1)} %shard_map.138.p0), channel_id=1, source_target_pairs={{0,1},{1,2},{2,3},{3,0},{4,5},{5,6},{6,7},{7,4},{8,9},{9,10},{10,1... | collective-permute-start | bytes 393224 | tf_op jit(solution)/shard_map/ppermute | solution.py:461

commit v6 on v4

--- a/solution.py
+++ b/solution.py
@@ -170,8 +170,8 @@
     low = turn(low, choice_ref[:many, :] > 0.5)[0]
     odd = jnp.bitwise_and(iota((many, both), 0), MOST) > 0
     mine = odd & (iota((many, both), 1) < both // 2)
-    out_ref[:many] = jnp.where(mine, low, early_ref[:many])
-    out_ref[many:] = early_ref[many:]
+    out_ref[:many] = jnp.where(mine, low, early_ref[:many]).astype(bf16)
+    out_ref[many:] = early_ref[many:].astype(bf16)
 
 
 def delta_kernel(choice_ref, p0, p1, p2, p3, own, last, d1, u1, d2, u2, d3, u3, out_ref):
@@ -179,7 +179,8 @@
     half, both = p0.shape
     rank = both // 2
     tile = 2 * MOST
-    low = (p0[...] + p1[...]) + (p2[...] + p3[...])
+    own_low, *rest = [p[...].astype(f32) for p in (p0, p1, p2, p3)]
+    low = (own_low + rest[0]) + (rest[1] + rest[2])
     turned = pltpu.roll(low, rank, 1)
     lane = iota((half, both), 1) < rank
     twice = jnp.concatenate([jnp.where(lane, low, turned), jnp.where(lane, turned, low)], axis=0)
@@ -472,7 +473,7 @@
     )
     last_a, last_b, early, kept, un = lax.optimization_barrier((last_a, last_b, early, kept, un))
     (partial,) = vmem_call(
-        final_kernel, [((count // 2, both), f32)], choice, kept, last_a, last_b, early
+        final_kernel, [((count // 2, both), bf16)], choice, kept, last_a, last_b, early
     )
     others = [
         lax.ppermute(partial, "tp", [(j, (j + k) % tp) for j in range(tp)]) for k in range(1, tp)

time: 92.7 us -> 91.3 us (0.985)
  waiting for transfers between devices: 7.4 us -> 5.99 us
    ppermute x3, waiting for transfers between devices: 2.04 us -> 0.63 us  [body(): lax.ppermute(partial, 'tp', [(j, (j + k) % tp) for j in range(tp)])]
  transfers between devices with their start and end apart: 12 -> 12, of which waited for: 6 -> 5; matrix products, arithmetic and copies ran while one was open for 7% -> 7% of each run, Pallas kernels for 29% -> 29%
where the time goes in v6:
time: 91.3 us; the launch traced here: 90.7 us
  Pallas kernels  31 us (34%)
  starting transfers between devices  23.6 us (26%)
  blocking collectives  16.7 us (18%)
  local copies, waits for them, and re-layouts  8.15 us (9%)
  waiting for transfers between devices  5.99 us (7%)
  matrix products  3.51 us (4%)
    pallas_call x2, Pallas kernels, attend(): pl.pallas_call(functools.partial(attend_kernel, 1.0 / math.sqrt(HEAD)), o...  20.5 us
    all_to_all x1, blocking collectives, over_plane(): lax.all_to_all(x.reshape(PLANE, size // PLANE, wide), 'rows', split_axis=...  16.7 us
    ppermute x8, starting transfers between devices, shift_z(): lax.ppermute(x, 'rows', [(r, (r + by * PLANE) % groups) for r in range(gr...  14.5 us
    all_to_all x1, starting transfers between devices, over_plane(): lax.all_to_all(x.reshape(PLANE, size // PLANE, wide), 'rows', split_axis=...  5.42 us
    ppermute x8, waiting for transfers between devices, shift_z(): lax.ppermute(x, 'rows', [(r, (r + by * PLANE) % groups) for r in range(gr...  5.36 us
    pallas_call x4, Pallas kernels, vmem_call(): pl.pallas_call(kernel, out_shape=tuple((jax.ShapeDtypeStruct(shape, dtype...  4.77 us
    unnamed x26, local copies, waits for them, and re-layouts  3.95 us
    ppermute x3, starting transfers between devices, body(): lax.ppermute(partial, 'tp', [(j, (j + k) % tp) for j in range(tp)])  3.67 us
  transfers between devices with their start and end apart: 12, of which 5 were waited for; matrix products, arithmetic and copies ran while one was open for 7% of the time, Pallas kernels for 29%

profile of v6, /device:TPU:1, one launch (start us, length us, event | category | flops | bytes accessed | tf_op | source)
XLA Modules:
  0.0 90.7 jit_solution(17445163163693389497)
XLA Ops:
  0.6 0.8 fusion
  1.4 1.3 %copy.17 = bf16[2048,128]{1,0:T(8,128)(2,1)S(1)} copy(bf16[2048,128]{0,1:T(8,128)(2,1)} %bitcast.16) | data formatting | bytes 1048576 | tf_op jit(solution)/shard_map/reshape | solution.py:435
  2.7 0.0 copy-start.12
  2.8 6.5 %collective-permute-start.1 = (bf16[2304,128]{1,0:T(8,128)(2,1)S(1)}, bf16[2304,128]{1,0:T(8,128)(2,1)S(1)}, u32[]{:S(2)}, u32[]{:S(2)}) collective-permute-start(bf16[2304,128]{1,0:T(8,128)(2,1)S(1)} %pad_maximum_fusion.own_ref.own), channel_id=1, source_target_pairs={{0,224},{4,228},{8,232},{12,236},{16,240},{20,244},{24,248},{28,25... | collective-permute-start | bytes 1769480 | tf_op jit(solution)/shard_map/ppermute | solution.py:418
  9.3 0.0 collective-permute-start
  9.3 0.8 pad_add_fusion.meta_ref
  10.0 1.3 %constant_dynamic-slice_fusion.x_ref = bf16[256,2048]{1,0:T(8,128)(2,1)S(1)} fusion(bf16[256,8192]{1,0:T(8,128)(2,1)} %param.12, s32[]{:T(128)S(6)} %select_n.3), kind=kLoop, calls=%fused_computation.3 | loop fusion | bytes 2097156 | tf_op jit(solution)/shard_map/dynamic_slice | solution.py:442
  11.4 1.0 %shard_map.131 = (bf16[512,2048]{1,0:T(8,128)(2,1)S(1)}, s32[8,128]{1,0:T(8,128)S(1)}) custom-call(s32[66,128]{1,0:T(8,128)S(1)} %pad_add_fusion.meta_ref, bf16[256,2048]{1,0:T(8,128)(2,1)S(1)} %constant_dynamic-slice_fusion.x_ref), custom_call_target="tpu_custom_call" | custom-call | tf_op jit(solution)/shard_map/pallas_call | solution.py:84
  12.3 1.3 %copy-done.4 = bf16[512,2048]{1,0:T(8,128)(2,1)} copy-done((bf16[512,2048]{1,0:T(8,128)(2,1)}, bf16[512,2048]{1,0:T(8,128)(2,1)S(1)}, u32[]{:S(2)}) %copy-start.4) | copy-done | bytes 2097176
  13.7 5.4 %all-to-all-start = ((bf16[8,64,2048]{2,1,0:T(8,128)(2,1)}), bf16[8,64,2048]{2,1,0:T(8,128)(2,1)S(1)}, u32[]{:S(2)}, u32[]{:S(2)}) async-start(bf16[8,64,2048]{2,1,0:T(8,128)(2,1)} %bitcast.13), calls=%async_computation | async-start | bytes 4194304 | tf_op jit(solution)/shard_map/all_to_all | solution.py:424
  19.1 0.0 copy-done.7
  19.1 0.8 copy-done.8
  19.9 0.5 shard_map.132.choice_ref
  20.4 0.9 collective-permute-done.1.d1
  21.3 3.2 %collective-permute-done.u1 = bf16[2304,128]{1,0:T(8,128)(2,1)} collective-permute-done((bf16[2304,128]{1,0:T(8,128)(2,1)S(1)}, bf16[2304,128]{1,0:T(8,128)(2,1)}, u32[]{:S(2)}, u32[]{:S(2)}) %collective-permute-start) | collective-permute-done | bytes 589856 | tf_op jit(solution)/shard_map/ppermute | solution.py:418
  24.5 0.0 collective-permute-start.2
  24.5 2.7 %collective-permute-start.3 = (bf16[2304,128]{1,0:T(8,128)(2,1)S(1)}, bf16[2304,128]{1,0:T(8,128)(2,1)}, u32[]{:S(2)}, u32[]{:S(2)}) collective-permute-start(bf16[2304,128]{1,0:T(8,128)(2,1)S(1)} %collective-permute-done.1.d1), channel_id=1, source_target_pairs={{0,224},{4,228},{8,232},{12,236},{16,240},{20,244},{24,248},{28,25... | collective-permute-start | bytes 1769480 | tf_op jit(solution)/shard_map/ppermute | solution.py:418
  27.1 0.8 copy.18.len_ref
  27.9 10.3 %shard_map.133 = (f32[256,2048]{1,0:T(8,128)}, f32[256,128]{1,0:T(8,128)}) custom-call(bf16[256,2048]{1,0:T(8,128)(2,1)} %q_ref.1, bf16[256,256]{1,0:T(8,128)(2,1)} %nk_ref.3, bf16[256,32,256]{2,1,0:T(8,128)(2,1)} %k_ref.3, bf16[256,32,256]{2,1,0:T(8,128)(2,1)} %v_ref.3, s32[256,1]{1,0:T(8,128)} %copy.18.len_ref), custom_call_target="tpu_custom_call" | custom-call | tf_op jit(solution)/shard_map/pallas_call | solution.py:323
  38.2 0.7 collective-permute-done.2.u2
  38.9 0.0 collective-permute-done.3.d2
  39.0 0.0 collective-permute-start.4
  39.0 2.7 %collective-permute-start.5 = (bf16[2304,128]{1,0:T(8,128)(2,1)}, bf16[2304,128]{1,0:T(8,128)(2,1)}, u32[]{:S(2)}, u32[]{:S(2)}) collective-permute-start(bf16[2304,128]{1,0:T(8,128)(2,1)} %collective-permute-done.3.d2), channel_id=1, source_target_pairs={{0,224},{4,228},{8,232},{12,236},{16,240},{20,244},{24,248},{28,25... | collective-permute-start | bytes 1769480 | tf_op jit(solution)/shard_map/ppermute | solution.py:418
  41.6 10.3 %shard_map.134 = (f32[256,2048]{1,0:T(8,128)}, f32[256,128]{1,0:T(8,128)}) custom-call(bf16[256,2048]{1,0:T(8,128)(2,1)} %q_ref.1, bf16[256,256]{1,0:T(8,128)(2,1)} %nk_ref.3, bf16[256,32,256]{2,1,0:T(8,128)(2,1)} %k_ref.3, bf16[256,32,256]{2,1,0:T(8,128)(2,1)} %v_ref.3, s32[256,1]{1,0:T(8,128)} %copy.18.len_ref, ...), custom_call_target="tpu_custom_call", output_to_operand_aliasing={{0}: (5, {}), {1}: (6, {})} | custom-call | tf_op jit(solution)/shard_map/pallas_call | solution.py:323
  51.9 0.5 collective-permute-done.4.a_ref.u3
  52.4 0.0 collective-permute-done.5.b_ref.d3
  52.4 1.8 %shard_map.135 = (bf16[1152,128]{1,0:T(8,128)(2,1)}, bf16[1152,128]{1,0:T(8,128)(2,1)}) custom-call(bf16[2304,128]{1,0:T(8,128)(2,1)S(1)} %collective-permute-done.4.a_ref.u3, bf16[2304,128]{1,0:T(8,128)(2,1)} %collective-permute-done.5.b_ref.d3), custom_call_target="tpu_custom_call" | custom-call | tf_op jit(solution)/shard_map/pallas_call | solution.py:224
  54.2 0.0 collective-permute-start.6
  54.2 2.7 %collective-permute-start.7 = (bf16[1152,128]{1,0:T(8,128)(2,1)}, bf16[1152,128]{1,0:T(8,128)(2,1)}, u32[]{:S(2)}, u32[]{:S(2)}) collective-permute-start(bf16[1152,128]{1,0:T(8,128)(2,1)} %get-tuple-element.60), channel_id=1, source_target_pairs={{0,224},{4,228},{8,232},{12,236},{16,240},{20,244},{24,248},{28,25... | collective-permute-start | bytes 884744 | tf_op jit(solution)/shard_map/ppermute | solution.py:418
  56.9 0.3 shard_map.137.un_ref
  57.2 0.7 copy-done.5
  57.9 0.0 all-to-all-done
  57.9 1.1 %copy-done.2 = bf16[2304,128]{1,0:T(8,128)(2,1)S(1)} copy-done((bf16[2304,128]{1,0:T(8,128)(2,1)S(1)}, bf16[2304,128]{1,0:T(8,128)(2,1)}, u32[]{:S(2)}) %copy-start.2) | copy-done | bytes 589848
  59.0 2.6 %shard_map.136 = (f32[256,128]{1,0:T(8,128)S(1)}, bf16[128,2048]{1,0:T(8,128)(2,1)S(1)}) custom-call(f32[512,128]{1,0:T(8,128)S(1)} %shard_map.132.choice_ref, bf16[512,2048]{1,0:T(8,128)(2,1)S(1)} %bitcast.12, bf16[2304,128]{1,0:T(8,128)(2,1)S(1)} %pad_maximum_fusion.own_ref.own, bf16[2304,128]{1,0:T(8,128)(2,1)S(1)} %copy-done.2, ...), custom_call_target="tpu_custom_call" | custom-call | tf_op jit(solution)/shard_map/pallas_call | solution.py:255
  61.5 0.0 collective-permute-done.6.a_ref
  61.6 0.0 collective-permute-done.7.b_ref.last
  61.6 1.4 %shard_map.138.p0 = bf16[256,128]{1,0:T(8,128)(2,1)S(1)} custom-call(f32[512,128]{1,0:T(8,128)S(1)} %shard_map.132.choice_ref, bf16[128,2048]{1,0:T(8,128)(2,1)S(1)} %get-tuple-element.68.kept_ref, bf16[1152,128]{1,0:T(8,128)(2,1)} %collective-permute-done.6.a_ref, bf16[1152,128]{1,0:T(8,128)(2,1)} %collective-permute-done.7.b_ref.last, ...), custom_call_target="tpu_custom_call" | custom-call | tf_op jit(solution)/shard_map/pallas_call | solution.py:255
  63.0 0.0 copy-start.3
  63.0 2.5 %collective-permute-start.10 = (bf16[256,128]{1,0:T(8,128)(2,1)S(1)}, bf16[256,128]{1,0:T(8,128)(2,1)S(1)}, u32[]{:S(2)}, u32[]{:S(2)}) collective-permute-start(bf16[256,128]{1,0:T(8,128)(2,1)S(1)} %shard_map.138.p0), channel_id=1, source_target_pairs={{0,3},{1,0},{2,1},{3,2},{4,7},{5,4},{6,5},{7,6},{8,11},{9,8},{10,9... | collective-permute-start | bytes 196616 | tf_op jit(solution)/shard_map/ppermute | solution.py:479
  65.5 0.5 collective-permute-start.9
  66.1 0.6 collective-permute-start.8
  66.7 3.5 %fusion.1.base_ref = f32[256,256]{1,0:T(8,128)S(1)} fusion(bf16[256,8192]{1,0:T(8,128)(2,1)S(1)} %copy-done.11, bf16[8192,256]{1,0:T(8,128)(2,1)} %param.13), kind=kOutput, calls=%fused_computation.5 | convolution fusion | flops 1073741824 | bytes 8650752 | tf_op jit(solution)/shard_map/dot_general | solution.py:482
  70.2 0.0 collective-permute-done.10.p3
  70.2 0.0 collective-permute-done.9.p2
  70.2 0.6 collective-permute-done.8.p1
  70.9 1.4 %shard_map.139 = bf16[512,256]{1,0:T(8,128)(2,1)S(1)} custom-call(f32[512,128]{1,0:T(8,128)S(1)} %shard_map.132.choice_ref, bf16[256,128]{1,0:T(8,128)(2,1)S(1)} %shard_map.138.p0, bf16[256,128]{1,0:T(8,128)(2,1)S(1)} %collective-permute-done.8.p1, bf16[256,128]{1,0:T(8,128)(2,1)S(1)} %collective-permute-done.9.p2, ...), custom_call_target="tpu_custom_call" | custom-call | tf_op jit(solution)/shard_map/pallas_call | solution.py:243
  72.3 16.7 %all_to_all.10 = bf16[8,64,256]{2,1,0:T(8,128)(2,1)S(1)} all-to-all(bf16[8,64,256]{2,1,0:T(8,128)(2,1)S(1)} %bitcast.14), channel_id=1, replica_groups={{0,4,8,12,16,20,24,28},{32,36,40,44,48,52,56,60},{64,68,72,76,80,84,88,..., dimensions={0} | all-to-all | bytes 524288 | tf_op jit(solution)/shard_map/all_to_all | solution.py:424
  89.0 1.6 %shard_map.140 = (bf16[256,256]{1,0:T(8,128)(2,1)}, bf16[256,2048]{1,0:T(8,128)(2,1)}) custom-call(bf16[256,512]{1,0:T(8,128)(2,1)S(1)} %copy-done.6, bf16[512,256]{1,0:T(8,128)(2,1)S(1)} %bitcast.15, f32[256,256]{1,0:T(8,128)S(1)} %fusion.1.base_ref, f32[256,2048]{1,0:T(8,128)S(1)} %copy-done, f32[256,128]{1,0:T(8,128)S(1)} %copy-done.10), custom_call_target="tpu_custom_call" | custom-call | tf_op jit(solution)/shard_map/pallas_call | solution.py:368
  (20 shorter events, 0.1 us)
Async XLA Ops:
  2.7 24.4 %copy-start.12 = (s32[1,256]{1,0:T(1,128)S(1)}, s32[1,256]{1,0:T(1,128)}, u32[]{:S(2)}) copy-start(s32[1,256]{1,0:T(1,128)} %param.19) | copy-start | bytes 3076
  2.8 18.5 %collective-permute-start.1 = (bf16[2304,128]{1,0:T(8,128)(2,1)S(1)}, bf16[2304,128]{1,0:T(8,128)(2,1)S(1)}, u32[]{:S(2)}, u32[]{:S(2)}) collective-permute-start(bf16[2304,128]{1,0:T(8,128)(2,1)S(1)} %pad_maximum_fusion.own_ref.own), channel_id=1, source_target_pairs={{0,224},{4,228},{8,232},{12,236},{16,240},{20,244},{24,248},{28,25... | collective-permute-start | bytes 1769480 | tf_op jit(solution)/shard_map/ppermute | solution.py:418
  9.3 15.2 %collective-permute-start = (bf16[2304,128]{1,0:T(8,128)(2,1)S(1)}, bf16[2304,128]{1,0:T(8,128)(2,1)}, u32[]{:S(2)}, u32[]{:S(2)}) collective-permute-start(bf16[2304,128]{1,0:T(8,128)(2,1)S(1)} %pad_maximum_fusion.own_ref.own), channel_id=1, source_target_pairs={{0,32},{4,36},{8,40},{12,44},{16,48},{20,52},{24,56},{28,60},{32,6... | collective-permute-start | bytes 1769480 | tf_op jit(solution)/shard_map/ppermute | solution.py:418
  10.0 9.0 %copy-start.7 = (s32[66,128]{1,0:T(8,128)}, s32[66,128]{1,0:T(8,128)S(1)}, u32[]{:S(2)}) copy-start(s32[66,128]{1,0:T(8,128)S(1)} %pad_add_fusion.meta_ref) | copy-start | bytes 101380
  12.3 1.3 %copy-start.4 = (bf16[512,2048]{1,0:T(8,128)(2,1)}, bf16[512,2048]{1,0:T(8,128)(2,1)S(1)}, u32[]{:S(2)}) copy-start(bf16[512,2048]{1,0:T(8,128)(2,1)S(1)} %get-tuple-element.62) | copy-start | bytes 6291460
  13.7 44.2 %all-to-all-start = ((bf16[8,64,2048]{2,1,0:T(8,128)(2,1)}), bf16[8,64,2048]{2,1,0:T(8,128)(2,1)S(1)}, u32[]{:S(2)}, u32[]{:S(2)}) async-start(bf16[8,64,2048]{2,1,0:T(8,128)(2,1)} %bitcast.13), calls=%async_computation | async-start | bytes 4194304 | tf_op jit(solution)/shard_map/all_to_all | solution.py:424
  19.1 0.8 copy-start.8
  21.3 16.9 %copy-start.1 = (bf16[2304,128]{1,0:T(8,128)(2,1)}, bf16[2304,128]{1,0:T(8,128)(2,1)S(1)}, u32[]{:S(2)}) copy-start(bf16[2304,128]{1,0:T(8,128)(2,1)S(1)} %collective-permute-done.1.d1) | copy-start | bytes 1769476
  24.5 14.5 %collective-permute-start.2 = (bf16[2304,128]{1,0:T(8,128)(2,1)}, bf16[2304,128]{1,0:T(8,128)(2,1)}, u32[]{:S(2)}, u32[]{:S(2)}) collective-permute-start(bf16[2304,128]{1,0:T(8,128)(2,1)} %collective-permute-done.u1), channel_id=1, source_target_pairs={{0,32},{4,36},{8,40},{12,44},{16,48},{20,52},{24,56},{28,60},{32,6... | collective-permute-start | bytes 1769480 | tf_op jit(solution)/shard_map/ppermute | solution.py:418
  24.5 14.5 %collective-permute-start.3 = (bf16[2304,128]{1,0:T(8,128)(2,1)S(1)}, bf16[2304,128]{1,0:T(8,128)(2,1)}, u32[]{:S(2)}, u32[]{:S(2)}) collective-permute-start(bf16[2304,128]{1,0:T(8,128)(2,1)S(1)} %collective-permute-done.1.d1), channel_id=1, source_target_pairs={{0,224},{4,228},{8,232},{12,236},{16,240},{20,244},{24,248},{28,25... | collective-permute-start | bytes 1769480 | tf_op jit(solution)/shard_map/ppermute | solution.py:418
  39.0 17.9 %copy-start.9 = (s32[66,128]{1,0:T(8,128)S(1)}, s32[66,128]{1,0:T(8,128)}, u32[]{:S(2)}) copy-start(s32[66,128]{1,0:T(8,128)} %copy-done.7) | copy-start | bytes 101380
  39.0 13.5 %collective-permute-start.4 = (bf16[2304,128]{1,0:T(8,128)(2,1)}, bf16[2304,128]{1,0:T(8,128)(2,1)S(1)}, u32[]{:S(2)}, u32[]{:S(2)}) collective-permute-start(bf16[2304,128]{1,0:T(8,128)(2,1)} %collective-permute-done.2.u2), channel_id=1, source_target_pairs={{0,32},{4,36},{8,40},{12,44},{16,48},{20,52},{24,56},{28,60},{32,6... | collective-permute-start | bytes 1769480 | tf_op jit(solution)/shard_map/ppermute | solution.py:418
  39.0 13.5 %collective-permute-start.5 = (bf16[2304,128]{1,0:T(8,128)(2,1)}, bf16[2304,128]{1,0:T(8,128)(2,1)}, u32[]{:S(2)}, u32[]{:S(2)}) collective-permute-start(bf16[2304,128]{1,0:T(8,128)(2,1)} %collective-permute-done.3.d2), channel_id=1, source_target_pairs={{0,224},{4,228},{8,232},{12,236},{16,240},{20,244},{24,248},{28,25... | collective-permute-start | bytes 1769480 | tf_op jit(solution)/shard_map/ppermute | solution.py:418
  54.2 7.4 %collective-permute-start.6 = (bf16[1152,128]{1,0:T(8,128)(2,1)}, bf16[1152,128]{1,0:T(8,128)(2,1)}, u32[]{:S(2)}, u32[]{:S(2)}) collective-permute-start(bf16[1152,128]{1,0:T(8,128)(2,1)} %get-tuple-element.59), channel_id=1, source_target_pairs={{0,32},{4,36},{8,40},{12,44},{16,48},{20,52},{24,56},{28,60},{32,6... | collective-permute-start | bytes 884744 | tf_op jit(solution)/shard_map/ppermute | solution.py:418
  54.2 7.4 %collective-permute-start.7 = (bf16[1152,128]{1,0:T(8,128)(2,1)}, bf16[1152,128]{1,0:T(8,128)(2,1)}, u32[]{:S(2)}, u32[]{:S(2)}) collective-permute-start(bf16[1152,128]{1,0:T(8,128)(2,1)} %get-tuple-element.60), channel_id=1, source_target_pairs={{0,224},{4,228},{8,232},{12,236},{16,240},{20,244},{24,248},{28,25... | collective-permute-start | bytes 884744 | tf_op jit(solution)/shard_map/ppermute | solution.py:418
  57.1 0.7 copy-start.5
  57.9 1.1 %copy-start.2 = (bf16[2304,128]{1,0:T(8,128)(2,1)S(1)}, bf16[2304,128]{1,0:T(8,128)(2,1)}, u32[]{:S(2)}) copy-start(bf16[2304,128]{1,0:T(8,128)(2,1)} %copy-done.1) | copy-start | bytes 1769476
  59.0 7.7 %copy-start.11 = (bf16[256,8192]{1,0:T(8,128)(2,1)S(1)}, bf16[256,8192]{1,0:T(8,128)(2,1)}, u32[]{:S(2)}) copy-start(bf16[256,8192]{1,0:T(8,128)(2,1)} %param.12) | copy-start | bytes 12582916
  63.0 7.9 %copy-start.3 = (bf16[2304,128]{1,0:T(8,128)(2,1)S(1)}, bf16[2304,128]{1,0:T(8,128)(2,1)}, u32[]{:S(2)}) copy-start(bf16[2304,128]{1,0:T(8,128)(2,1)} %copy-done.1) | copy-start | bytes 1769476
  63.0 7.2 %collective-permute-start.10 = (bf16[256,128]{1,0:T(8,128)(2,1)S(1)}, bf16[256,128]{1,0:T(8,128)(2,1)S(1)}, u32[]{:S(2)}, u32[]{:S(2)}) collective-permute-start(bf16[256,128]{1,0:T(8,128)(2,1)S(1)} %shard_map.138.p0), channel_id=1, source_target_pairs={{0,3},{1,0},{2,1},{3,2},{4,7},{5,4},{6,5},{7,6},{8,11},{9,8},{10,9... | collective-permute-start | bytes 196616 | tf_op jit(solution)/shard_map/ppermute | solution.py:479
  65.5 4.7 %collective-permute-start.9 = (bf16[256,128]{1,0:T(8,128)(2,1)S(1)}, bf16[256,128]{1,0:T(8,128)(2,1)S(1)}, u32[]{:S(2)}, u32[]{:S(2)}) collective-permute-start(bf16[256,128]{1,0:T(8,128)(2,1)S(1)} %shard_map.138.p0), channel_id=1, source_target_pairs={{0,2},{1,3},{2,0},{3,1},{4,6},{5,7},{6,4},{7,5},{8,10},{9,11},{10,... | collective-permute-start | bytes 196616 | tf_op jit(solution)/shard_map/ppermute | solution.py:479
  66.1 4.8 %collective-permute-start.8 = (bf16[256,128]{1,0:T(8,128)(2,1)S(1)}, bf16[256,128]{1,0:T(8,128)(2,1)S(1)}, u32[]{:S(2)}, u32[]{:S(2)}) collective-permute-start(bf16[256,128]{1,0:T(8,128)(2,1)S(1)} %shard_map.138.p0), channel_id=1, source_target_pairs={{0,1},{1,2},{2,3},{3,0},{4,5},{5,6},{6,7},{7,4},{8,9},{9,10},{10,1... | collective-permute-start | bytes 196616 | tf_op jit(solution)/shard_map/ppermute | solution.py:479
  70.2 18.8 %copy-start = (f32[256,2048]{1,0:T(8,128)S(1)}, f32[256,2048]{1,0:T(8,128)}, u32[]{:S(2)}) copy-start(f32[256,2048]{1,0:T(8,128)} %get-tuple-element.78.ctx_ref) | copy-start | bytes 6291460
  70.2 18.8 %copy-start.6 = (bf16[256,512]{1,0:T(8,128)(2,1)S(1)}, bf16[256,512]{1,0:T(8,128)(2,1)}, u32[]{:S(2)}) copy-start(bf16[256,512]{1,0:T(8,128)(2,1)} %copy-done.5) | copy-start | bytes 786436
  70.2 18.8 %copy-start.10 = (f32[256,128]{1,0:T(8,128)S(1)}, f32[256,128]{1,0:T(8,128)}, u32[]{:S(2)}) copy-start(f32[256,128]{1,0:T(8,128)} %get-tuple-element.79.own_ref) | copy-start | bytes 393220
